TPU v7x, 32 devices: a whole 2x2x4 slice. The times are simulated.
32 devices in a mesh: face: 4 (over y, x), tile: 8 (over z, core).
Axes of the slice: x: 2, y: 2, z: 4, core: 2. Of those that a mesh axis runs over, the one named last changes fastest.
Arguments:
- latlon: bfloat16 [2048, 74, 128], P(('face', 'tile')), may hold values from -6 to 6
- intersection_weight: bfloat16 [2048, 4, 128, 128], P(('face', 'tile')), may hold values from -0.5 to 0.5
- target_dev: int32 [2048, 4], P(('face', 'tile')), may hold values from 0 to 31, all different within a row; in each aligned block of 64 rows (0 to 63, 64 to 127, ...) at most 8 rows name the same one
- target_piece: int32 [2048, 4], P(('face', 'tile')), may hold values from 0 to 63
- counts: int32 [2048], P(('face', 'tile')), may hold values from 1 to 4
- conv_weight: bfloat16 [9, 256, 74], replicated, may hold values from -0.25 to 0.25
- cotangent: bfloat16 [4, 256, 128, 512], P('face', None, 'tile'), may hold values from -6 to 6
Outputs:
- activation: bfloat16 [4, 256, 128, 512], P('face', None, 'tile')
- grad_conv: float32 [9, 256, 74], replicated
- grad_latlon: bfloat16 [2048, 74, 128], P(('face', 'tile'))
Inputs may be any that keep to these rules, and one draw needn't show every extreme that they name: `target_dev`: among the 4 entries of one block all owners differ; among the entries of one device's 64 blocks (aligned blocks of rows) no owner is named more than 8 times, a bound that some block reaches. Entries j >= counts[b] of block b are not live.
All inputs are finite; a program needn't handle non-finite values.
Results may differ from a plain program's by a relative error of at most 0.0091.
Values may be sent and summed in bfloat16 or wider, within the bound.
No kernel may reach another device: no remote copies, remote signals or barrier semaphores. Data moves between devices by JAX's collectives and lax.ppermute only.
A program may use at most 192 MiB of HBM per device.

v0:
```python
import math

import jax
import jax.numpy as jnp
from jax import lax
from jax.sharding import PartitionSpec as P

C = 74
HID = 256
ROWS = 16
COLS = 512
PP = 128
K = 4
PIECES = 64


def padded_2(cells, sides, width):
    for axis, dim in sides:
        count = lax.axis_size(axis)
        head = lax.slice_in_dim(cells, 0, width, axis=dim)
        tail = lax.slice_in_dim(cells, cells.shape[dim] - width, cells.shape[dim], axis=dim)
        cells = jnp.concatenate(
            [
                lax.ppermute(tail, axis, [(i, (i + 1) % count) for i in range(count)]),
                cells,
                lax.ppermute(head, axis, [((i + 1) % count, i) for i in range(count)]),
            ],
            axis=dim,
        )
    return cells


def gelu_parts(value):
    inner = 0.7978845608 * (value + 0.044715 * value * value * value)
    tanh_part = jnp.tanh(inner)
    result = 0.5 * value * (1.0 + tanh_part)
    slope = 0.5 * (1.0 + tanh_part) + 0.5 * value * (1.0 - tanh_part * tanh_part) * 0.7978845608 * (
        1.0 + 0.134145 * value * value
    )
    return (result, slope)


def strip_edges(padded):
    tile_at = lax.axis_index("tile")
    last_tile = lax.axis_size("tile") - 1
    rows = jnp.arange(padded.shape[1], dtype=jnp.int32)
    outside = (rows == 0) & (tile_at == 0) | (rows == padded.shape[1] - 1) & (tile_at == last_tile)
    return jnp.where(outside[None, :, None], jnp.zeros((), padded.dtype), padded)


def to_owners(buffers):
    return (
        lax.all_to_all(buffers[0], ("face", "tile"), split_axis=0, concat_axis=0, tiled=True),
        lax.all_to_all(buffers[1], ("face", "tile"), split_axis=0, concat_axis=0, tiled=True),
    )


def to_sources(buffer):
    return lax.all_to_all(buffer, ("face", "tile"), split_axis=0, concat_axis=0, tiled=True)


def local(latlon, intersection_weight, target_dev, target_piece, counts, conv_weight, cotangent):
    faces = lax.axis_size("face")
    tiles = lax.axis_size("tile")
    devices = faces * tiles
    blocks = latlon.shape[0]
    slots = max(2, (blocks * K + devices - 1) // devices)
    live = jnp.arange(K, dtype=jnp.int32)[None, :] < counts[:, None]
    partial_value = jnp.einsum(
        "bcp,bjpq->bjcq", latlon, intersection_weight, preferred_element_type=jnp.float32
    )
    partial_value = jnp.where(live[:, :, None, None], partial_value, 0.0).astype(jnp.bfloat16)
    flat_dev = target_dev.reshape(-1)
    owner_hits = (flat_dev[:, None] == jnp.arange(devices, dtype=jnp.int32)[None, :]).astype(
        jnp.int32
    )
    earlier = jnp.cumsum(owner_hits, axis=0) - owner_hits
    slot = jnp.sum(earlier * owner_hits, axis=1)
    send = (
        jnp.zeros((devices, slots, C, PP), jnp.bfloat16)
        .at[flat_dev, slot]
        .set(partial_value.reshape(-1, C, PP))
    )
    send_piece = (
        jnp.full((devices, slots), -1, jnp.int32).at[flat_dev, slot].set(target_piece.reshape(-1))
    )
    recv, recv_piece = to_owners((send, send_piece))
    select = (
        recv_piece.reshape(-1)[None, :] == jnp.arange(PIECES, dtype=jnp.int32)[:, None]
    ).astype(jnp.bfloat16)
    field_sum = jnp.einsum(
        "pr,rcq->cpq", select, recv.reshape(-1, C, PP), preferred_element_type=jnp.float32
    )
    field = field_sum.astype(jnp.bfloat16).reshape(C, ROWS, COLS)
    field_pad = padded_2(field, (("tile", 1), ("face", 2)), 1)
    field_pad = strip_edges(field_pad)
    pre = jnp.zeros((HID, ROWS, COLS), jnp.float32)
    for k in range(9):
        ky, kx = divmod(k, 3)
        pre = pre + jnp.einsum(
            "oc,crw->orw",
            conv_weight[k],
            field_pad[:, ky : ky + ROWS, kx : kx + COLS],
            preferred_element_type=jnp.float32,
        )
    result, slope = gelu_parts(pre)
    activation = result.astype(jnp.bfloat16)[None]
    dpre = (cotangent[0].astype(jnp.float32) * slope).astype(jnp.bfloat16)
    terms = []
    for k in range(9):
        ky, kx = divmod(k, 3)
        terms.append(
            jnp.einsum(
                "orw,crw->oc",
                dpre,
                field_pad[:, ky : ky + ROWS, kx : kx + COLS],
                preferred_element_type=jnp.float32,
            )
        )
    grad_sum = lax.psum(jnp.stack(terms), ("face", "tile"))
    grad_conv = grad_sum * (1.0 / math.sqrt(devices * ROWS * COLS))
    dpre_pad = padded_2(dpre, (("tile", 1), ("face", 2)), 1)
    dpre_pad = strip_edges(dpre_pad)
    dfield_sum = jnp.zeros((C, ROWS, COLS), jnp.float32)
    for k in range(9):
        ky, kx = divmod(k, 3)
        dfield_sum = dfield_sum + jnp.einsum(
            "oc,orw->crw",
            conv_weight[k],
            dpre_pad[:, 2 - ky : 2 - ky + ROWS, 2 - kx : 2 - kx + COLS],
            preferred_element_type=jnp.float32,
        )
    dfield = dfield_sum.astype(jnp.bfloat16).reshape(C, PIECES, PP)
    reply = jnp.einsum("pr,cpq->rcq", select, dfield, preferred_element_type=jnp.float32).astype(
        jnp.bfloat16
    )
    back = to_sources(reply.reshape(devices, slots, C, PP))
    got = back[flat_dev, slot].reshape(blocks, K, C, PP)
    got = jnp.where(live[:, :, None, None], got, jnp.zeros((), jnp.bfloat16))
    grad_latlon = jnp.einsum(
        "bjcq,bjpq->bcp", got, intersection_weight, preferred_element_type=jnp.float32
    ).astype(jnp.bfloat16)
    return (activation, grad_conv, grad_latlon)


def solution(mesh):
    placed = (
        P(("face", "tile"), None, None),
        P(("face", "tile"), None, None, None),
        P(("face", "tile"), None),
        P(("face", "tile"), None),
        P(("face", "tile")),
        P(),
        P("face", None, "tile", None),
    )
    return jax.shard_map(
        local,
        mesh=mesh,
        in_specs=placed,
        out_specs=(P("face", None, "tile", None), P(), P(("face", "tile"), None, None)),
        check_vma=False,
    )
```

profile of v0, /device:TPU:0, one launch (start us, length us, event | category | flops | bytes accessed | tf_op | source)
XLA Modules:
  0.0 555.9 jit_solution(7310163502966046793)
XLA Ops:
  10.2 11.3 %scatter_fusion.1 = s32[32,8]{0,1:T(8,128)S(1)} fusion(s32[32,8]{0,1:T(8,128)S(1)} %broadcast_in_dim.76, s32[256]{0:T(256)S(1)} %bitcast.186, s32[256]{0:T(256)S(1)} %reshape.148), kind=kCustom, calls=%fused_computation.2 | custom fusion | bytes 5120 | tf_op jit(solution)/shard_map/scatter | solution.py:85
  22.2 7.3 %all-to-all-start.1 = ((s32[32,1,8]{2,1,0:T(1,128)}), s32[32,1,8]{2,1,0:T(1,128)S(1)}, u32[]{:S(2)}, u32[]{:S(2)}) async-start(s32[32,1,8]{2,1,0:T(1,128)} %copy.78), calls=%async_computation.1 | async-start | bytes 32768 | tf_op jit(solution)/shard_map/all_to_all | solution.py:54
  30.3 7.9 %select_convert_fusion = bf16[64,4,128,74]{2,3,1,0:T(8,128)(2,1)} fusion(pred[64,4]{1,0:T(8,128)(4,1)S(1)} %iota_compare_fusion.1, bf16[64,4,128,128]{3,2,1,0:T(8,128)(2,1)} %param.8, bf16[64,74,128,1]{2,0,1,3:T(8,128)(2,1)S(1)} %bitcast.184), kind=kOutput, calls=%fused_computation.5 | convolution fusion | flops 625606656 | bytes 14450944 | tf_op jit(solution)/shard_map/bcp,bjpq->bjcq/dot_general | solution.py:69
  38.2 3.5 broadcast_in_dim.73
  41.7 37.2 %scatter_fusion = bf16[32,8,74,128]{3,2,1,0:T(8,128)(2,1)} fusion(bf16[32,8,74,128]{3,2,1,0:T(8,128)(2,1)} %broadcast_in_dim.73, s32[256]{0:T(256)S(1)} %bitcast.187, bf16[256,74,128]{2,1,0:T(8,128)(2,1)} %bitcast.189), kind=kCustom, calls=%fused_computation.1 | custom fusion | bytes 14551040 | tf_op jit(solution)/shard_map/scatter | solution.py:82
  78.9 6.0 %copy.75 = bf16[32,8,74,128]{3,1,2,0:T(8,128)(2,1)} copy(bf16[32,8,74,128]{3,2,1,0:T(8,128)(2,1)} %scatter_fusion) | data formatting | bytes 9699328 | tf_op jit(solution)/shard_map/scatter | solution.py:82
  84.8 5.9 %all-to-all-start = ((bf16[32,8,74,128]{3,1,2,0:T(8,128)(2,1)}), bf16[32,8,74,128]{3,1,2,0:T(8,128)(2,1)}, u32[]{:S(2)}, u32[]{:S(2)}) async-start(bf16[32,8,74,128]{3,1,2,0:T(8,128)(2,1)} %copy.75), calls=%async_computation | async-start | bytes 9699328 | tf_op jit(solution)/shard_map/all_to_all | solution.py:53
  92.0 107.8 %all-to-all-done = bf16[32,8,74,128]{3,1,2,0:T(8,128)(2,1)} async-done(((bf16[32,8,74,128]{3,1,2,0:T(8,128)(2,1)}), bf16[32,8,74,128]{3,1,2,0:T(8,128)(2,1)}, u32[]{:S(2)}, u32[]{:S(2)}) %all-to-all-start) | async-done | bytes 4849696 | tf_op jit(solution)/shard_map/all_to_all | solution.py:53
  199.8 3.3 fusion.38
  204.3 3.6 collective-permute-start.1
  214.9 7.8 %copy.82 = bf16[1,256,16,512]{1,3,2,0:T(8,128)(2,1)} copy(bf16[1,256,16,512]{3,2,1,0:T(8,128)(2,1)} %param.13) | data formatting | bytes 8388608 | tf_op args[6]
  224.4 4.0 collective-permute-done.3
  231.1 5.7 %fusion.48 = f32[16,512,256]{2,1,0:T(8,128)} fusion(bf16[74,18,514]{2,0,1:T(8,128)(2,1)S(1)} %maximum_select_fusion.1, bf16[9,256,74]{1,2,0:T(8,128)(2,1)S(1)} %copy-done.7), kind=kOutput, calls=%fused_computation.56 | convolution fusion | flops 310378496 | bytes 9740288 | tf_op jit(solution)/shard_map/oc,crw->orw/dot_general | solution.py:100
  236.9 4.5 fusion.52
  241.4 5.7 %fusion.56 = f32[16,512,256]{2,1,0:T(8,128)} fusion(bf16[74,18,514]{2,0,1:T(8,128)(2,1)S(1)} %maximum_select_fusion.1, bf16[9,256,74]{1,2,0:T(8,128)(2,1)S(1)} %copy-done.7), kind=kOutput, calls=%fused_computation.64 | convolution fusion | flops 310378496 | bytes 9740288 | tf_op jit(solution)/shard_map/oc,crw->orw/dot_general | solution.py:100
  247.1 5.7 %fusion.60 = f32[16,512,256]{2,1,0:T(8,128)} fusion(bf16[74,18,514]{2,0,1:T(8,128)(2,1)S(1)} %maximum_select_fusion.1, bf16[9,256,74]{1,2,0:T(8,128)(2,1)S(1)} %copy-done.7), kind=kOutput, calls=%fused_computation.68 | convolution fusion | flops 310378496 | bytes 9740288 | tf_op jit(solution)/shard_map/oc,crw->orw/dot_general | solution.py:100
  252.9 4.5 fusion.64
  257.4 5.7 %fusion.68 = f32[16,512,256]{2,1,0:T(8,128)} fusion(bf16[74,18,514]{2,0,1:T(8,128)(2,1)S(1)} %maximum_select_fusion.1, bf16[9,256,74]{1,2,0:T(8,128)(2,1)S(1)} %copy-done.7), kind=kOutput, calls=%fused_computation.76 | convolution fusion | flops 310378496 | bytes 9740288 | tf_op jit(solution)/shard_map/oc,crw->orw/dot_general | solution.py:100
  263.1 5.7 %fusion.72 = f32[16,512,256]{2,1,0:T(8,128)} fusion(bf16[74,18,514]{2,0,1:T(8,128)(2,1)S(1)} %maximum_select_fusion.1, bf16[9,256,74]{1,2,0:T(8,128)(2,1)S(1)} %copy-done.7), kind=kOutput, calls=%fused_computation.80 | convolution fusion | flops 310378496 | bytes 9740288 | tf_op jit(solution)/shard_map/oc,crw->orw/dot_general | solution.py:100
  268.8 15.5 %fusion.76 = f32[16,512,256]{2,1,0:T(8,128)} fusion(bf16[74,18,514]{2,0,1:T(8,128)(2,1)S(1)} %maximum_select_fusion.1, bf16[9,256,74]{1,2,0:T(8,128)(2,1)S(1)} %copy-done.7), kind=kOutput, calls=%fused_computation.84 | convolution fusion | flops 310378496 | bytes 9740288 | tf_op jit(solution)/shard_map/oc,crw->orw/dot_general | solution.py:100
  284.3 24.8 %fusion.6 = (bf16[256,16,512]{0,2,1:T(8,128)(2,1)S(1)}, bf16[1,256,16,512]{1,3,2,0:T(8,128)(2,1)}) fusion(bf16[1,256,16,512]{1,3,2,0:T(8,128)(2,1)S(1)} %copy-done.4, bf16[9,256,74]{1,2,0:T(8,128)(2,1)S(1)} %copy-done.7, bf16[74,18,514]{2,0,1:T(8,128)(2,1)S(1)} %maximum_select_fusion.1, f32[16,512,256]{2,1,0:T(8,128)} %fusion.48, ...), kind=kOutput, calls=%fused_computation.12 | convolution fusion | flops 373293056 | bytes 81043456 | tf_op jit(solution)/shard_map/oc,crw->orw/dot_general | solution.py:100
  309.3 3.5 collective-permute-start.5
  312.8 5.5 collective-permute-done.4
  323.6 3.9 maximum_select_fusion
  344.8 5.1 fusion.41
  358.7 3.6 all-to-all-start.2
  362.4 3.1 fusion.81
  373.5 8.1 %copy.104 = bf16[1,256,16,512]{3,2,1,0:T(8,128)(2,1)} copy(bf16[1,256,16,512]{1,3,2,0:T(8,128)(2,1)} %get-tuple-element.15) | data formatting | bytes 8388608
  381.6 143.4 %all-reduce.2.cloned.1.call-done = f32[9,256,74]{1,2,0:T(8,128)} async-done(((f32[9,256,74]{1,2,0:T(8,128)}), f32[9,256,74]{1,2,0:T(8,128)}) %all-reduce.2.cloned.1.call-update) | async-done | bytes 682000 | tf_op jit(solution)/shard_map/psum | solution.py:120
  527.1 5.8 %copy.103 = bf16[32,8,74,128]{3,2,1,0:T(8,128)(2,1)} copy(bf16[32,8,74,128]{3,1,2,0:T(8,128)(2,1)} %all-to-all-done.2) | data formatting | bytes 9699328 | tf_op jit(solution)/shard_map/all_to_all | solution.py:59
  532.9 6.3 %gather_fusion = bf16[256,74,128]{2,1,0:T(8,128)(2,1)} fusion(bf16[32,8,74,128]{3,2,1,0:T(8,128)(2,1)} %copy.103, s32[256]{0:T(256)S(1)} %bitcast.188), kind=kCustom, calls=%fused_computation | custom fusion | bytes 9701376 | tf_op jit(solution)/shard_map/gather | solution.py:138
  539.2 8.0 %bitcast_convert_fusion = bf16[64,74,128]{2,1,0:T(8,128)(2,1)S(1)} fusion(bf16[64,4,128,128]{3,2,1,0:T(8,128)(2,1)} %param.8, bf16[64,4,74,128]{3,2,1,0:T(8,128)(2,1)} %bitcast.190, pred[64,4]{1,0:T(8,128)(4,1)S(1)} %iota_compare_fusion.1), kind=kOutput, calls=%fused_computation.43 | convolution fusion | flops 623788032 | bytes 14450944 | tf_op jit(solution)/shard_map/bjcq,bjpq->bcp/dot_general | solution.py:140
  (85 shorter events, 61.0 us)
Async XLA Ops:
  7.2 23.1 %copy-start = (bf16[64,74,128]{2,0,1:T(8,128)(2,1)S(1)}, bf16[64,74,128]{2,0,1:T(8,128)(2,1)}, u32[]{:S(2)}) copy-start(bf16[64,74,128]{2,0,1:T(8,128)(2,1)} %param.7) | copy-start | bytes 3637252
  22.2 62.6 %all-to-all-start.1 = ((s32[32,1,8]{2,1,0:T(1,128)}), s32[32,1,8]{2,1,0:T(1,128)S(1)}, u32[]{:S(2)}, u32[]{:S(2)}) async-start(s32[32,1,8]{2,1,0:T(1,128)} %copy.78), calls=%async_computation.1 | async-start | bytes 32768 | tf_op jit(solution)/shard_map/all_to_all | solution.py:54
  84.8 115.0 %all-to-all-start = ((bf16[32,8,74,128]{3,1,2,0:T(8,128)(2,1)}), bf16[32,8,74,128]{3,1,2,0:T(8,128)(2,1)}, u32[]{:S(2)}, u32[]{:S(2)}) async-start(bf16[32,8,74,128]{3,1,2,0:T(8,128)(2,1)} %copy.75), calls=%async_computation | async-start | bytes 9699328 | tf_op jit(solution)/shard_map/all_to_all | solution.py:53
  204.2 5.7 %collective-permute-start = (bf16[74,1,512]{2,0,1:T(8,128)(2,1)S(1)}, bf16[74,1,512]{2,0,1:T(8,128)(2,1)S(1)}, u32[]{:S(2)}, u32[]{:S(2)}) collective-permute-start(bf16[74,1,512]{2,0,1:T(8,128)(2,1)S(1)} %copy.141), channel_id=1, source_target_pairs={{0,1},{1,2},{2,3},{3,4},{4,5},{5,6},{6,7},{7,0},{8,9},{9,10},{10,1... | collective-permute-start | bytes 227336 | tf_op jit(solution)/shard_map/ppermute | solution.py:24
  204.3 6.3 %collective-permute-start.1 = (bf16[74,1,512]{2,0,1:T(8,128)(2,1)S(1)}, bf16[74,1,512]{2,0,1:T(8,128)(2,1)S(1)}, u32[]{:S(2)}, u32[]{:S(2)}) collective-permute-start(bf16[74,1,512]{2,0,1:T(8,128)(2,1)S(1)} %copy.142), channel_id=1, source_target_pairs={{1,0},{2,1},{3,2},{4,3},{5,4},{6,5},{7,6},{0,7},{9,8},{10,9},{11,1... | collective-permute-start | bytes 227336 | tf_op jit(solution)/shard_map/ppermute | solution.py:26
  210.6 1.1 copy-start.5
  211.9 12.5 %collective-permute-start.2 = (bf16[74,18,1]{2,0,1:T(8,128)(2,1)S(1)}, bf16[74,18,1]{2,0,1:T(8,128)(2,1)S(1)}, u32[]{:S(2)}, u32[]{:S(2)}) collective-permute-start(bf16[74,18,1]{2,0,1:T(8,128)(2,1)S(1)} %get-tuple-element.20), channel_id=1, source_target_pairs={{0,8},{8,16},{16,24},{24,0},{1,9},{9,17},{17,25},{25,1},{2,10},{10... | collective-permute-start | bytes 8000 | tf_op jit(solution)/shard_map/ppermute | solution.py:24
  212.4 16.0 %collective-permute-start.3 = (bf16[74,18,1]{2,0,1:T(8,128)(2,1)S(1)}, bf16[74,18,1]{2,0,1:T(8,128)(2,1)S(1)}, u32[]{:S(2)}, u32[]{:S(2)}) collective-permute-start(bf16[74,18,1]{2,0,1:T(8,128)(2,1)S(1)} %get-tuple-element.21), channel_id=1, source_target_pairs={{8,0},{16,8},{24,16},{0,24},{9,1},{17,9},{25,17},{1,25},{10,2},{18... | collective-permute-start | bytes 8000 | tf_op jit(solution)/shard_map/ppermute | solution.py:26
  214.9 16.2 %copy-start.7 = (bf16[9,256,74]{1,2,0:T(8,128)(2,1)S(1)}, bf16[9,256,74]{1,2,0:T(8,128)(2,1)}, u32[]{:S(2)}) copy-start(bf16[9,256,74]{1,2,0:T(8,128)(2,1)} %param.12) | copy-start | bytes 1022980
  268.8 15.5 %copy-start.4 = (bf16[1,256,16,512]{1,3,2,0:T(8,128)(2,1)S(1)}, bf16[1,256,16,512]{1,3,2,0:T(8,128)(2,1)}, u32[]{:S(2)}) copy-start(bf16[1,256,16,512]{1,3,2,0:T(8,128)(2,1)} %copy.82) | copy-start | bytes 12582916
  309.2 18.4 %copy-start.2 = (bf16[256,16,512]{0,2,1:T(8,128)(2,1)}, bf16[256,16,512]{0,2,1:T(8,128)(2,1)S(1)}, u32[]{:S(2)}) copy-start(bf16[256,16,512]{0,2,1:T(8,128)(2,1)S(1)} %get-tuple-element.14) | copy-start | bytes 12582916
  309.2 9.1 %collective-permute-start.4 = (bf16[256,1,512]{0,2,1:T(8,128)(2,1)S(1)}, bf16[256,1,512]{0,2,1:T(8,128)(2,1)S(1)}, u32[]{:S(2)}, u32[]{:S(2)}) collective-permute-start(bf16[256,1,512]{0,2,1:T(8,128)(2,1)S(1)} %get-tuple-element.18), channel_id=1, source_target_pairs={{0,1},{1,2},{2,3},{3,4},{4,5},{5,6},{6,7},{7,0},{8,9},{9,10},{10,1... | collective-permute-start | bytes 786440 | tf_op jit(solution)/shard_map/ppermute | solution.py:24
  309.3 9.1 %collective-permute-start.5 = (bf16[256,1,512]{0,2,1:T(8,128)(2,1)S(1)}, bf16[256,1,512]{0,2,1:T(8,128)(2,1)S(1)}, u32[]{:S(2)}, u32[]{:S(2)}) collective-permute-start(bf16[256,1,512]{0,2,1:T(8,128)(2,1)S(1)} %get-tuple-element.19), channel_id=1, source_target_pairs={{1,0},{2,1},{3,2},{4,3},{5,4},{6,5},{7,6},{0,7},{9,8},{10,9},{11,1... | collective-permute-start | bytes 786440 | tf_op jit(solution)/shard_map/ppermute | solution.py:26
  318.4 4.7 collective-permute-start.6
  319.9 3.8 collective-permute-start.7
  358.7 168.3 %all-to-all-start.2 = ((bf16[32,8,74,128]{3,1,2,0:T(8,128)(2,1)}), bf16[32,8,74,128]{3,1,2,0:T(8,128)(2,1)}, u32[]{:S(2)}, u32[]{:S(2)}) async-start(bf16[32,8,74,128]{3,1,2,0:T(8,128)(2,1)} %copy.102), calls=%async_computation.2 | async-start | bytes 9699328 | tf_op jit(solution)/shard_map/all_to_all | solution.py:59
  362.3 162.7 %all-reduce.2.cloned.1.call-start = ((), (), s32[]{:S(2)}) async-start(), calls=%async_computation.3 | async-start | bytes 1474560 | tf_op jit(solution)/shard_map/psum | solution.py:120
  362.4 3.5 copy-start.3
  372.6 0.9 copy-start.6
  539.2 9.4 %copy-start.1 = (bf16[64,74,128]{2,0,1:T(8,128)(2,1)S(1)}, bf16[64,74,128]{2,0,1:T(8,128)(2,1)}, u32[]{:S(2)}) copy-start(bf16[64,74,128]{2,0,1:T(8,128)(2,1)} %param.7) | copy-start | bytes 3637252
Sparse Core Ops, SparseCore 0:
  373.6 151.3 all-reduce.1
where the time goes:
time: 564 us; the launch traced here: 556 us
  waiting for transfers between devices  267 us (47%)
  matrix products  131 us (23%)
  local copies, waits for them, and re-layouts  102 us (18%)
  starting transfers between devices  30 us (5%)
  between operations  14.8 us (3%)
  other arithmetic  10.9 us (2%)
    psum x1, waiting for transfers between devices, local(): grad_sum = lax.psum(jnp.stack(terms), ('face', 'tile'))  143 us
    all_to_all x1, waiting for transfers between devices, to_owners(): lax.all_to_all(buffers[0], ('face', 'tile'), split_axis=0, concat_axis=0,...  108 us
    dot_general x9, matrix products, local(): jnp.einsum('oc,crw->orw', conv_weight[k], field_pad[:, ky:ky + ROWS, kx:k...  78 us
    scatter x2, local copies, waits for them, and re-layouts, local(): send = jnp.zeros((devices, slots, C, PP), jnp.bfloat16).at[flat_dev, slot...  43.2 us
    dot_general x9, matrix products, local(): jnp.einsum('oc,orw->crw', conv_weight[k], dpre_pad[:, 2 - ky:2 - ky + ROW...  22.3 us
    unnamed x25, local copies, waits for them, and re-layouts  21.9 us
    scatter x1, local copies, waits for them, and re-layouts, local(): jnp.full((devices, slots), -1, jnp.int32).at[flat_dev, slot]  11.3 us
  transfers between devices with their start and end apart: 12, of which 8 were waited for; matrix products, arithmetic and copies ran while one was open for 15% of the time, Pallas kernels for 0%

commit v1 on v0

v1 whole, which is shorter than its diff:
```python
import functools
import math

import jax
import jax.numpy as jnp
from jax import lax
from jax.experimental import pallas as pl
from jax.experimental.pallas import tpu as pltpu
from jax.sharding import PartitionSpec as P

C = 74
CP = 80
HID = 256
ROWS = 16
COLS = 512
PP = 128
K = 4
PIECES = 64
TILE = 16
BOTH = ("face", "tile")
VMEM_LIMIT = 58 * 1024 * 1024
F32 = jnp.float32
BF16 = jnp.bfloat16


def params():
    return pltpu.CompilerParams(vmem_limit_bytes=VMEM_LIMIT)


def whole(shape):
    return pl.BlockSpec(shape, lambda *_: (0,) * len(shape))


def smem():
    return pl.BlockSpec(memory_space=pltpu.SMEM)


def send_kernel(
    slots, part, group, dev_ref, piece_ref, counts_ref, lat_ref, weight_ref, send_ref, place_ref, lat_f, store, packed, tally, sem
):
    step = pl.program_id(0)
    blocks = lat_ref.shape[1]
    devices = send_ref.shape[0] // part
    trash = devices * part
    codes = part - TILE

    @pl.when(step == 0)
    def _():
        def clear(d, carry):
            tally[d] = 0
            at = pl.multiple_of(d * part, TILE)
            store[pl.ds(at, codes), :] = jnp.zeros((codes, PP), F32)
            store[pl.ds(at + codes, TILE), :] = jnp.full((TILE, PP), -1.0, F32)
            return carry

        lax.fori_loop(0, devices, clear, 0)
        for c in range(C):
            lat_f[c * blocks : (c + 1) * blocks, :] = lat_ref[c].astype(F32)

    for i in range(group):
        b = step * group + i
        rows = lat_f[pl.ds(b, C, stride=blocks), :].astype(BF16)
        for half in range(2):
            pair = jnp.concatenate([weight_ref[i, 2 * half], weight_ref[i, 2 * half + 1]], axis=1)
            product = jnp.dot(rows, pair, preferred_element_type=F32)
            for part_j in range(2):
                j = 2 * half + part_j
                live = j < counts_ref[b]
                d = dev_ref[b, j]
                s = tally[d]
                tally[d] = s + live.astype(jnp.int32)
                at = jnp.where(live, d * part + s, trash)
                place_ref[b * K + j] = jnp.where(live, d * (part - TILE) + s, -1)
                store[pl.ds(at, C, stride=slots), :] = product[:, part_j * PP : (part_j + 1) * PP]
                at_code = jnp.where(live, d * part + codes + s, trash)
                code = jnp.full((TILE // slots, PP), piece_ref[b, j].astype(F32), F32)
                store[pl.ds(at_code, TILE // slots, stride=slots), :] = code

    @pl.when(step == pl.num_programs(0) - 1)
    def _():
        quarter = devices // 4 * part

        def ship(k):
            return pltpu.make_async_copy(
                packed.at[pl.ds(k * quarter, quarter)], send_ref.at[pl.ds(k * quarter, quarter)], sem.at[k]
            )

        for k in range(4):

            def pack(d, carry):
                at = pl.multiple_of(k * quarter + d * part, TILE)
                packed[pl.ds(at, part), :] = store[pl.ds(at, part), :].astype(BF16)
                return carry

            lax.fori_loop(0, devices // 4, pack, 0)
            ship(k).start()
        for k in range(4):
            ship(k).wait()


def send_call(dev, piece, counts, lat, weights, devices, slots, part):
    blocks = lat.shape[1]
    group = 8
    return pl.pallas_call(
        functools.partial(send_kernel, slots, part, group),
        grid=(blocks // group,),
        in_specs=[
            smem(),
            smem(),
            smem(),
            whole(lat.shape),
            pl.BlockSpec((group, K, PP, PP), lambda g: (g, 0, 0, 0)),
        ],
        out_specs=[pl.BlockSpec(memory_space=pl.ANY), smem()],
        out_shape=[
            jax.ShapeDtypeStruct((devices * part, PP), BF16),
            jax.ShapeDtypeStruct((blocks * K,), jnp.int32),
        ],
        scratch_shapes=[
            pltpu.VMEM((CP * blocks, PP), F32),
            pltpu.VMEM((devices * part + CP * slots + 8, PP), F32),
            pltpu.VMEM((devices * part, PP), BF16),
            pltpu.SMEM((devices,), jnp.int32),
            pltpu.SemaphoreType.DMA((4,)),
        ],
        compiler_params=params(),
        name="block_products",
    )(dev, piece, counts, lat, weights)


def lane_of(shape):
    return lax.broadcasted_iota(jnp.int32, shape, 1)


def put_columns(message, row, lane, first, second):
    message = jnp.where(lane == row, first, message)
    return jnp.where(lane == 32 + row, second, message)


def gather_kernel(slots, recv_ref, field_ref, low_ref, high_ref, west_ref, east_ref, pick_ref, total):
    devices, part = recv_ref.shape[0], recv_ref.shape[1]
    per = TILE // slots
    tiles = part // TILE - 1
    keys = devices * TILE
    codes = recv_ref[:, part - TILE :, :].astype(F32).reshape(keys, PP).astype(jnp.int32)
    within = lax.rem(lax.broadcasted_iota(jnp.int32, (keys, PP), 0), TILE)
    codes = jnp.where(codes < 0, -4096, codes + within // slots * PIECES)
    wide = per * PIECES
    picks = []
    for t in range(wide // PP):
        picks.append((codes == lane_of((keys, PP)) + t * PP).astype(F32))
    pick = jnp.concatenate(picks, axis=1) if len(picks) > 1 else picks[0]
    pick_ref[...] = pick.astype(BF16)
    pick_t = jnp.transpose(pick).astype(BF16)
    total[...] = jnp.zeros(total.shape, F32)
    for t in range(0, tiles, 2):
        pair = [t, t + 1] if t + 1 < tiles else [t]
        data = [recv_ref[:, u * TILE : (u + 1) * TILE, :].reshape(keys, PP) for u in pair]
        data = jnp.concatenate(data, axis=1) if len(data) > 1 else data[0]
        sums = jnp.dot(pick_t, data, preferred_element_type=F32)
        for n, u in enumerate(pair):
            for p in range(per):
                c = u * per + p
                if c < C:
                    total[pl.ds(c, PIECES, stride=CP), :] = sums[
                        p * PIECES : (p + 1) * PIECES, n * PP : (n + 1) * PP
                    ]
    lane = lane_of((CP, PP))
    west = jnp.zeros((CP, PP), F32)
    east = jnp.zeros((CP, PP), F32)
    quarters = COLS // PP
    for r in range(ROWS):
        for q in range(quarters):
            piece = r * quarters + q
            block = total[piece * CP : (piece + 1) * CP, :]
            out = block.astype(BF16)
            field_ref[r, :, q * PP : (q + 1) * PP] = out
            if r < 2:
                low_ref[r, :, q * PP : (q + 1) * PP] = out
            if r >= ROWS - 2:
                high_ref[r - ROWS + 2, :, q * PP : (q + 1) * PP] = out
            if q == 0:
                west = put_columns(west, r + 2, lane, block[:, 0:1], block[:, 1:2])
            if q == quarters - 1:
                east = put_columns(east, r + 2, lane, block[:, PP - 2 : PP - 1], block[:, PP - 1 : PP])
    west_ref[...] = west.astype(BF16)
    east_ref[...] = east.astype(BF16)


def gather_call(recv, slots):
    devices = recv.shape[0]
    wide = TILE // slots * PIECES
    shapes = [(ROWS, CP, COLS), (2, CP, COLS), (2, CP, COLS), (CP, PP), (CP, PP), (devices * TILE, wide)]
    return pl.pallas_call(
        functools.partial(gather_kernel, slots),
        grid=(1,),
        in_specs=[whole(recv.shape)],
        out_specs=[whole(s) for s in shapes],
        out_shape=[jax.ShapeDtypeStruct(s, BF16) for s in shapes],
        scratch_shapes=[pltpu.VMEM((PIECES * CP, PP), F32)],
        compiler_params=params(),
        name="field_sum",
    )(recv)


def columns_kernel(west0, east0, top_ref, bottom_ref, west_ref, east_ref):
    lane = lane_of((CP, PP))
    west = west0[...].astype(F32)
    east = east0[...].astype(F32)
    for row, ref, i in ((0, top_ref, 0), (1, top_ref, 1), (ROWS + 2, bottom_ref, 0), (ROWS + 3, bottom_ref, 1)):
        left = ref[i, :, 0:PP].astype(F32)
        right = ref[i, :, COLS - PP : COLS].astype(F32)
        west = put_columns(west, row, lane, left[:, 0:1], left[:, 1:2])
        east = put_columns(east, row, lane, right[:, PP - 2 : PP - 1], right[:, PP - 1 : PP])
    west_ref[...] = west.astype(BF16)
    east_ref[...] = east.astype(BF16)


def columns_call(west, east, top, bottom):
    return pl.pallas_call(
        columns_kernel,
        out_shape=[jax.ShapeDtypeStruct((CP, PP), BF16)] * 2,
        name="edge_columns",
    )(west, east, top, bottom)


def gelu_parts(value):
    square = value * value
    tanh_part = jnp.tanh(value * (0.7978845608 + (0.7978845608 * 0.044715) * square))
    half = 0.5 + 0.5 * tanh_part
    inner = (0.5 * 0.7978845608) + (0.5 * 0.7978845608 * 0.134145) * square
    slope = half + value * inner * (1.0 - tanh_part * tanh_part)
    return (value * half, slope)


def conv_kernel(
    slots,
    field_ref,
    top_ref,
    bottom_ref,
    own_west,
    own_east,
    far_west,
    far_east,
    cot_ref,
    cot_top,
    cot_bottom,
    cot_cols,
    forward_ref,
    backward_ref,
    pick_ref,
    act_ref,
    grad_ref,
    reply_ref,
    stack,
    dpre,
    side,
    dfield,
    packed,
    sem,
):
    step = pl.program_id(0)
    last = ROWS + 1
    lane = lane_of((CP, PP))
    lane_wide = lane_of((CP, COLS))

    def column(ref, at):
        return jnp.sum(jnp.where(lane == at, ref[...].astype(F32), 0.0), axis=1, keepdims=True)

    def build(row, rows):
        before = column(far_west, 32 + row)
        after = column(far_east, row)
        middle = rows.astype(F32)
        left = jnp.where(lane_wide == 0, before, pltpu.roll(middle, 1, 1))
        right = jnp.where(lane_wide == COLS - 1, after, pltpu.roll(middle, COLS - 1, 1))
        stack[row, 0:CP, :] = left.astype(BF16)
        stack[row, CP : 2 * CP, :] = rows
        stack[row, 2 * CP : 3 * CP, :] = right.astype(BF16)

    @pl.when(step == 0)
    def _():
        build(0, top_ref[0])
        build(1, top_ref[1])
        build(2, field_ref[0])
        grad_ref[...] = jnp.zeros(grad_ref.shape, F32)
        wests = [far_west[...].astype(F32)] * 2 + [own_west[...].astype(F32)]
        easts = [own_east[...].astype(F32)] + [far_east[...].astype(F32)] * 2
        west_at = (0, 32, 0)
        east_at = (32, 0, 32)
        pre = jnp.zeros((HID, PP), F32)
        for ky in range(3):
            parts = []
            for kx in range(3):
                w = pltpu.roll(wests[kx], (2 * PP - west_at[kx] - ky) % PP, 1)
                e = pltpu.roll(easts[kx], (2 * PP + 64 - east_at[kx] - ky) % PP, 1)
                parts.append(jnp.where(lane < 64, w, e))
            columns = jnp.concatenate(parts, axis=0).astype(BF16)
            pre = pre + jnp.dot(forward_ref[ky], columns, preferred_element_type=F32)
        unused, slope = gelu_parts(pre)
        dcol = (cot_cols[...].astype(F32) * slope).astype(BF16).astype(F32)
        sums = jnp.zeros((3 * CP, PP), F32)
        for ky in range(3):
            moved = pltpu.roll(dcol, (PP - (2 - ky)) % PP, 1).astype(BF16)
            sums = sums + jnp.dot(backward_ref[ky], moved, preferred_element_type=F32)
        side[...] = sums

    @pl.when(step <= last)
    def _():
        for n in range(2):
            cols = slice(n * 256, (n + 1) * 256)
            pre = jnp.dot(forward_ref[0], stack[step, :, cols], preferred_element_type=F32)
            pre = pre + jnp.dot(forward_ref[1], stack[step + 1, :, cols], preferred_element_type=F32)
            pre = pre + jnp.dot(forward_ref[2], stack[step + 2, :, cols], preferred_element_type=F32)
            result, slope = gelu_parts(pre)
            cot = jnp.where(
                step == 0, cot_top[:, cols], jnp.where(step == last, cot_bottom[:, cols], cot_ref[0, :, cols])
            )
            dpre[step, :, cols] = (cot.astype(F32) * slope).astype(BF16)

            @pl.when(step < last)
            def _():
                act_ref[0, :, cols] = result.astype(BF16)

    @pl.when(step <= ROWS - 2)
    def _():
        build(step + 3, field_ref[jnp.minimum(step + 1, ROWS - 1)])

    @pl.when(step == ROWS - 1)
    def _():
        build(ROWS + 2, bottom_ref[0])

    @pl.when(step == ROWS)
    def _():
        build(ROWS + 3, bottom_ref[1])

    @pl.when((step >= 3) & (step <= ROWS + 2))
    def _():
        r = step - 3
        own = dpre[r + 1]
        for ky in range(3):
            grad_ref[ky] += lax.dot_general(
                stack[r + 1 + ky], own, (((1,), (1,)), ((), ())), preferred_element_type=F32
            )
        out = jnp.dot(backward_ref[0], dpre[r + 2], preferred_element_type=F32)
        out = out + jnp.dot(backward_ref[1], own, preferred_element_type=F32)
        out = out + jnp.dot(backward_ref[2], dpre[r], preferred_element_type=F32)
        after = jnp.sum(jnp.where(lane == 64 + r, side[0:CP, :], 0.0), axis=1, keepdims=True)
        before = jnp.sum(jnp.where(lane == r, side[2 * CP :, :], 0.0), axis=1, keepdims=True)
        rows = (
            jnp.where(lane_wide == COLS - 1, after, pltpu.roll(out[0:CP], COLS - 1, 1))
            + out[CP : 2 * CP]
            + jnp.where(lane_wide == 0, before, pltpu.roll(out[2 * CP :], 1, 1))
        )
        quarters = COLS // PP
        for q in range(quarters):
            at = pl.multiple_of((r * quarters + q) * CP, 8)
            dfield[pl.ds(at, CP), :] = rows[:, q * PP : (q + 1) * PP]

    @pl.when(step == ROWS + 2)
    def _():
        devices = packed.shape[0]
        per = TILE // slots
        tiles = packed.shape[1] // TILE
        middle = tiles // 4 * 2
        pick = pick_ref[...]

        def ship(k):
            rows = pl.ds(0, middle * TILE) if k == 0 else pl.ds(middle * TILE, (tiles - middle) * TILE)
            return pltpu.make_async_copy(packed.at[:, rows, :], reply_ref.at[:, rows, :], sem.at[k])

        for t in range(0, tiles, 2):
            pair = [t, t + 1] if t + 1 < tiles else [t]
            data = []
            for u in pair:
                chans = [
                    dfield[pl.ds(min(u * per + p, CP - 1), PIECES, stride=CP), :].astype(BF16) for p in range(per)
                ]
                data.append(jnp.concatenate(chans, axis=0) if per > 1 else chans[0])
            data = jnp.concatenate(data, axis=1) if len(data) > 1 else data[0]
            got = jnp.dot(pick, data, preferred_element_type=F32).astype(BF16)
            for n, u in enumerate(pair):
                packed[:, u * TILE : (u + 1) * TILE, :] = got[:, n * PP : (n + 1) * PP].reshape(devices, TILE, PP)
            if t + 2 == middle:
                ship(0).start()
        ship(1).start()
        ship(0).wait()
        ship(1).wait()


def conv_call(slots, part, field, top, bottom, own_west, own_east, far_west, far_east, cot, cot_top, cot_bottom, cot_cols, forward, backward, pick):
    devices = pick.shape[0] // TILE

    def row(s):
        return (jnp.clip(s - 1, 0, ROWS - 1), 0, 0)

    reply_rows = part - TILE
    return pl.pallas_call(
        functools.partial(conv_kernel, slots),
        grid=(ROWS + 3,),
        in_specs=[
            whole(field.shape),
            whole(top.shape),
            whole(bottom.shape),
            whole(own_west.shape),
            whole(own_east.shape),
            whole(far_west.shape),
            whole(far_east.shape),
            pl.BlockSpec((1, HID, COLS), row),
            whole(cot_top.shape),
            whole(cot_bottom.shape),
            whole(cot_cols.shape),
            whole(forward.shape),
            whole(backward.shape),
            whole(pick.shape),
        ],
        out_specs=[
            pl.BlockSpec((1, HID, COLS), row),
            whole((3, 3 * CP, HID)),
            pl.BlockSpec(memory_space=pl.ANY),
        ],
        out_shape=[
            jax.ShapeDtypeStruct((ROWS, HID, COLS), BF16),
            jax.ShapeDtypeStruct((3, 3 * CP, HID), F32),
            jax.ShapeDtypeStruct((devices, reply_rows, PP), BF16),
        ],
        scratch_shapes=[
            pltpu.VMEM((ROWS + 4, 3 * CP, COLS), BF16),
            pltpu.VMEM((ROWS + 2, HID, COLS), BF16),
            pltpu.VMEM((3 * CP, PP), F32),
            pltpu.VMEM((PIECES * CP, PP), F32),
            pltpu.VMEM((devices, reply_rows, PP), BF16),
            pltpu.SemaphoreType.DMA((2,)),
        ],
        compiler_params=params(),
        name="conv_level",
    )(field, top, bottom, own_west, own_east, far_west, far_east, cot, cot_top, cot_bottom, cot_cols, forward, backward, pick)


def return_kernel(slots, group, place_ref, back_ref, weight_ref, out_ref, back_f, out_f):
    step = pl.program_id(0)
    blocks = out_ref.shape[1]
    rows = back_ref.shape[0]
    chunk = 256

    @pl.when(step == 0)
    def _():
        def widen(k, carry):
            at = pl.multiple_of(k * chunk, chunk)
            back_f[pl.ds(at, chunk), :] = back_ref[pl.ds(at, chunk), :].astype(F32)
            return carry

        lax.fori_loop(0, rows // chunk, widen, 0)

    for i in range(group):
        b = step * group + i
        total = jnp.zeros((C, PP), F32)
        for half in range(2):
            got = []
            for part_j in range(2):
                at = place_ref[b * K + 2 * half + part_j]
                values = back_f[pl.ds(jnp.maximum(at, 0), C, stride=slots), :]
                got.append(jnp.where(at >= 0, values, 0.0).astype(BF16))
            pair = jnp.concatenate([weight_ref[i, 2 * half], weight_ref[i, 2 * half + 1]], axis=1)
            total = total + lax.dot_general(
                jnp.concatenate(got, axis=1), pair, (((1,), (1,)), ((), ())), preferred_element_type=F32
            )
        out_f[pl.ds(b, C, stride=blocks), :] = total

    @pl.when(step == pl.num_programs(0) - 1)
    def _():
        for c in range(C):
            out_ref[c] = out_f[c * blocks : (c + 1) * blocks, :].astype(BF16)


def return_call(place, back, weights, slots):
    blocks = weights.shape[0]
    group = 8
    return pl.pallas_call(
        functools.partial(return_kernel, slots, group),
        grid=(blocks // group,),
        in_specs=[
            smem(),
            whole(back.shape),
            pl.BlockSpec((group, K, PP, PP), lambda g: (g, 0, 0, 0)),
        ],
        out_specs=whole((C, blocks, PP)),
        out_shape=jax.ShapeDtypeStruct((C, blocks, PP), BF16),
        scratch_shapes=[
            pltpu.VMEM((back.shape[0] + CP * slots, PP), F32),
            pltpu.VMEM((CP * blocks, PP), F32),
        ],
        compiler_params=params(),
        name="block_gradients",
    )(place, back, weights)


def shift(value, axis, by, wrap):
    count = lax.axis_size(axis)
    pairs = [(i, (i + by) % count) for i in range(count) if wrap or 0 <= i + by < count]
    return lax.ppermute(value, axis, pairs)


def local(latlon, intersection_weight, target_dev, target_piece, counts, conv_weight, cotangent):
    devices = lax.axis_size("face") * lax.axis_size("tile")
    blocks = latlon.shape[0]
    slots = max(2, (blocks * K + devices - 1) // devices)
    part = -(-C * slots // TILE) * TILE + TILE

    lat = jnp.swapaxes(latlon, 0, 1)
    send, place = send_call(target_dev, target_piece, counts, lat, intersection_weight, devices, slots, part)
    recv = lax.all_to_all(send.reshape(devices, part, PP), BOTH, split_axis=0, concat_axis=0, tiled=True)

    taps = jnp.pad(conv_weight.reshape(3, 3, HID, C), ((0, 0), (0, 0), (0, 0), (0, CP - C)))
    forward = taps.transpose(0, 2, 1, 3).reshape(3, HID, 3 * CP)
    backward = taps.transpose(0, 1, 3, 2).reshape(3, 3 * CP, HID)
    cot = jnp.swapaxes(cotangent[0], 0, 1)
    cot_top = shift(cotangent[0, :, ROWS - 1, :], "tile", 1, False)
    cot_bottom = shift(cotangent[0, :, 0, :], "tile", -1, False)

    def rim(at):
        inner = cotangent[0, :, :, at]
        return jnp.concatenate([cot_top[:, at : at + 1], inner, cot_bottom[:, at : at + 1]], axis=1)

    cot_west = shift(rim(COLS - 1), "face", 1, True)
    cot_east = shift(rim(0), "face", -1, True)
    gap = jnp.zeros((HID, 64 - ROWS - 2), BF16)
    cot_cols = jnp.concatenate([cot_west, gap, cot_east, gap], axis=1)

    field, low, high, west, east, pick = gather_call(recv, slots)
    top = shift(high, "tile", 1, False)
    bottom = shift(low, "tile", -1, False)
    west, east = columns_call(west, east, top, bottom)
    far_west = shift(east, "face", 1, True)
    far_east = shift(west, "face", -1, True)
    act, grad, reply = conv_call(
        slots, part, field, top, bottom, west, east, far_west, far_east, cot, cot_top, cot_bottom, cot_cols, forward, backward, pick
    )
    activation = jnp.swapaxes(act, 0, 1)[None]
    grad = lax.psum(lax.psum(grad, "tile"), "face")
    grad = grad * (1.0 / math.sqrt(devices * ROWS * COLS))
    grad_conv = jnp.swapaxes(grad.reshape(9, CP, HID)[:, :C, :], 1, 2)

    back = lax.all_to_all(reply, BOTH, split_axis=0, concat_axis=0, tiled=True)
    back = back.reshape(devices * (part - TILE), PP)
    grad_lat = return_call(place, back, intersection_weight, slots)
    return (activation, grad_conv, jnp.swapaxes(grad_lat, 0, 1))


def solution(mesh):
    placed = (
        P(BOTH, None, None),
        P(BOTH, None, None, None),
        P(BOTH, None),
        P(BOTH, None),
        P(BOTH),
        P(),
        P("face", None, "tile", None),
    )
    return jax.shard_map(
        local,
        mesh=mesh,
        in_specs=placed,
        out_specs=(P("face", None, "tile", None), P(), P(BOTH, None, None)),
        check_vma=False,
    )
```

time: 564 us -> 377 us (0.67); the launches traced: 556 us -> 376 us
  matrix products: 131 us -> 0 us
  local copies, waits for them, and re-layouts: 102 us -> 23.9 us
  Pallas kernels: 0 us -> 69.7 us
  waiting for transfers between devices: 267 us -> 241 us
  other arithmetic: 10.9 us -> 2.14 us
    dot_general x31 -> x0, matrix products: 131 us -> none  [the longest x9 78 us: local(): jnp.einsum('oc,crw->orw', conv_weight[k], field_pad[:, ky:ky + ROWS, kx:k...]
    pallas_call x0 -> x5, Pallas kernels: none -> 69.7 us  [the longest x1 37.7 us: conv_call(): pl.pallas_call(functools.partial(conv_kernel, slots), grid=(ROWS + 3,), i...]
    scatter x3 -> x0, local copies, waits for them, and re-layouts: 54.5 us -> none  [the longest x2 43.2 us: local(): send = jnp.zeros((devices, slots, C, PP), jnp.bfloat16).at[flat_dev, slot...]
    ppermute x8, waiting for transfers between devices: 15.6 us -> 2.55 us  [shift(): return lax.ppermute(value, axis, pairs)]
    all_to_all x3 -> x2, waiting for transfers between devices: 108 us -> 96.1 us  [the longest x1 96.1 us: local(): lax.all_to_all(send.reshape(devices, part, PP), BOTH, split_axis=0, conca...]
    all_to_all x3 -> x0, local copies, waits for them, and re-layouts: 7.02 us -> none  [the longest x1 5.83 us: to_sources(): lax.all_to_all(buffer, ('face', 'tile'), split_axis=0, concat_axis=0, til...]
    select_n x2 -> x0, other arithmetic: 6.63 us -> none  [strip_edges(): jnp.where(outside[None, :, None], jnp.zeros((), padded.dtype), padded)]
    gather x1 -> x0, local copies, waits for them, and re-layouts: 6.29 us -> none  [local(): got = back[flat_dev, slot].reshape(blocks, K, C, PP)]
  transfers between devices with their start and end apart: 12 -> 12, of which waited for: 8 -> 5; matrix products, arithmetic and copies ran while one was open for 15% -> 5% of each run, Pallas kernels for 0% -> 0%
where the time goes in v1:
time: 377 us; the launch traced here: 376 us
  waiting for transfers between devices  241 us (64%)
  Pallas kernels  69.7 us (18%)
  starting transfers between devices  26 us (7%)
  local copies, waits for them, and re-layouts  23.9 us (6%)
  between operations  14.2 us (4%)
    psum x2, waiting for transfers between devices, local(): grad = lax.psum(lax.psum(grad, 'tile'), 'face')  141 us
    all_to_all x1, waiting for transfers between devices, local(): lax.all_to_all(send.reshape(devices, part, PP), BOTH, split_axis=0, conca...  96.1 us
    pallas_call x1, Pallas kernels, conv_call(): pl.pallas_call(functools.partial(conv_kernel, slots), grid=(ROWS + 3,), i...  37.7 us
    unnamed x26, local copies, waits for them, and re-layouts  20.5 us
    pallas_call x1, Pallas kernels, send_call(): pl.pallas_call(functools.partial(send_kernel, slots, part, group), grid=(...  13.2 us
    ppermute x8, starting transfers between devices, shift(): return lax.ppermute(value, axis, pairs)  12.2 us
    pallas_call x1, Pallas kernels, return_call(): pl.pallas_call(functools.partial(return_kernel, slots, group), grid=(bloc...  11.6 us
  transfers between devices with their start and end apart: 12, of which 5 were waited for; matrix products, arithmetic and copies ran while one was open for 5% of the time, Pallas kernels for 0%

profile of v1, /device:TPU:0, one launch (start us, length us, event | category | flops | bytes accessed | tf_op | source)
XLA Modules:
  0.0 376.5 jit_solution(6230147927029465844)
XLA Ops:
  7.2 1.4 copy.43.dev_ref
  8.5 1.4 copy.44.piece_ref
  9.9 13.2 %block_products.1 = (bf16[19456,128]{1,0:T(8,128)(2,1)}, s32[256]{0:T(256)}) custom-call(s32[64,4]{1,0:T(8,128)} %copy.43.dev_ref, s32[64,4]{1,0:T(8,128)} %copy.44.piece_ref, s32[64]{0:T(128)} %counts_ref.1, bf16[74,64,128]{2,1,0:T(8,128)(2,1)} %bitcast.33, bf16[64,4,128,128]{3,2,1,0:T(8,128)(2,1)} %weight_ref.3), custom_call_target="tpu_custom_call" | custom-call | tf_op jit(solution)/shard_map/block_products/pallas_call | solution.py:104
  23.1 7.4 %all-to-all-start = ((bf16[32,608,128]{2,1,0:T(8,128)(2,1)}), bf16[32,608,128]{2,1,0:T(8,128)(2,1)}, u32[]{:S(2)}, u32[]{:S(2)}) async-start(bf16[32,608,128]{2,1,0:T(8,128)(2,1)} %bitcast.28), calls=%async_computation | async-start | bytes 9961472 | tf_op jit(solution)/shard_map/all_to_all | solution.py:511
  30.5 4.7 %copy.56 = bf16[1,256,16,512]{3,1,2,0:T(8,128)(2,1)S(1)} copy(bf16[1,256,16,512]{3,2,1,0:T(8,128)(2,1)} %param.13) | data formatting | bytes 8388608 | tf_op args[6]
  35.2 2.0 copy-done
  37.2 0.7 slice_bitcast_fusion.1
  38.0 1.3 collective-permute-start.5
  39.3 3.0 collective-permute-start.4
  42.9 1.6 copy.52
  44.5 1.6 copy.53
  46.3 96.1 %all-to-all-done.recv_ref = bf16[32,608,128]{2,1,0:T(8,128)(2,1)} async-done(((bf16[32,608,128]{2,1,0:T(8,128)(2,1)}), bf16[32,608,128]{2,1,0:T(8,128)(2,1)}, u32[]{:S(2)}, u32[]{:S(2)}) %all-to-all-start) | async-done | bytes 4980768 | tf_op jit(solution)/shard_map/all_to_all | solution.py:511
  142.4 5.4 %field_sum.1 = (bf16[16,80,512]{2,1,0:T(8,128)(2,1)}, bf16[2,80,512]{2,1,0:T(8,128)(2,1)}, bf16[2,80,512]{2,1,0:T(8,128)(2,1)}, bf16[80,128]{1,0:T(8,128)(2,1)},...) custom-call(bf16[32,608,128]{2,1,0:T(8,128)(2,1)} %all-to-all-done.recv_ref), custom_call_target="tpu_custom_call" | custom-call | tf_op jit(solution)/shard_map/field_sum/pallas_call | solution.py:194
  147.8 1.6 collective-permute-start
  149.4 1.3 collective-permute-start.1
  150.8 1.4 collective-permute-start.6
  152.3 1.6 collective-permute-start.7
  154.0 0.9 copy.50.forward_ref
  155.7 1.8 edge_columns.1
  157.9 1.6 collective-permute-start.2
  159.5 0.8 pad_maximum_fusion.2.cot_cols
  160.3 1.2 collective-permute-done.3.far_east
  161.5 1.3 collective-permute-done.2.far_west
  163.4 37.7 %conv_level.1 = (bf16[16,256,512]{2,1,0:T(8,128)(2,1)}, f32[3,240,256]{2,1,0:T(8,128)}, bf16[32,592,128]{2,1,0:T(8,128)(2,1)}) custom-call(bf16[16,80,512]{2,1,0:T(8,128)(2,1)} %get-tuple-element.17.field_ref, bf16[2,80,512]{2,1,0:T(8,128)(2,1)} %copy-done.3, bf16[2,80,512]{2,1,0:T(8,128)(2,1)} %copy-done.4, bf16[80,128]{1,0:T(8,128)(2,1)} %get-tuple-element.22.own_west, ...), custom_call_target="tpu_custom_call" | custom-call | tf_op jit(solution)/shard_map/conv_level/pallas_call | solution.py:397
  201.1 6.2 %all-to-all-start.1 = ((bf16[32,592,128]{2,1,0:T(8,128)(2,1)}), bf16[32,592,128]{2,1,0:T(8,128)(2,1)}, u32[]{:S(2)}, u32[]{:S(2)}) async-start(bf16[32,592,128]{2,1,0:T(8,128)(2,1)} %get-tuple-element.28), calls=%async_computation.1 | async-start | bytes 9699328 | tf_op jit(solution)/shard_map/all_to_all | solution.py:543
  207.4 0.7 all-reduce.4.cloned.1.call-update
  208.1 92.2 %all-reduce.4.cloned.1.call-done = f32[3,240,256]{2,1,0:T(8,128)} async-done(((f32[3,240,256]{2,1,0:T(8,128)}), f32[3,240,256]{2,1,0:T(8,128)}) %all-reduce.4.cloned.1.call-update) | async-done | bytes 737296 | tf_op jit(solution)/shard_map/psum | solution.py:539
  300.4 6.5 %copy.51 = bf16[1,256,16,512]{3,2,1,0:T(8,128)(2,1)} copy(bf16[1,256,16,512]{3,1,2,0:T(8,128)(2,1)} %bitcast.29) | data formatting | bytes 8388608
  306.9 49.0 %all-reduce.6.cloned.1.call-done = f32[3,240,256]{2,1,0:T(8,128)} async-done(((f32[3,240,256]{2,1,0:T(8,128)}), f32[3,240,256]{2,1,0:T(8,128)}) %all-reduce.6.cloned.1.call-update) | async-done | bytes 737296 | tf_op jit(solution)/shard_map/psum | solution.py:539
  355.9 1.2 broadcast_multiply_fusion
  357.1 0.9 slice_bitcast_fusion
  358.0 11.6 %block_gradients.1 = bf16[74,64,128]{2,1,0:T(8,128)(2,1)} custom-call(s32[256]{0:T(256)} %get-tuple-element.27.place_ref, bf16[18944,128]{1,0:T(8,128)(2,1)} %bitcast.17.back_ref, bf16[64,4,128,128]{3,2,1,0:T(8,128)(2,1)} %weight_ref.3), custom_call_target="tpu_custom_call" | custom-call | tf_op jit(solution)/shard_map/block_gradients/pallas_call | solution.py:478
  (37 shorter events, 2.9 us)
Async XLA Ops:
  23.1 119.3 %all-to-all-start = ((bf16[32,608,128]{2,1,0:T(8,128)(2,1)}), bf16[32,608,128]{2,1,0:T(8,128)(2,1)}, u32[]{:S(2)}, u32[]{:S(2)}) async-start(bf16[32,608,128]{2,1,0:T(8,128)(2,1)} %bitcast.28), calls=%async_computation | async-start | bytes 9961472 | tf_op jit(solution)/shard_map/all_to_all | solution.py:511
  30.5 11.8 %copy-start.1 = (bf16[1,256,16,512]{3,2,1,0:T(8,128)(2,1)S(1)}, bf16[1,256,16,512]{3,2,1,0:T(8,128)(2,1)}, u32[]{:S(2)}) copy-start(bf16[1,256,16,512]{3,2,1,0:T(8,128)(2,1)} %param.13) | copy-start | bytes 12582916
  35.2 2.0 copy-start
  38.0 8.1 %collective-permute-start.5 = (bf16[256,512]{1,0:T(8,128)(2,1)}, bf16[256,512]{1,0:T(8,128)(2,1)S(1)}, u32[]{:S(2)}, u32[]{:S(2)}) collective-permute-start(bf16[256,512]{1,0:T(8,128)(2,1)} %get-tuple-element.43), channel_id=1, source_target_pairs={{1,0},{2,1},{3,2},{4,3},{5,4},{6,5},{7,6},{9,8},{10,9},{11,10},{12... | collective-permute-start | bytes 786440 | tf_op jit(solution)/shard_map/ppermute | solution.py:500
  39.3 7.0 %collective-permute-start.4 = (bf16[256,512]{1,0:T(8,128)(2,1)S(1)}, bf16[256,512]{1,0:T(8,128)(2,1)S(1)}, u32[]{:S(2)}, u32[]{:S(2)}) collective-permute-start(bf16[256,512]{1,0:T(8,128)(2,1)S(1)} %get-tuple-element.44), channel_id=1, source_target_pairs={{0,1},{1,2},{2,3},{3,4},{4,5},{5,6},{6,7},{8,9},{9,10},{10,11},{11... | collective-permute-start | bytes 786440 | tf_op jit(solution)/shard_map/ppermute | solution.py:500
  42.9 111.0 %copy-start.7 = (bf16[9,256,74]{1,2,0:T(8,128)(2,1)S(1)}, bf16[9,256,74]{1,2,0:T(8,128)(2,1)}, u32[]{:S(2)}) copy-start(bf16[9,256,74]{1,2,0:T(8,128)(2,1)} %param.12) | copy-start | bytes 1022980
  46.1 116.7 %copy-start.5 = (bf16[256,512]{1,0:T(8,128)(2,1)}, bf16[256,512]{1,0:T(8,128)(2,1)S(1)}, u32[]{:S(2)}) copy-start(bf16[256,512]{1,0:T(8,128)(2,1)S(1)} %collective-permute-done.5.cot_bottom) | copy-start | bytes 786436
  46.2 116.6 %copy-start.6 = (bf16[256,512]{1,0:T(8,128)(2,1)}, bf16[256,512]{1,0:T(8,128)(2,1)S(1)}, u32[]{:S(2)}) copy-start(bf16[256,512]{1,0:T(8,128)(2,1)S(1)} %collective-permute-done.4.cot_top) | copy-start | bytes 786436
  147.8 7.1 %collective-permute-start = (bf16[2,80,512]{2,1,0:T(8,128)(2,1)}, bf16[2,80,512]{2,1,0:T(8,128)(2,1)S(1)}, u32[]{:S(2)}, u32[]{:S(2)}) collective-permute-start(bf16[2,80,512]{2,1,0:T(8,128)(2,1)} %get-tuple-element.18), channel_id=1, source_target_pairs={{0,1},{1,2},{2,3},{3,4},{4,5},{5,6},{6,7},{8,9},{9,10},{10,11},{11... | collective-permute-start | bytes 491528 | tf_op jit(solution)/shard_map/ppermute | solution.py:500
  149.4 5.5 %collective-permute-start.1 = (bf16[2,80,512]{2,1,0:T(8,128)(2,1)}, bf16[2,80,512]{2,1,0:T(8,128)(2,1)S(1)}, u32[]{:S(2)}, u32[]{:S(2)}) collective-permute-start(bf16[2,80,512]{2,1,0:T(8,128)(2,1)} %get-tuple-element.19), channel_id=1, source_target_pairs={{1,0},{2,1},{3,2},{4,3},{5,4},{6,5},{7,6},{9,8},{10,9},{11,10},{12... | collective-permute-start | bytes 491528 | tf_op jit(solution)/shard_map/ppermute | solution.py:500
  150.8 8.7 %collective-permute-start.6 = (bf16[256,18]{1,0:T(8,128)(2,1)S(1)}, bf16[256,18]{1,0:T(8,128)(2,1)S(1)}, u32[]{:S(2)}, u32[]{:S(2)}) collective-permute-start(bf16[256,18]{1,0:T(8,128)(2,1)S(1)} %pad_maximum_fusion), channel_id=1, source_target_pairs={{0,8},{8,16},{16,24},{24,0},{1,9},{9,17},{17,25},{25,1},{2,10},{10... | collective-permute-start | bytes 27656 | tf_op jit(solution)/shard_map/ppermute | solution.py:500
  152.3 7.2 %collective-permute-start.7 = (bf16[256,18]{1,0:T(8,128)(2,1)S(1)}, bf16[256,18]{1,0:T(8,128)(2,1)S(1)}, u32[]{:S(2)}, u32[]{:S(2)}) collective-permute-start(bf16[256,18]{1,0:T(8,128)(2,1)S(1)} %pad_maximum_fusion.1), channel_id=1, source_target_pairs={{0,24},{8,0},{16,8},{24,16},{1,25},{9,1},{17,9},{25,17},{2,26},{10... | collective-permute-start | bytes 27656 | tf_op jit(solution)/shard_map/ppermute | solution.py:500
  154.0 8.8 %copy-start.2 = (bf16[3,3,256,80]{2,3,1,0:T(8,128)(2,1)}, bf16[3,3,256,80]{2,3,1,0:T(8,128)(2,1)S(1)}, u32[]{:S(2)}) copy-start(bf16[3,3,256,80]{2,3,1,0:T(8,128)(2,1)S(1)} %pad.4) | copy-start | bytes 1105924
  154.9 0.7 copy-start.3
  154.9 0.7 copy-start.4
  157.5 4.0 %collective-permute-start.3 = (bf16[80,128]{1,0:T(8,128)(2,1)}, bf16[80,128]{1,0:T(8,128)(2,1)S(1)}, u32[]{:S(2)}, u32[]{:S(2)}) collective-permute-start(bf16[80,128]{1,0:T(8,128)(2,1)} %get-tuple-element.22.own_west), channel_id=1, source_target_pairs={{0,24},{8,0},{16,8},{24,16},{1,25},{9,1},{17,9},{25,17},{2,26},{10... | collective-permute-start | bytes 61448 | tf_op jit(solution)/shard_map/ppermute | solution.py:500
  157.9 4.9 %collective-permute-start.2 = (bf16[80,128]{1,0:T(8,128)(2,1)}, bf16[80,128]{1,0:T(8,128)(2,1)S(1)}, u32[]{:S(2)}, u32[]{:S(2)}) collective-permute-start(bf16[80,128]{1,0:T(8,128)(2,1)} %get-tuple-element.23.own_east), channel_id=1, source_target_pairs={{0,8},{8,16},{16,24},{24,0},{1,9},{9,17},{17,25},{25,1},{2,10},{10... | collective-permute-start | bytes 61448 | tf_op jit(solution)/shard_map/ppermute | solution.py:500
  161.5 1.4 copy-start.8
  162.8 0.6 copy-start.9
  201.1 156.9 %all-to-all-start.1 = ((bf16[32,592,128]{2,1,0:T(8,128)(2,1)}), bf16[32,592,128]{2,1,0:T(8,128)(2,1)}, u32[]{:S(2)}, u32[]{:S(2)}) async-start(bf16[32,592,128]{2,1,0:T(8,128)(2,1)} %get-tuple-element.28), calls=%async_computation.1 | async-start | bytes 9699328 | tf_op jit(solution)/shard_map/all_to_all | solution.py:543
  207.3 93.0 %all-reduce.4.cloned.1.call-start = ((), (), s32[]{:S(2)}) async-start(), calls=%async_computation.2 | async-start | bytes 1474560 | tf_op jit(solution)/shard_map/psum | solution.py:539
  208.1 147.8 %all-reduce.6.cloned.1.call-start = ((), (), s32[]{:S(2)}) async-start(), calls=%async_computation.3 | async-start | bytes 1474560 | tf_op jit(solution)/shard_map/psum | solution.py:539
Sparse Core Ops, SparseCore 0:
  211.1 89.1 all-reduce.3
  303.7 52.1 all-reduce.5

commit v2 on v1

v2 whole, which is shorter than its diff:
```python
import functools
import math

import jax
import jax.numpy as jnp
from jax import lax
from jax.experimental import pallas as pl
from jax.experimental.pallas import tpu as pltpu
from jax.sharding import PartitionSpec as P

C = 74
CP = 80
HID = 256
ROWS = 16
COLS = 512
PP = 128
K = 4
PIECES = 64
TILE = 16
GRAD_ROWS = 768
BOTH = ("face", "tile")
VMEM_LIMIT = 58 * 1024 * 1024
F32 = jnp.float32
BF16 = jnp.bfloat16


def params():
    return pltpu.CompilerParams(vmem_limit_bytes=VMEM_LIMIT)


def whole(shape):
    return pl.BlockSpec(shape, lambda *_: (0,) * len(shape))


def smem():
    return pl.BlockSpec(memory_space=pltpu.SMEM)


def send_kernel(
    slots, part, dev_ref, piece_ref, counts_ref, lat_hbm, weight_hbm, send_ref, place_ref, lat, weights, lat_f, store, packed, tally, lat_sem, in_sem, out_sem
):
    blocks = lat.shape[1]
    devices = send_ref.shape[0] // part
    trash = devices * part
    codes = part - TILE
    chunks = in_sem.shape[0]
    group = blocks // chunks
    ships = out_sem.shape[0]
    share = devices // ships

    def load(k):
        rows = pl.ds(k * group, group)
        return pltpu.make_async_copy(weight_hbm.at[rows], weights.at[rows], in_sem.at[k])

    def ship(k):
        rows = pl.ds(k * share * part, share * part)
        return pltpu.make_async_copy(packed.at[rows], send_ref.at[rows], out_sem.at[k])

    fetch = pltpu.make_async_copy(lat_hbm, lat, lat_sem)
    fetch.start()
    for k in range(chunks):
        load(k).start()

    def clear(d, carry):
        tally[d] = 0
        at = pl.multiple_of(d * part, TILE)
        store[pl.ds(at, codes), :] = jnp.zeros((codes, PP), F32)
        store[pl.ds(at + codes, TILE), :] = jnp.full((TILE, PP), -1.0, F32)
        return carry

    lax.fori_loop(0, devices, clear, 0)

    def settle(b, carry):
        for j in range(K):
            live = j < counts_ref[b]
            d = dev_ref[j, b]
            s = tally[d]
            tally[d] = s + live.astype(jnp.int32)
            place_ref[b * K + j] = jnp.where(live, d * part + s, trash)
        return carry

    lax.fori_loop(0, blocks, settle, 0, unroll=4)
    fetch.wait()
    for c in range(C):
        lat_f[c * blocks : (c + 1) * blocks, :] = lat[c].astype(F32)

    def products(k, carry):
        load(k).wait()
        for i in range(group):
            b = k * group + i
            rows = lat_f[pl.ds(b, C, stride=blocks), :].astype(BF16)
            for half in range(2):
                pair = jnp.concatenate([weights[b, 2 * half], weights[b, 2 * half + 1]], axis=1)
                product = jnp.dot(rows, pair, preferred_element_type=F32)
                for part_j in range(2):
                    j = 2 * half + part_j
                    at = place_ref[b * K + j]
                    store[pl.ds(at, C, stride=slots), :] = product[:, part_j * PP : (part_j + 1) * PP]
                    code = jnp.full((TILE // slots, PP), piece_ref[j, b].astype(F32), F32)
                    store[pl.ds(at + codes, TILE // slots, stride=slots), :] = code
        return carry

    lax.fori_loop(0, chunks, products, 0)
    for k in range(ships):

        def pack(d, carry):
            at = pl.multiple_of((k * share + d) * part, TILE)
            packed[pl.ds(at, part), :] = store[pl.ds(at, part), :].astype(BF16)
            return carry

        lax.fori_loop(0, share, pack, 0)
        ship(k).start()
    for k in range(ships):
        ship(k).wait()


def anywhere():
    return pl.BlockSpec(memory_space=pl.ANY)


def send_call(dev, piece, counts, lat, weights, devices, slots, part):
    blocks = lat.shape[1]
    return pl.pallas_call(
        functools.partial(send_kernel, slots, part),
        in_specs=[smem(), smem(), smem(), anywhere(), anywhere()],
        out_specs=[anywhere(), smem()],
        out_shape=[
            jax.ShapeDtypeStruct((devices * part, PP), BF16),
            jax.ShapeDtypeStruct((blocks * K,), jnp.int32),
        ],
        scratch_shapes=[
            pltpu.VMEM(lat.shape, BF16),
            pltpu.VMEM(weights.shape, BF16),
            pltpu.VMEM((CP * blocks, PP), F32),
            pltpu.VMEM((devices * part + part + CP * slots, PP), F32),
            pltpu.VMEM((devices * part, PP), BF16),
            pltpu.SMEM((devices,), jnp.int32),
            pltpu.SemaphoreType.DMA,
            pltpu.SemaphoreType.DMA((4,)),
            pltpu.SemaphoreType.DMA((8,)),
        ],
        compiler_params=params(),
        name="block_products",
    )(dev, piece, counts, lat, weights)


def lane_of(shape):
    return lax.broadcasted_iota(jnp.int32, shape, 1)


def put_columns(message, row, lane, first, second):
    message = jnp.where(lane == row, first, message)
    return jnp.where(lane == 32 + row, second, message)


def gather_kernel(slots, recv_hbm, field_ref, low_ref, high_ref, west_ref, east_ref, pick_ref, recv_ref, total, sem):
    devices, part = recv_ref.shape[0], recv_ref.shape[1]
    per = TILE // slots
    tiles = part // TILE - 1
    keys = devices * TILE
    step = -(-tiles // 8) * 2
    cuts = list(range(0, tiles, step)) + [tiles]

    def load(k):
        first, end = (tiles, tiles + 1) if k == 0 else (cuts[k - 1], cuts[k])
        rows = pl.ds(first * TILE, (end - first) * TILE)
        return pltpu.make_async_copy(recv_hbm.at[:, rows, :], recv_ref.at[:, rows, :], sem.at[k])

    for k in range(len(cuts)):
        load(k).start()
    load(0).wait()
    codes = recv_ref[:, part - TILE :, :].astype(F32).reshape(keys, PP).astype(jnp.int32)
    within = lax.rem(lax.broadcasted_iota(jnp.int32, (keys, PP), 0), TILE)
    codes = jnp.where(codes < 0, -4096, codes + within // slots * PIECES)
    wide = per * PIECES
    picks = []
    for t in range(wide // PP):
        picks.append((codes == lane_of((keys, PP)) + t * PP).astype(F32))
    pick = jnp.concatenate(picks, axis=1) if len(picks) > 1 else picks[0]
    pick_ref[...] = pick.astype(BF16)
    pick_t = jnp.transpose(pick).astype(BF16)
    total[...] = jnp.zeros(total.shape, F32)
    for t in range(0, tiles, 2):
        if t in cuts:
            load(cuts.index(t) + 1).wait()
        pair = [t, t + 1] if t + 1 < tiles else [t]
        data = [recv_ref[:, u * TILE : (u + 1) * TILE, :].reshape(keys, PP) for u in pair]
        data = jnp.concatenate(data, axis=1) if len(data) > 1 else data[0]
        sums = jnp.dot(pick_t, data, preferred_element_type=F32)
        for n, u in enumerate(pair):
            for p in range(per):
                c = u * per + p
                if c < C:
                    total[pl.ds(c, PIECES, stride=CP), :] = sums[
                        p * PIECES : (p + 1) * PIECES, n * PP : (n + 1) * PP
                    ]
    lane = lane_of((CP, PP))
    west = jnp.zeros((CP, PP), F32)
    east = jnp.zeros((CP, PP), F32)
    quarters = COLS // PP
    for r in range(ROWS):
        for q in range(quarters):
            piece = r * quarters + q
            block = total[piece * CP : (piece + 1) * CP, :]
            out = block.astype(BF16)
            field_ref[r, :, q * PP : (q + 1) * PP] = out
            if r < 2:
                low_ref[r, :, q * PP : (q + 1) * PP] = out
            if r >= ROWS - 2:
                high_ref[r - ROWS + 2, :, q * PP : (q + 1) * PP] = out
            if q == 0:
                west = put_columns(west, r + 2, lane, block[:, 0:1], block[:, 1:2])
            if q == quarters - 1:
                east = put_columns(east, r + 2, lane, block[:, PP - 2 : PP - 1], block[:, PP - 1 : PP])
    west_ref[...] = west.astype(BF16)
    east_ref[...] = east.astype(BF16)


def gather_call(recv, slots):
    devices = recv.shape[0]
    wide = TILE // slots * PIECES
    shapes = [(ROWS, CP, COLS), (2, CP, COLS), (2, CP, COLS), (CP, PP), (CP, PP), (devices * TILE, wide)]
    return pl.pallas_call(
        functools.partial(gather_kernel, slots),
        grid=(1,),
        in_specs=[anywhere()],
        out_specs=[whole(s) for s in shapes],
        out_shape=[jax.ShapeDtypeStruct(s, BF16) for s in shapes],
        scratch_shapes=[
            pltpu.VMEM(recv.shape, BF16),
            pltpu.VMEM((PIECES * CP, PP), F32),
            pltpu.SemaphoreType.DMA((8,)),
        ],
        compiler_params=params(),
        name="field_sum",
    )(recv)


def columns_kernel(west0, east0, top_ref, bottom_ref, west_ref, east_ref):
    lane = lane_of((CP, PP))
    west = west0[...].astype(F32)
    east = east0[...].astype(F32)
    for row, ref, i in ((0, top_ref, 0), (1, top_ref, 1), (ROWS + 2, bottom_ref, 0), (ROWS + 3, bottom_ref, 1)):
        left = ref[i, :, 0:PP].astype(F32)
        right = ref[i, :, COLS - PP : COLS].astype(F32)
        west = put_columns(west, row, lane, left[:, 0:1], left[:, 1:2])
        east = put_columns(east, row, lane, right[:, PP - 2 : PP - 1], right[:, PP - 1 : PP])
    west_ref[...] = west.astype(BF16)
    east_ref[...] = east.astype(BF16)


def columns_call(west, east, top, bottom):
    return pl.pallas_call(
        columns_kernel,
        out_shape=[jax.ShapeDtypeStruct((CP, PP), BF16)] * 2,
        name="edge_columns",
    )(west, east, top, bottom)


def gelu_parts(value):
    square = value * value
    tanh_part = jnp.tanh(value * (0.7978845608 + (0.7978845608 * 0.044715) * square))
    half = 0.5 + 0.5 * tanh_part
    inner = (0.5 * 0.7978845608) + (0.5 * 0.7978845608 * 0.134145) * square
    slope = half + value * inner * (1.0 - tanh_part * tanh_part)
    return (value * half, slope)


def conv_kernel(
    slots,
    field_ref,
    top_ref,
    bottom_ref,
    own_west,
    own_east,
    far_west,
    far_east,
    cot_hbm,
    cot_top,
    cot_bottom,
    cot_cols,
    forward_ref,
    backward_ref,
    pick_ref,
    act_hbm,
    grad_ref,
    reply_ref,
    stack,
    dpre,
    cots,
    acts,
    side,
    dfield,
    packed,
    in_sem,
    out_sem,
    sem,
):
    step = pl.program_id(0)
    lane = lane_of((CP, PP))
    lane_wide = lane_of((CP, COLS))
    taps = 9 * CP

    def column(ref, at):
        return jnp.sum(jnp.where(lane == at, ref[...].astype(F32), 0.0), axis=1, keepdims=True)

    def build(row, rows):
        before = column(far_west, 32 + row)
        after = column(far_east, row)
        middle = rows.astype(F32)
        left = jnp.where(lane_wide == 0, before, pltpu.roll(middle, 1, 1))
        right = jnp.where(lane_wide == COLS - 1, after, pltpu.roll(middle, COLS - 1, 1))
        stack[row, 0:CP, :] = left.astype(BF16)
        stack[row, CP : 2 * CP, :] = rows
        stack[row, 2 * CP : 3 * CP, :] = right.astype(BF16)

    def load(k):
        if k < 4:
            return pltpu.make_async_copy(cot_hbm.at[pl.ds(4 * k, 4)], cots.at[pl.ds(4 * k + 1, 4)], in_sem.at[k])
        ref, row = (cot_top, 0) if k == 4 else (cot_bottom, ROWS + 1)
        return pltpu.make_async_copy(ref, cots.at[row], in_sem.at[k])

    def ship_act(k):
        return pltpu.make_async_copy(acts.at[pl.ds(4 * k + 1, 4)], act_hbm.at[pl.ds(4 * k, 4)], out_sem.at[k])

    @pl.when(step == 0)
    def _():
        for k in (4, 0, 1, 2, 3, 5):
            load(k).start()
        build(0, top_ref[0])
        build(1, top_ref[1])
        build(2, field_ref[0])
        build(3, field_ref[1])
        grad_ref[...] = jnp.zeros(grad_ref.shape, F32)
        wests = [far_west[...].astype(F32)] * 2 + [own_west[...].astype(F32)]
        easts = [own_east[...].astype(F32)] + [far_east[...].astype(F32)] * 2
        west_at = (0, 32, 0)
        east_at = (32, 0, 32)
        parts = []
        for ky in range(3):
            for kx in range(3):
                w = pltpu.roll(wests[kx], (2 * PP - west_at[kx] - ky) % PP, 1)
                e = pltpu.roll(easts[kx], (2 * PP + 64 - east_at[kx] - ky) % PP, 1)
                parts.append(jnp.where(lane < 64, w, e))
        columns = jnp.concatenate(parts, axis=0).astype(BF16)
        pre = jnp.dot(forward_ref[...], columns, preferred_element_type=F32)
        unused, slope = gelu_parts(pre)
        dcol = (cot_cols[...].astype(F32) * slope).astype(BF16).astype(F32)
        moved = [dcol] + [pltpu.roll(dcol, PP - m, 1) for m in (1, 2)]
        side[...] = jnp.dot(
            backward_ref[...], jnp.concatenate(moved, axis=0).astype(BF16), preferred_element_type=F32
        )
        load(4).wait()
        load(0).wait()

    for k in (1, 2, 3):

        @pl.when(step == 2 * k)
        def _():
            load(k).wait()

    @pl.when(step == ROWS // 2)
    def _():
        load(5).wait()

    @pl.when(step <= ROWS // 2)
    def _():
        for i in range(2):
            p = 2 * step + i
            pre = jnp.dot(
                forward_ref[...], stack[pl.ds(p, 3)].reshape(taps, COLS), preferred_element_type=F32
            )
            result, slope = gelu_parts(pre)
            dpre[p] = (cots[p].astype(F32) * slope).astype(BF16)
            acts[p] = result.astype(BF16)

    for k in range(4):

        @pl.when(step == 2 * k + 2)
        def _():
            ship_act(k).start()

    @pl.when(step < ROWS // 2 - 1)
    def _():
        for i in range(2):
            build(2 * step + 4 + i, field_ref[2 * step + 2 + i])

    @pl.when(step == ROWS // 2 - 1)
    def _():
        for i in range(2):
            build(ROWS + 2 + i, bottom_ref[i])

    @pl.when(step >= 2)
    def _():
        quarters = COLS // PP
        for i in range(2):
            r = 2 * (step - 2) + i
            out = jnp.dot(
                backward_ref[...], dpre[pl.ds(r, 3)].reshape(3 * HID, COLS), preferred_element_type=F32
            )
            after = jnp.sum(jnp.where(lane == 64 + r, side[0:CP, :], 0.0), axis=1, keepdims=True)
            before = jnp.sum(jnp.where(lane == r, side[2 * CP :, :], 0.0), axis=1, keepdims=True)
            rows = (
                jnp.where(lane_wide == COLS - 1, after, pltpu.roll(out[0:CP], COLS - 1, 1))
                + out[CP : 2 * CP]
                + jnp.where(lane_wide == 0, before, pltpu.roll(out[2 * CP :], 1, 1))
            )
            for q in range(quarters):
                at = pl.multiple_of((r * quarters + q) * CP, 8)
                dfield[pl.ds(at, CP), :] = rows[:, q * PP : (q + 1) * PP]
        first = 2 * (step - 2) + 1
        fields = [stack[pl.ds(first + i, 3)].reshape(taps, COLS) for i in range(2)]
        owns = [dpre[first + i] for i in range(2)]
        grad_ref[0:taps, :] += lax.dot_general(
            jnp.concatenate(fields, axis=1),
            jnp.concatenate(owns, axis=1),
            (((1,), (1,)), ((), ())),
            preferred_element_type=F32,
        )

    @pl.when(step == ROWS // 2 + 1)
    def _():
        devices = packed.shape[0]
        per = TILE // slots
        tiles = packed.shape[1] // TILE
        ships = sem.shape[0]
        cut = -(-tiles // (2 * ships)) * 2
        pick = pick_ref[...]

        def ship(k):
            rows = pl.ds(k * cut * TILE, (min(tiles, (k + 1) * cut) - k * cut) * TILE)
            return pltpu.make_async_copy(packed.at[:, rows, :], reply_ref.at[:, rows, :], sem.at[k])

        started = []
        for t in range(0, tiles, 2):
            pair = [t, t + 1] if t + 1 < tiles else [t]
            data = []
            for u in pair:
                chans = [
                    dfield[pl.ds(min(u * per + p, CP - 1), PIECES, stride=CP), :].astype(BF16) for p in range(per)
                ]
                data.append(jnp.concatenate(chans, axis=0) if per > 1 else chans[0])
            data = jnp.concatenate(data, axis=1) if len(data) > 1 else data[0]
            got = jnp.dot(pick, data, preferred_element_type=F32).astype(BF16)
            for n, u in enumerate(pair):
                packed[:, u * TILE : (u + 1) * TILE, :] = got[:, n * PP : (n + 1) * PP].reshape(devices, TILE, PP)
            if (t + 2) % cut == 0 or t + 2 >= tiles:
                k = t // cut
                ship(k).start()
                started.append(k)
        for k in range(4):
            ship_act(k).wait()
        for k in started:
            ship(k).wait()


def conv_call(slots, part, field, top, bottom, own_west, own_east, far_west, far_east, cot, cot_top, cot_bottom, cot_cols, forward, backward, pick):
    devices = pick.shape[0] // TILE
    reply_rows = part - TILE
    edges = [whole(x.shape) for x in (field, top, bottom, own_west, own_east, far_west, far_east)]
    return pl.pallas_call(
        functools.partial(conv_kernel, slots),
        grid=(ROWS // 2 + 2,),
        in_specs=edges
        + [anywhere(), anywhere(), anywhere()]
        + [whole(x.shape) for x in (cot_cols, forward, backward, pick)],
        out_specs=[anywhere(), whole((GRAD_ROWS, HID)), anywhere()],
        out_shape=[
            jax.ShapeDtypeStruct((ROWS, HID, COLS), BF16),
            jax.ShapeDtypeStruct((GRAD_ROWS, HID), F32),
            jax.ShapeDtypeStruct((devices, reply_rows, PP), BF16),
        ],
        scratch_shapes=[
            pltpu.VMEM((ROWS + 4, 3 * CP, COLS), BF16),
            pltpu.VMEM((ROWS + 2, HID, COLS), BF16),
            pltpu.VMEM((ROWS + 2, HID, COLS), BF16),
            pltpu.VMEM((ROWS + 2, HID, COLS), BF16),
            pltpu.VMEM((3 * CP, PP), F32),
            pltpu.VMEM((PIECES * CP, PP), F32),
            pltpu.VMEM((devices, reply_rows, PP), BF16),
            pltpu.SemaphoreType.DMA((6,)),
            pltpu.SemaphoreType.DMA((4,)),
            pltpu.SemaphoreType.DMA((4,)),
        ],
        compiler_params=params(),
        name="conv_level",
    )(field, top, bottom, own_west, own_east, far_west, far_east, cot, cot_top, cot_bottom, cot_cols, forward, backward, pick)


def return_kernel(slots, devices, place_ref, back_hbm, weight_hbm, out_ref, back, weights, back_f, out_f, back_sem, in_sem):
    blocks = out_ref.shape[1]
    chunks = in_sem.shape[0]
    group = blocks // chunks
    cuts = back_sem.shape[0]
    size = back.shape[0] // cuts
    share = devices // cuts
    rows = back.shape[0] // devices
    part = rows + TILE
    trash = devices * part

    def fetch(k):
        span = pl.ds(k * size, size)
        return pltpu.make_async_copy(back_hbm.at[span], back.at[span], back_sem.at[k])

    def load(k):
        rows = pl.ds(k * group, group)
        return pltpu.make_async_copy(weight_hbm.at[rows], weights.at[rows], in_sem.at[k])

    for k in range(cuts):
        fetch(k).start()
    for k in range(chunks):
        load(k).start()

    def widen(k, carry):
        fetch(k).wait()
        for i in range(share):
            at = pl.multiple_of((k * share + i) * rows, TILE)
            to = pl.multiple_of((k * share + i) * part, TILE)
            back_f[pl.ds(to, rows), :] = back[pl.ds(at, rows), :].astype(F32)
        return carry

    lax.fori_loop(0, cuts, widen, 0)
    back_f[pl.ds(trash, CP * slots), :] = jnp.zeros((CP * slots, PP), F32)

    def gradients(k, carry):
        load(k).wait()
        for i in range(group):
            b = k * group + i
            total = jnp.zeros((C, PP), F32)
            for half in range(2):
                got = []
                for part_j in range(2):
                    at = place_ref[b * K + 2 * half + part_j]
                    got.append(back_f[pl.ds(at, C, stride=slots), :].astype(BF16))
                pair = jnp.concatenate([weights[b, 2 * half], weights[b, 2 * half + 1]], axis=1)
                total = total + lax.dot_general(
                    jnp.concatenate(got, axis=1), pair, (((1,), (1,)), ((), ())), preferred_element_type=F32
                )
            out_f[pl.ds(b, C, stride=blocks), :] = total
        return carry

    lax.fori_loop(0, chunks, gradients, 0)
    for c in range(C):
        out_ref[c] = out_f[c * blocks : (c + 1) * blocks, :].astype(BF16)


def return_call(place, back, weights, devices, slots):
    blocks = weights.shape[0]
    return pl.pallas_call(
        functools.partial(return_kernel, slots, devices),
        grid=(1,),
        in_specs=[smem(), anywhere(), anywhere()],
        out_specs=whole((C, blocks, PP)),
        out_shape=jax.ShapeDtypeStruct((C, blocks, PP), BF16),
        scratch_shapes=[
            pltpu.VMEM(back.shape, BF16),
            pltpu.VMEM(weights.shape, BF16),
            pltpu.VMEM((back.shape[0] + devices * TILE + CP * slots, PP), F32),
            pltpu.VMEM((CP * blocks, PP), F32),
            pltpu.SemaphoreType.DMA((8,)),
            pltpu.SemaphoreType.DMA((2,)),
        ],
        compiler_params=params(),
        name="block_gradients",
    )(place, back, weights)


def shift(value, face_by, tile_by):
    faces, tiles = lax.axis_size("face"), lax.axis_size("tile")
    pairs = [
        (f * tiles + t, (f + face_by) % faces * tiles + t + tile_by)
        for f in range(faces)
        for t in range(tiles)
        if 0 <= t + tile_by < tiles
    ]
    return lax.ppermute(value, BOTH, pairs)


def swap(value, axis, bit):
    return lax.ppermute(value, axis, [(i, i ^ (1 << bit)) for i in range(lax.axis_size(axis))])


def upper(axis, bit):
    return (lax.axis_index(axis) >> bit) & 1


def fold(value, axis, bit):
    half = value.shape[0] // 2
    mine = upper(axis, bit)
    keep = lax.dynamic_slice_in_dim(value, mine * half, half, axis=0)
    send = lax.dynamic_slice_in_dim(value, (1 - mine) * half, half, axis=0)
    return keep + swap(send, axis, bit)


def unfold(value, axis, bit):
    got = swap(value, axis, bit)
    first = upper(axis, bit) == 0
    return jnp.concatenate([jnp.where(first, value, got), jnp.where(first, got, value)], axis=0)


def local(latlon, intersection_weight, target_dev, target_piece, counts, conv_weight, cotangent):
    faces, tiles = lax.axis_size("face"), lax.axis_size("tile")
    devices = faces * tiles
    blocks = latlon.shape[0]
    slots = max(2, (blocks * K + devices - 1) // devices)
    part = -(-C * slots // TILE) * TILE + TILE

    lat = jnp.swapaxes(latlon, 0, 1)
    send, place = send_call(
        target_dev.T, target_piece.T, counts, lat, intersection_weight, devices, slots, part
    )
    recv = lax.all_to_all(send.reshape(devices, part, PP), BOTH, split_axis=0, concat_axis=0, tiled=True)

    taps = jnp.pad(conv_weight.reshape(3, 3, HID, C), ((0, 0), (0, 0), (0, 0), (0, CP - C)))
    forward = taps.transpose(2, 0, 1, 3).reshape(HID, 9 * CP)
    backward = taps[::-1].transpose(1, 3, 0, 2).reshape(3 * CP, 3 * HID)
    cot = jnp.swapaxes(cotangent[0], 0, 1)
    cot_top = shift(cotangent[0, :, ROWS - 1, :], 0, 1)
    cot_bottom = shift(cotangent[0, :, 0, :], 0, -1)

    def rim(at, face_by):
        column = cotangent[0, :, :, at]
        above = shift(column[:, ROWS - 1 :], face_by, 1)
        below = shift(column[:, :1], face_by, -1)
        return [above, shift(column, face_by, 0), below]

    gap = [jnp.zeros((HID, 64 - ROWS - 2), BF16)]
    cot_cols = jnp.concatenate(rim(COLS - 1, 1) + gap + rim(0, -1) + gap, axis=1)
    recv, forward, backward, cot, cot_top, cot_bottom, cot_cols = lax.optimization_barrier(
        (recv, forward, backward, cot, cot_top, cot_bottom, cot_cols)
    )

    field, low, high, west, east, pick = gather_call(recv, slots)
    top = shift(high, 0, 1)
    bottom = shift(low, 0, -1)
    west, east = columns_call(west, east, top, bottom)
    far_west = shift(east, 1, 0)
    far_east = shift(west, -1, 0)
    act, grad, reply = conv_call(
        slots, part, field, top, bottom, west, east, far_west, far_east, cot, cot_top, cot_bottom, cot_cols, forward, backward, pick
    )
    activation = jnp.swapaxes(act, 0, 1)[None]

    back = lax.all_to_all(reply, BOTH, split_axis=0, concat_axis=0, tiled=True)

    halves = [("tile", 0)] + [("face", bit) for bit in range((faces - 1).bit_length())]
    for axis, bit in halves:
        grad = fold(grad, axis, bit)
    groups = [list(range(first, tiles, 2)) for first in range(2)]
    grad = lax.psum(grad, "tile", axis_index_groups=groups)
    grad = grad * (1.0 / math.sqrt(devices * ROWS * COLS))
    for axis, bit in reversed(halves):
        grad = unfold(grad, axis, bit)
    grad_conv = jnp.swapaxes(grad[: 9 * CP].reshape(9, CP, HID)[:, :C, :], 1, 2)

    back = back.reshape(devices * (part - TILE), PP)
    grad_lat = return_call(place, back, intersection_weight, devices, slots)
    return (activation, grad_conv, jnp.swapaxes(grad_lat, 0, 1))


def solution(mesh):
    placed = (
        P(BOTH, None, None),
        P(BOTH, None, None, None),
        P(BOTH, None),
        P(BOTH, None),
        P(BOTH),
        P(),
        P("face", None, "tile", None),
    )
    return jax.shard_map(
        local,
        mesh=mesh,
        in_specs=placed,
        out_specs=(P("face", None, "tile", None), P(), P(BOTH, None, None)),
        check_vma=False,
    )
```

time: 377 us -> 328 us (0.87)
  waiting for transfers between devices: 241 us -> 178 us
  starting transfers between devices: 26 us -> 56.2 us
  Pallas kernels: 69.7 us -> 53.2 us
    ppermute x8 -> x18, waiting for transfers between devices: 2.55 us -> 112 us  [the longest x12 63.7 us: shift(): return lax.ppermute(value, BOTH, pairs)]
    psum x2 -> x1, waiting for transfers between devices: 141 us -> 43.5 us  [local(): grad = lax.psum(grad, 'tile', axis_index_groups=groups)]
    all_to_all x1, waiting for transfers between devices: 96.1 us -> 20.4 us  [local(): lax.all_to_all(send.reshape(devices, part, PP), BOTH, split_axis=0, conca...]
    ppermute x8 -> x18, starting transfers between devices: 12.2 us -> 39.1 us  [the longest x12 30.7 us: shift(): return lax.ppermute(value, BOTH, pairs)]
    pallas_call x3, Pallas kernels: 62.5 us -> 46.8 us  [the longest x1 25.7 us: conv_call(): pl.pallas_call(functools.partial(conv_kernel, slots), grid=(ROWS // 2 + 2...]
    unnamed x26 -> x23, local copies, waits for them, and re-layouts: 20.5 us -> 18.4 us
  transfers between devices with their start and end apart: 12 -> 21, of which waited for: 5 -> 13; matrix products, arithmetic and copies ran while one was open for 5% -> 7% of each run, Pallas kernels for 0% -> 0%
where the time goes in v2:
time: 328 us
  waiting for transfers between devices  178 us (54%)
  starting transfers between devices  56.2 us (17%)
  Pallas kernels  53.2 us (16%)
  local copies, waits for them, and re-layouts  23.7 us (7%)
  between operations  14.4 us (4%)
    ppermute x12, waiting for transfers between devices, shift(): return lax.ppermute(value, BOTH, pairs)  63.7 us
    ppermute x6, waiting for transfers between devices, swap(): lax.ppermute(value, axis, [(i, i ^ 1 << bit) for i in range(lax.axis_size...  48.5 us
    psum x1, waiting for transfers between devices, local(): grad = lax.psum(grad, 'tile', axis_index_groups=groups)  43.5 us
    ppermute x12, starting transfers between devices, shift(): return lax.ppermute(value, BOTH, pairs)  30.7 us
    pallas_call x1, Pallas kernels, conv_call(): pl.pallas_call(functools.partial(conv_kernel, slots), grid=(ROWS // 2 + 2...  25.7 us
    all_to_all x1, waiting for transfers between devices, local(): lax.all_to_all(send.reshape(devices, part, PP), BOTH, split_axis=0, conca...  20.4 us
    unnamed x23, local copies, waits for them, and re-layouts  18.4 us
    pallas_call x1, Pallas kernels, send_call(): pl.pallas_call(functools.partial(send_kernel, slots, part), in_specs=[sme...  11.7 us
  transfers between devices with their start and end apart: 21, of which 13 were waited for; matrix products, arithmetic and copies ran while one was open for 7% of the time, Pallas kernels for 0%

profile of v2, /device:TPU:0, one launch (start us, length us, event | category | flops | bytes accessed | tf_op | source)
XLA Modules:
  0.0 327.7 jit_solution(13752183899380484866)
XLA Ops:
  7.2 11.7 %block_products.1 = (bf16[19456,128]{1,0:T(8,128)(2,1)}, s32[256]{0:T(256)}) custom-call(s32[4,64]{1,0:T(4,128)} %bitcast.45, s32[4,64]{1,0:T(4,128)} %bitcast.46, s32[64]{0:T(128)} %counts_ref.1, bf16[74,64,128]{2,1,0:T(8,128)(2,1)} %bitcast.39, bf16[64,4,128,128]{3,2,1,0:T(8,128)(2,1)} %weight_hbm.3), custom_call_target="tpu_custom_call" | custom-call | tf_op jit(solution)/shard_map/block_products/pallas_call | solution.py:123
  18.8 7.4 %all-to-all-start = ((bf16[32,608,128]{2,1,0:T(8,128)(2,1)}), bf16[32,608,128]{2,1,0:T(8,128)(2,1)}, u32[]{:S(2)}, u32[]{:S(2)}) async-start(bf16[32,608,128]{2,1,0:T(8,128)(2,1)} %bitcast.32), calls=%async_computation | async-start | bytes 9961472 | tf_op jit(solution)/shard_map/all_to_all | solution.py:612
  26.2 2.0 fusion
  28.3 1.6 copy.26
  30.0 3.4 %collective-permute-start.2 = (bf16[256,1]{1,0:T(8,128)(2,1)S(1)}, bf16[256,1]{1,0:T(8,128)(2,1)S(1)}, u32[]{:S(2)}, u32[]{:S(2)}) collective-permute-start(bf16[256,1]{1,0:T(8,128)(2,1)S(1)} %get-tuple-element.64), channel_id=1, source_target_pairs={{0,9},{1,10},{2,11},{3,12},{4,13},{5,14},{6,15},{8,17},{9,18},{10,... | collective-permute-start | bytes 1544 | tf_op jit(solution)/shard_map/ppermute | solution.py:576
  34.8 4.5 %copy.31 = bf16[1,256,16,512]{3,1,2,0:T(8,128)(2,1)S(1)} copy(bf16[1,256,16,512]{3,2,1,0:T(8,128)(2,1)} %param.13) | data formatting | bytes 8388608 | tf_op args[6]
  39.3 2.0 copy-done
  41.4 4.1 %collective-permute-start = (bf16[256,512]{1,0:T(8,128)(2,1)S(1)}, bf16[256,512]{1,0:T(8,128)(2,1)S(1)}, u32[]{:S(2)}, u32[]{:S(2)}) collective-permute-start(bf16[256,512]{1,0:T(8,128)(2,1)S(1)} %get-tuple-element.52), channel_id=1, source_target_pairs={{0,1},{1,2},{2,3},{3,4},{4,5},{5,6},{6,7},{8,9},{9,10},{10,11},{11... | collective-permute-start | bytes 786440 | tf_op jit(solution)/shard_map/ppermute | solution.py:576
  46.8 1.6 copy.27
  48.5 5.9 %collective-permute-start.5 = (bf16[256,1]{1,0:T(8,128)(2,1)S(1)}, bf16[256,1]{1,0:T(8,128)(2,1)S(1)}, u32[]{:S(2)}, u32[]{:S(2)}) collective-permute-start(bf16[256,1]{1,0:T(8,128)(2,1)S(1)} %get-tuple-element.62), channel_id=1, source_target_pairs={{0,25},{1,26},{2,27},{3,28},{4,29},{5,30},{6,31},{8,1},{9,2},{10,3... | collective-permute-start | bytes 1544 | tf_op jit(solution)/shard_map/ppermute | solution.py:576
  54.7 6.7 %collective-permute-start.3 = (bf16[256,16]{1,0:T(8,128)(2,1)S(1)}, bf16[256,16]{1,0:T(8,128)(2,1)S(1)}, u32[]{:S(2)}, u32[]{:S(2)}) collective-permute-start(bf16[256,16]{1,0:T(8,128)(2,1)S(1)} %bitcast.41), channel_id=1, source_target_pairs={{0,8},{1,9},{2,10},{3,11},{4,12},{5,13},{6,14},{7,15},{8,16},{9,17... | collective-permute-start | bytes 24584 | tf_op jit(solution)/shard_map/ppermute | solution.py:576
  64.7 52.3 %collective-permute-done.7 = bf16[256,1]{1,0:T(8,128)(2,1)S(1)} collective-permute-done((bf16[256,1]{1,0:T(8,128)(2,1)S(1)}, bf16[256,1]{1,0:T(8,128)(2,1)S(1)}, u32[]{:S(2)}, u32[]{:S(2)}) %collective-permute-start.7) | collective-permute-done | bytes 544 | tf_op jit(solution)/shard_map/ppermute | solution.py:576
  117.8 20.4 %all-to-all-done.recv_hbm = bf16[32,608,128]{2,1,0:T(8,128)(2,1)} async-done(((bf16[32,608,128]{2,1,0:T(8,128)(2,1)}), bf16[32,608,128]{2,1,0:T(8,128)(2,1)}, u32[]{:S(2)}, u32[]{:S(2)}) %all-to-all-start) | async-done | bytes 4980768 | tf_op jit(solution)/shard_map/all_to_all | solution.py:612
  138.2 4.6 %field_sum.1 = (bf16[16,80,512]{2,1,0:T(8,128)(2,1)}, bf16[2,80,512]{2,1,0:T(8,128)(2,1)}, bf16[2,80,512]{2,1,0:T(8,128)(2,1)}, bf16[80,128]{1,0:T(8,128)(2,1)},...) custom-call(bf16[32,608,128]{2,1,0:T(8,128)(2,1)} %all-to-all-done.recv_hbm), custom_call_target="tpu_custom_call" | custom-call | tf_op jit(solution)/shard_map/field_sum/pallas_call | solution.py:223
  142.7 1.6 collective-permute-start.8
  145.6 9.9 %collective-permute-done.9.bottom_ref = bf16[2,80,512]{2,1,0:T(8,128)(2,1)S(1)} collective-permute-done((bf16[2,80,512]{2,1,0:T(8,128)(2,1)}, bf16[2,80,512]{2,1,0:T(8,128)(2,1)S(1)}, u32[]{:S(2)}, u32[]{:S(2)}) %collective-permute-start.9) | collective-permute-done | bytes 163872 | tf_op jit(solution)/shard_map/ppermute | solution.py:576
  156.2 1.8 edge_columns.1
  159.2 1.8 collective-permute-start.11
  163.8 25.7 %conv_level.1 = (bf16[16,256,512]{2,1,0:T(8,128)(2,1)}, f32[768,256]{1,0:T(8,128)}, bf16[32,592,128]{2,1,0:T(8,128)(2,1)}) custom-call(bf16[16,80,512]{2,1,0:T(8,128)(2,1)} %get-tuple-element.25.field_ref, bf16[2,80,512]{2,1,0:T(8,128)(2,1)} %copy-done.2, bf16[2,80,512]{2,1,0:T(8,128)(2,1)} %copy-done.3, bf16[80,128]{1,0:T(8,128)(2,1)} %get-tuple-element.30.own_west, ...), custom_call_target="tpu_custom_call" | custom-call | tf_op jit(solution)/shard_map/conv_level/pallas_call | solution.py:461
  189.6 9.6 %all-to-all-start.1 = ((bf16[32,592,128]{2,1,0:T(8,128)(2,1)}), bf16[32,592,128]{2,1,0:T(8,128)(2,1)}, u32[]{:S(2)}, u32[]{:S(2)}) async-start(bf16[32,592,128]{2,1,0:T(8,128)(2,1)} %get-tuple-element.42), calls=%async_computation.1 | async-start | bytes 9699328 | tf_op jit(solution)/shard_map/all_to_all | solution.py:644
  199.6 1.5 collective-permute-done.12
  201.2 1.8 collective-permute-start.13
  203.0 34.4 %collective-permute-done.13 = f32[192,256]{1,0:T(8,128)S(1)} collective-permute-done((f32[192,256]{1,0:T(8,128)S(1)}, f32[192,256]{1,0:T(8,128)S(1)}, u32[]{:S(2)}, u32[]{:S(2)}) %collective-permute-start.13) | collective-permute-done | bytes 196640 | tf_op jit(solution)/shard_map/ppermute | solution.py:580
  237.5 1.5 collective-permute-start.14
  239.0 4.7 %collective-permute-done.14 = f32[96,256]{1,0:T(8,128)S(1)} collective-permute-done((f32[96,256]{1,0:T(8,128)S(1)}, f32[96,256]{1,0:T(8,128)S(1)}, u32[]{:S(2)}, u32[]{:S(2)}) %collective-permute-start.14) | collective-permute-done | bytes 98336 | tf_op jit(solution)/shard_map/ppermute | solution.py:580
  244.4 43.5 %all-reduce.3.cloned.1.call-done = f32[96,256]{1,0:T(8,128)} async-done(((f32[96,256]{1,0:T(8,128)}), f32[96,256]{1,0:T(8,128)}) %all-reduce.3.cloned.1.call-update) | async-done | bytes 98320 | tf_op jit(solution)/shard_map/psum | solution.py:650
  288.7 2.1 collective-permute-start.15
  290.8 2.6 collective-permute-done.15
  294.4 2.7 collective-permute-start.16
  297.1 5.2 %collective-permute-done.16 = f32[192,256]{1,0:T(8,128)S(1)} collective-permute-done((f32[192,256]{1,0:T(8,128)S(1)}, f32[192,256]{1,0:T(8,128)S(1)}, u32[]{:S(2)}, u32[]{:S(2)}) %collective-permute-start.16) | collective-permute-done | bytes 196640 | tf_op jit(solution)/shard_map/ppermute | solution.py:580
  302.4 6.5 %copy.25 = bf16[1,256,16,512]{3,2,1,0:T(8,128)(2,1)} copy(bf16[1,256,16,512]{3,1,2,0:T(8,128)(2,1)} %bitcast.33) | data formatting | bytes 8388608
  311.5 9.4 %block_gradients.1 = bf16[74,64,128]{2,1,0:T(8,128)(2,1)} custom-call(s32[256]{0:T(256)} %get-tuple-element.41.place_ref, bf16[18944,128]{1,0:T(8,128)(2,1)} %bitcast.18.back_hbm, bf16[64,4,128,128]{3,2,1,0:T(8,128)(2,1)} %weight_hbm.3), custom_call_target="tpu_custom_call" | custom-call | tf_op jit(solution)/shard_map/block_gradients/pallas_call | solution.py:549
  (63 shorter events, 18.9 us)
Async XLA Ops:
  18.8 119.3 %all-to-all-start = ((bf16[32,608,128]{2,1,0:T(8,128)(2,1)}), bf16[32,608,128]{2,1,0:T(8,128)(2,1)}, u32[]{:S(2)}, u32[]{:S(2)}) async-start(bf16[32,608,128]{2,1,0:T(8,128)(2,1)} %bitcast.32), calls=%async_computation | async-start | bytes 9961472 | tf_op jit(solution)/shard_map/all_to_all | solution.py:612
  30.0 24.7 %collective-permute-start.2 = (bf16[256,1]{1,0:T(8,128)(2,1)S(1)}, bf16[256,1]{1,0:T(8,128)(2,1)S(1)}, u32[]{:S(2)}, u32[]{:S(2)}) collective-permute-start(bf16[256,1]{1,0:T(8,128)(2,1)S(1)} %get-tuple-element.64), channel_id=1, source_target_pairs={{0,9},{1,10},{2,11},{3,12},{4,13},{5,14},{6,15},{8,17},{9,18},{10,... | collective-permute-start | bytes 1544 | tf_op jit(solution)/shard_map/ppermute | solution.py:576
  33.3 21.1 %copy-start.4 = (bf16[9,256,74]{1,2,0:T(8,128)(2,1)S(1)}, bf16[9,256,74]{1,2,0:T(8,128)(2,1)}, u32[]{:S(2)}) copy-start(bf16[9,256,74]{1,2,0:T(8,128)(2,1)} %param.12) | copy-start | bytes 1022980
  33.3 28.0 %collective-permute-start.4 = (bf16[256,1]{1,0:T(8,128)(2,1)S(1)}, bf16[256,1]{1,0:T(8,128)(2,1)S(1)}, u32[]{:S(2)}, u32[]{:S(2)}) collective-permute-start(bf16[256,1]{1,0:T(8,128)(2,1)S(1)} %get-tuple-element.63), channel_id=1, source_target_pairs={{1,8},{2,9},{3,10},{4,11},{5,12},{6,13},{7,14},{9,16},{10,17},{11,... | collective-permute-start | bytes 1544 | tf_op jit(solution)/shard_map/ppermute | solution.py:576
  39.3 2.0 copy-start
  41.4 76.4 %collective-permute-start = (bf16[256,512]{1,0:T(8,128)(2,1)S(1)}, bf16[256,512]{1,0:T(8,128)(2,1)S(1)}, u32[]{:S(2)}, u32[]{:S(2)}) collective-permute-start(bf16[256,512]{1,0:T(8,128)(2,1)S(1)} %get-tuple-element.52), channel_id=1, source_target_pairs={{0,1},{1,2},{2,3},{3,4},{4,5},{5,6},{6,7},{8,9},{9,10},{10,11},{11... | collective-permute-start | bytes 786440 | tf_op jit(solution)/shard_map/ppermute | solution.py:576
  45.5 72.3 %collective-permute-start.1 = (bf16[256,512]{1,0:T(8,128)(2,1)S(1)}, bf16[256,512]{1,0:T(8,128)(2,1)S(1)}, u32[]{:S(2)}, u32[]{:S(2)}) collective-permute-start(bf16[256,512]{1,0:T(8,128)(2,1)S(1)} %get-tuple-element.51), channel_id=1, source_target_pairs={{1,0},{2,1},{3,2},{4,3},{5,4},{6,5},{7,6},{9,8},{10,9},{11,10},{12... | collective-permute-start | bytes 786440 | tf_op jit(solution)/shard_map/ppermute | solution.py:576
  48.5 13.8 %collective-permute-start.5 = (bf16[256,1]{1,0:T(8,128)(2,1)S(1)}, bf16[256,1]{1,0:T(8,128)(2,1)S(1)}, u32[]{:S(2)}, u32[]{:S(2)}) collective-permute-start(bf16[256,1]{1,0:T(8,128)(2,1)S(1)} %get-tuple-element.62), channel_id=1, source_target_pairs={{0,25},{1,26},{2,27},{3,28},{4,29},{5,30},{6,31},{8,1},{9,2},{10,3... | collective-permute-start | bytes 1544 | tf_op jit(solution)/shard_map/ppermute | solution.py:576
  54.7 62.2 %collective-permute-start.3 = (bf16[256,16]{1,0:T(8,128)(2,1)S(1)}, bf16[256,16]{1,0:T(8,128)(2,1)S(1)}, u32[]{:S(2)}, u32[]{:S(2)}) collective-permute-start(bf16[256,16]{1,0:T(8,128)(2,1)S(1)} %bitcast.41), channel_id=1, source_target_pairs={{0,8},{1,9},{2,10},{3,11},{4,12},{5,13},{6,14},{7,15},{8,16},{9,17... | collective-permute-start | bytes 24584 | tf_op jit(solution)/shard_map/ppermute | solution.py:576
  61.4 55.5 %collective-permute-start.6 = (bf16[256,16]{1,0:T(8,128)(2,1)S(1)}, bf16[256,16]{1,0:T(8,128)(2,1)S(1)}, u32[]{:S(2)}, u32[]{:S(2)}) collective-permute-start(bf16[256,16]{1,0:T(8,128)(2,1)S(1)} %bitcast.43), channel_id=1, source_target_pairs={{0,24},{1,25},{2,26},{3,27},{4,28},{5,29},{6,30},{7,31},{8,0},{9,1... | collective-permute-start | bytes 24584 | tf_op jit(solution)/shard_map/ppermute | solution.py:576
  62.3 54.7 %collective-permute-start.7 = (bf16[256,1]{1,0:T(8,128)(2,1)S(1)}, bf16[256,1]{1,0:T(8,128)(2,1)S(1)}, u32[]{:S(2)}, u32[]{:S(2)}) collective-permute-start(bf16[256,1]{1,0:T(8,128)(2,1)S(1)} %get-tuple-element.61), channel_id=1, source_target_pairs={{1,24},{2,25},{3,26},{4,27},{5,28},{6,29},{7,30},{9,0},{10,1},{11,... | collective-permute-start | bytes 1544 | tf_op jit(solution)/shard_map/ppermute | solution.py:576
  117.8 45.4 %copy-start.5 = (bf16[256,512]{1,0:T(8,128)(2,1)}, bf16[256,512]{1,0:T(8,128)(2,1)S(1)}, u32[]{:S(2)}) copy-start(bf16[256,512]{1,0:T(8,128)(2,1)S(1)} %collective-permute-done.cot_top) | copy-start | bytes 786436
  117.8 45.4 %copy-start.6 = (bf16[256,512]{1,0:T(8,128)(2,1)}, bf16[256,512]{1,0:T(8,128)(2,1)S(1)}, u32[]{:S(2)}) copy-start(bf16[256,512]{1,0:T(8,128)(2,1)S(1)} %collective-permute-done.1.cot_bottom) | copy-start | bytes 786436
  142.7 2.9 collective-permute-start.8
  144.3 11.2 %collective-permute-start.9 = (bf16[2,80,512]{2,1,0:T(8,128)(2,1)}, bf16[2,80,512]{2,1,0:T(8,128)(2,1)S(1)}, u32[]{:S(2)}, u32[]{:S(2)}) collective-permute-start(bf16[2,80,512]{2,1,0:T(8,128)(2,1)} %get-tuple-element.27), channel_id=1, source_target_pairs={{1,0},{2,1},{3,2},{4,3},{5,4},{6,5},{7,6},{9,8},{10,9},{11,10},{12... | collective-permute-start | bytes 491528 | tf_op jit(solution)/shard_map/ppermute | solution.py:576
  145.6 9.9 %copy-start.2 = (bf16[2,80,512]{2,1,0:T(8,128)(2,1)}, bf16[2,80,512]{2,1,0:T(8,128)(2,1)S(1)}, u32[]{:S(2)}) copy-start(bf16[2,80,512]{2,1,0:T(8,128)(2,1)S(1)} %collective-permute-done.8.top_ref) | copy-start | bytes 491524
  155.5 0.7 copy-start.3
  158.1 4.9 %collective-permute-start.10 = (bf16[80,128]{1,0:T(8,128)(2,1)}, bf16[80,128]{1,0:T(8,128)(2,1)S(1)}, u32[]{:S(2)}, u32[]{:S(2)}) collective-permute-start(bf16[80,128]{1,0:T(8,128)(2,1)} %get-tuple-element.31.own_east), channel_id=1, source_target_pairs={{0,8},{1,9},{2,10},{3,11},{4,12},{5,13},{6,14},{7,15},{8,16},{9,17... | collective-permute-start | bytes 61448 | tf_op jit(solution)/shard_map/ppermute | solution.py:576
  159.2 4.0 %collective-permute-start.11 = (bf16[80,128]{1,0:T(8,128)(2,1)}, bf16[80,128]{1,0:T(8,128)(2,1)S(1)}, u32[]{:S(2)}, u32[]{:S(2)}) collective-permute-start(bf16[80,128]{1,0:T(8,128)(2,1)} %get-tuple-element.30.own_west), channel_id=1, source_target_pairs={{0,24},{1,25},{2,26},{3,27},{4,28},{5,29},{6,30},{7,31},{8,0},{9,1... | collective-permute-start | bytes 61448 | tf_op jit(solution)/shard_map/ppermute | solution.py:576
  163.0 0.6 copy-start.7
  163.2 0.6 copy-start.8
  189.6 9.7 %copy-start.1 = (f32[768,256]{1,0:T(8,128)S(1)}, f32[768,256]{1,0:T(8,128)}, u32[]{:S(2)}) copy-start(f32[768,256]{1,0:T(8,128)} %get-tuple-element.40) | copy-start | bytes 2359300
  189.6 121.9 %all-to-all-start.1 = ((bf16[32,592,128]{2,1,0:T(8,128)(2,1)}), bf16[32,592,128]{2,1,0:T(8,128)(2,1)}, u32[]{:S(2)}, u32[]{:S(2)}) async-start(bf16[32,592,128]{2,1,0:T(8,128)(2,1)} %get-tuple-element.42), calls=%async_computation.1 | async-start | bytes 9699328 | tf_op jit(solution)/shard_map/all_to_all | solution.py:644
  199.2 88.6 %all-reduce.3.cloned.1.call-start = ((), (), s32[]{:S(2)}) async-start(), calls=%async_computation.2 | async-start | bytes 196608 | tf_op jit(solution)/shard_map/psum | solution.py:650
  199.3 1.8 collective-permute-start.12
  201.2 36.2 %collective-permute-start.13 = (f32[192,256]{1,0:T(8,128)S(1)}, f32[192,256]{1,0:T(8,128)S(1)}, u32[]{:S(2)}, u32[]{:S(2)}) collective-permute-start(f32[192,256]{1,0:T(8,128)S(1)} %constant_dynamic-slice_fusion.1), channel_id=1, source_target_pairs={{0,8},{8,0},{16,24},{24,16},{1,9},{9,1},{17,25},{25,17},{2,10},{10... | collective-permute-start | bytes 589832 | tf_op jit(solution)/shard_map/ppermute | solution.py:580
  237.5 6.2 %collective-permute-start.14 = (f32[96,256]{1,0:T(8,128)S(1)}, f32[96,256]{1,0:T(8,128)S(1)}, u32[]{:S(2)}, u32[]{:S(2)}) collective-permute-start(f32[96,256]{1,0:T(8,128)S(1)} %constant_dynamic-slice_fusion), channel_id=1, source_target_pairs={{0,16},{8,24},{16,0},{24,8},{1,17},{9,25},{17,1},{25,9},{2,18},{10... | collective-permute-start | bytes 294920 | tf_op jit(solution)/shard_map/ppermute | solution.py:580
  288.7 4.7 %collective-permute-start.15 = (f32[96,256]{1,0:T(8,128)S(1)}, f32[96,256]{1,0:T(8,128)S(1)}, u32[]{:S(2)}, u32[]{:S(2)}) collective-permute-start(f32[96,256]{1,0:T(8,128)S(1)} %broadcast_multiply_fusion), channel_id=1, source_target_pairs={{0,16},{8,24},{16,0},{24,8},{1,17},{9,25},{17,1},{25,9},{2,18},{10... | collective-permute-start | bytes 294920 | tf_op jit(solution)/shard_map/ppermute | solution.py:580
  294.4 7.9 %collective-permute-start.16 = (f32[192,256]{1,0:T(8,128)S(1)}, f32[192,256]{1,0:T(8,128)S(1)}, u32[]{:S(2)}, u32[]{:S(2)}) collective-permute-start(f32[192,256]{1,0:T(8,128)S(1)} %pad_maximum_fusion.2), channel_id=1, source_target_pairs={{0,8},{8,0},{16,24},{24,16},{1,9},{9,1},{17,25},{25,17},{2,10},{10... | collective-permute-start | bytes 589832 | tf_op jit(solution)/shard_map/ppermute | solution.py:580
  302.3 6.6 %collective-permute-start.17 = (f32[384,256]{1,0:T(8,128)S(1)}, f32[384,256]{1,0:T(8,128)S(1)}, u32[]{:S(2)}, u32[]{:S(2)}) collective-permute-start(f32[384,256]{1,0:T(8,128)S(1)} %pad_maximum_fusion.1), channel_id=1, source_target_pairs={{0,1},{1,0},{2,3},{3,2},{4,5},{5,4},{6,7},{7,6},{8,9},{9,8},{10,11... | collective-permute-start | bytes 1179656 | tf_op jit(solution)/shard_map/ppermute | solution.py:580
Sparse Core Ops, SparseCore 0:
  244.5 43.2 all-reduce.2

commit v3 on v2

--- a/solution.py
+++ b/solution.py
@@ -5,6 +5,7 @@
 import jax.numpy as jnp
 from jax import lax
 from jax.experimental import pallas as pl
+from jax.experimental.layout import Layout, with_layout_constraint
 from jax.experimental.pallas import tpu as pltpu
 from jax.sharding import PartitionSpec as P
 
@@ -48,6 +49,9 @@
     ships = out_sem.shape[0]
     share = devices // ships
 
+    def slot_of(rows):
+        return lax.rem(lax.broadcasted_iota(jnp.int32, (rows, PP), 0), slots)
+
     def load(k):
         rows = pl.ds(k * group, group)
         return pltpu.make_async_copy(weight_hbm.at[rows], weights.at[rows], in_sem.at[k])
@@ -63,9 +67,6 @@
 
     def clear(d, carry):
         tally[d] = 0
-        at = pl.multiple_of(d * part, TILE)
-        store[pl.ds(at, codes), :] = jnp.zeros((codes, PP), F32)
-        store[pl.ds(at + codes, TILE), :] = jnp.full((TILE, PP), -1.0, F32)
         return carry
 
     lax.fori_loop(0, devices, clear, 0)
@@ -104,8 +105,12 @@
     for k in range(ships):
 
         def pack(d, carry):
+            used = tally[k * share + d]
             at = pl.multiple_of((k * share + d) * part, TILE)
-            packed[pl.ds(at, part), :] = store[pl.ds(at, part), :].astype(BF16)
+            values = jnp.where(slot_of(codes) < used, store[pl.ds(at, codes), :], 0.0)
+            packed[pl.ds(at, codes), :] = values.astype(BF16)
+            subtiles = jnp.where(slot_of(TILE) < used, store[pl.ds(at + codes, TILE), :], -1.0)
+            packed[pl.ds(at + codes, TILE), :] = subtiles.astype(BF16)
             return carry
 
         lax.fori_loop(0, share, pack, 0)
@@ -153,7 +158,29 @@
     return jnp.where(lane == 32 + row, second, message)
 
 
-def gather_kernel(slots, recv_hbm, field_ref, low_ref, high_ref, west_ref, east_ref, pick_ref, recv_ref, total, sem):
+def taps_kernel(weight_ref, forward_ref, backward_ref, taps):
+    taps[...] = jnp.zeros(taps.shape, F32)
+    for k in range(9):
+        taps[k * CP : k * CP + C, :] = weight_ref[k].astype(F32)
+    forward_ref[...] = jnp.transpose(taps[...]).astype(BF16)[:, 0 : 9 * CP]
+    for m in range(3):
+        rows = slice((2 - m) * 3 * CP, (3 - m) * 3 * CP)
+        backward_ref[:, m * HID : (m + 1) * HID] = taps[rows, :].astype(BF16)
+
+
+def taps_call(weight):
+    return pl.pallas_call(
+        taps_kernel,
+        out_shape=[
+            jax.ShapeDtypeStruct((HID, 9 * CP), BF16),
+            jax.ShapeDtypeStruct((3 * CP, 3 * HID), BF16),
+        ],
+        scratch_shapes=[pltpu.VMEM((GRAD_ROWS, HID), F32)],
+        name="taps",
+    )(weight)
+
+
+def gather_kernel(slots, recv_hbm, first_ref, last_ref, field_ref, low_ref, high_ref, west_ref, east_ref, pick_ref, recv_ref, total, sem):
     devices, part = recv_ref.shape[0], recv_ref.shape[1]
     per = TILE // slots
     tiles = part // TILE - 1
@@ -205,25 +232,28 @@
             out = block.astype(BF16)
             field_ref[r, :, q * PP : (q + 1) * PP] = out
             if r < 2:
-                low_ref[r, :, q * PP : (q + 1) * PP] = out
+                low_ref[r * CP : (r + 1) * CP, q * PP : (q + 1) * PP] = out
             if r >= ROWS - 2:
-                high_ref[r - ROWS + 2, :, q * PP : (q + 1) * PP] = out
+                high_ref[(r - ROWS + 2) * CP : (r - ROWS + 3) * CP, q * PP : (q + 1) * PP] = out
             if q == 0:
                 west = put_columns(west, r + 2, lane, block[:, 0:1], block[:, 1:2])
             if q == quarters - 1:
                 east = put_columns(east, r + 2, lane, block[:, PP - 2 : PP - 1], block[:, PP - 1 : PP])
     west_ref[...] = west.astype(BF16)
     east_ref[...] = east.astype(BF16)
-
-
-def gather_call(recv, slots):
+    low_ref[2 * CP :, :] = first_ref[...]
+    high_ref[2 * CP :, :] = last_ref[...]
+
+
+def gather_call(recv, first, last, slots):
     devices = recv.shape[0]
     wide = TILE // slots * PIECES
-    shapes = [(ROWS, CP, COLS), (2, CP, COLS), (2, CP, COLS), (CP, PP), (CP, PP), (devices * TILE, wide)]
+    edge = (2 * CP + HID, COLS)
+    shapes = [(ROWS, CP, COLS), edge, edge, (CP, PP), (CP, PP), (devices * TILE, wide)]
     return pl.pallas_call(
         functools.partial(gather_kernel, slots),
         grid=(1,),
-        in_specs=[anywhere()],
+        in_specs=[anywhere(), whole(first.shape), whole(last.shape)],
         out_specs=[whole(s) for s in shapes],
         out_shape=[jax.ShapeDtypeStruct(s, BF16) for s in shapes],
         scratch_shapes=[
@@ -233,28 +263,36 @@
         ],
         compiler_params=params(),
         name="field_sum",
-    )(recv)
-
-
-def columns_kernel(west0, east0, top_ref, bottom_ref, west_ref, east_ref):
+    )(recv, first, last)
+
+
+def columns_kernel(west0, east0, cot_west, cot_east, top_ref, bottom_ref, west_ref, east_ref):
     lane = lane_of((CP, PP))
     west = west0[...].astype(F32)
     east = east0[...].astype(F32)
     for row, ref, i in ((0, top_ref, 0), (1, top_ref, 1), (ROWS + 2, bottom_ref, 0), (ROWS + 3, bottom_ref, 1)):
-        left = ref[i, :, 0:PP].astype(F32)
-        right = ref[i, :, COLS - PP : COLS].astype(F32)
+        left = ref[i * CP : (i + 1) * CP, 0:PP].astype(F32)
+        right = ref[i * CP : (i + 1) * CP, COLS - PP : COLS].astype(F32)
         west = put_columns(west, row, lane, left[:, 0:1], left[:, 1:2])
         east = put_columns(east, row, lane, right[:, PP - 2 : PP - 1], right[:, PP - 1 : PP])
-    west_ref[...] = west.astype(BF16)
-    east_ref[...] = east.astype(BF16)
-
-
-def columns_call(west, east, top, bottom):
+    west_ref[0:CP, :] = west.astype(BF16)
+    east_ref[0:CP, :] = east.astype(BF16)
+    lane = lane_of((HID, PP))
+    west = cot_west[...].astype(F32)
+    east = cot_east[...].astype(F32)
+    for row, ref in ((0, top_ref), (ROWS + 1, bottom_ref)):
+        west = jnp.where(lane == row, ref[2 * CP :, 0:PP].astype(F32)[:, 0:1], west)
+        east = jnp.where(lane == row, ref[2 * CP :, COLS - PP : COLS].astype(F32)[:, PP - 1 : PP], east)
+    west_ref[CP:, :] = west.astype(BF16)
+    east_ref[CP:, :] = east.astype(BF16)
+
+
+def columns_call(west, east, cot_west, cot_east, top, bottom):
     return pl.pallas_call(
         columns_kernel,
-        out_shape=[jax.ShapeDtypeStruct((CP, PP), BF16)] * 2,
+        out_shape=[jax.ShapeDtypeStruct((CP + HID, PP), BF16)] * 2,
         name="edge_columns",
-    )(west, east, top, bottom)
+    )(west, east, cot_west, cot_east, top, bottom)
 
 
 def gelu_parts(value):
@@ -276,15 +314,13 @@
     far_west,
     far_east,
     cot_hbm,
-    cot_top,
-    cot_bottom,
-    cot_cols,
     forward_ref,
     backward_ref,
     pick_ref,
     act_hbm,
     grad_ref,
     reply_ref,
+    rims,
     stack,
     dpre,
     cots,
@@ -302,38 +338,94 @@
     taps = 9 * CP
 
     def column(ref, at):
-        return jnp.sum(jnp.where(lane == at, ref[...].astype(F32), 0.0), axis=1, keepdims=True)
-
-    def build(row, rows):
+        return jnp.sum(jnp.where(lane == at, ref[0:CP, :].astype(F32), 0.0), axis=1, keepdims=True)
+
+    def build(row):
         before = column(far_west, 32 + row)
         after = column(far_east, row)
+        rows = rims[row]
         middle = rows.astype(F32)
         left = jnp.where(lane_wide == 0, before, pltpu.roll(middle, 1, 1))
         right = jnp.where(lane_wide == COLS - 1, after, pltpu.roll(middle, COLS - 1, 1))
-        stack[row, 0:CP, :] = left.astype(BF16)
-        stack[row, CP : 2 * CP, :] = rows
-        stack[row, 2 * CP : 3 * CP, :] = right.astype(BF16)
+        return jnp.concatenate([left.astype(BF16), rows, right.astype(BF16)], axis=0)
+
+    def forward_rows():
+        return [
+            jnp.dot(
+                forward_ref[...], stack[pl.ds(2 * step + i, 3)].reshape(taps, COLS), preferred_element_type=F32
+            )
+            for i in range(2)
+        ]
+
+    def finish_rows(pres):
+        for i in range(2):
+            p = 2 * step + i
+            result, slope = gelu_parts(pres[i])
+            acts[p] = result.astype(BF16)
+            dpre[p] = (cots[p].astype(F32) * slope).astype(BF16)
+
+    def next_rows():
+        for i in range(2):
+            row = 2 * step + 4 + i
+            stack[row] = build(row)
+
+    def backward_rows():
+        first = 2 * (step - 2)
+        outs = [
+            jnp.dot(
+                backward_ref[...], dpre[pl.ds(first + i, 3)].reshape(3 * HID, COLS), preferred_element_type=F32
+            )
+            for i in range(2)
+        ]
+        fields = [stack[pl.ds(first + 1 + i, 3)].reshape(taps, COLS) for i in range(2)]
+        owns = [dpre[first + 1 + i] for i in range(2)]
+        terms = lax.dot_general(
+            jnp.concatenate(fields, axis=1),
+            jnp.concatenate(owns, axis=1),
+            (((1,), (1,)), ((), ())),
+            preferred_element_type=F32,
+        )
+        return outs, terms
+
+    def store_backward(outs, terms):
+        grad_ref[0:taps, :] += terms
+        quarters = COLS // PP
+        for i in range(2):
+            r = 2 * (step - 2) + i
+            out = outs[i]
+            after = jnp.sum(jnp.where(lane == 64 + r, side[0:CP, :], 0.0), axis=1, keepdims=True)
+            before = jnp.sum(jnp.where(lane == r, side[2 * CP :, :], 0.0), axis=1, keepdims=True)
+            rows = (
+                jnp.where(lane_wide == COLS - 1, after, pltpu.roll(out[0:CP], COLS - 1, 1))
+                + out[CP : 2 * CP]
+                + jnp.where(lane_wide == 0, before, pltpu.roll(out[2 * CP :], 1, 1))
+            )
+            for q in range(quarters):
+                at = pl.multiple_of((r * quarters + q) * CP, 8)
+                dfield[pl.ds(at, CP), :] = rows[:, q * PP : (q + 1) * PP]
 
     def load(k):
-        if k < 4:
-            return pltpu.make_async_copy(cot_hbm.at[pl.ds(4 * k, 4)], cots.at[pl.ds(4 * k + 1, 4)], in_sem.at[k])
-        ref, row = (cot_top, 0) if k == 4 else (cot_bottom, ROWS + 1)
-        return pltpu.make_async_copy(ref, cots.at[row], in_sem.at[k])
+        return pltpu.make_async_copy(cot_hbm.at[pl.ds(4 * k, 4)], cots.at[pl.ds(4 * k + 1, 4)], in_sem.at[k])
 
     def ship_act(k):
         return pltpu.make_async_copy(acts.at[pl.ds(4 * k + 1, 4)], act_hbm.at[pl.ds(4 * k, 4)], out_sem.at[k])
 
     @pl.when(step == 0)
     def _():
-        for k in (4, 0, 1, 2, 3, 5):
+        for k in range(4):
             load(k).start()
-        build(0, top_ref[0])
-        build(1, top_ref[1])
-        build(2, field_ref[0])
-        build(3, field_ref[1])
+        for i in range(2):
+            rims[i] = top_ref[i * CP : (i + 1) * CP, :]
+            rims[ROWS + 2 + i] = bottom_ref[i * CP : (i + 1) * CP, :]
+        rims[2 : ROWS + 2] = field_ref[...]
+        cots[0] = top_ref[2 * CP :, :]
+        cots[ROWS + 1] = bottom_ref[2 * CP :, :]
+        rims[ROWS + 4 : ROWS + 6] = jnp.zeros((2, CP, COLS), BF16)
+        for row in range(4):
+            stack[row] = build(row)
         grad_ref[...] = jnp.zeros(grad_ref.shape, F32)
-        wests = [far_west[...].astype(F32)] * 2 + [own_west[...].astype(F32)]
-        easts = [own_east[...].astype(F32)] + [far_east[...].astype(F32)] * 2
+        wests = [far_west[0:CP, :].astype(F32)] * 2 + [own_west[0:CP, :].astype(F32)]
+        easts = [own_east[0:CP, :].astype(F32)] + [far_east[0:CP, :].astype(F32)] * 2
         west_at = (0, 32, 0)
         east_at = (32, 0, 32)
         parts = []
@@ -345,12 +437,13 @@
         columns = jnp.concatenate(parts, axis=0).astype(BF16)
         pre = jnp.dot(forward_ref[...], columns, preferred_element_type=F32)
         unused, slope = gelu_parts(pre)
-        dcol = (cot_cols[...].astype(F32) * slope).astype(BF16).astype(F32)
+        cot_east = pltpu.roll(far_east[CP:, :].astype(F32), 64, 1)
+        cot_cols = jnp.where(lane_of((HID, PP)) < 64, far_west[CP:, :].astype(F32), cot_east)
+        dcol = (cot_cols * slope).astype(BF16).astype(F32)
         moved = [dcol] + [pltpu.roll(dcol, PP - m, 1) for m in (1, 2)]
         side[...] = jnp.dot(
             backward_ref[...], jnp.concatenate(moved, axis=0).astype(BF16), preferred_element_type=F32
         )
-        load(4).wait()
         load(0).wait()
 
     for k in (1, 2, 3):
@@ -359,64 +452,28 @@
         def _():
             load(k).wait()
 
-    @pl.when(step == ROWS // 2)
+    @pl.when(step < 2)
     def _():
-        load(5).wait()
-
-    @pl.when(step <= ROWS // 2)
+        finish_rows(forward_rows())
+        next_rows()
+
+    @pl.when((step >= 2) & (step <= ROWS // 2))
     def _():
-        for i in range(2):
-            p = 2 * step + i
-            pre = jnp.dot(
-                forward_ref[...], stack[pl.ds(p, 3)].reshape(taps, COLS), preferred_element_type=F32
-            )
-            result, slope = gelu_parts(pre)
-            dpre[p] = (cots[p].astype(F32) * slope).astype(BF16)
-            acts[p] = result.astype(BF16)
+        outs, terms = backward_rows()
+        pres = forward_rows()
+        finish_rows(pres)
+        next_rows()
+        store_backward(outs, terms)
+
+    @pl.when(step == ROWS // 2 + 1)
+    def _():
+        store_backward(*backward_rows())
 
     for k in range(4):
 
         @pl.when(step == 2 * k + 2)
         def _():
             ship_act(k).start()
-
-    @pl.when(step < ROWS // 2 - 1)
-    def _():
-        for i in range(2):
-            build(2 * step + 4 + i, field_ref[2 * step + 2 + i])
-
-    @pl.when(step == ROWS // 2 - 1)
-    def _():
-        for i in range(2):
-            build(ROWS + 2 + i, bottom_ref[i])
-
-    @pl.when(step >= 2)
-    def _():
-        quarters = COLS // PP
-        for i in range(2):
-            r = 2 * (step - 2) + i
-            out = jnp.dot(
-                backward_ref[...], dpre[pl.ds(r, 3)].reshape(3 * HID, COLS), preferred_element_type=F32
-            )
-            after = jnp.sum(jnp.where(lane == 64 + r, side[0:CP, :], 0.0), axis=1, keepdims=True)
-            before = jnp.sum(jnp.where(lane == r, side[2 * CP :, :], 0.0), axis=1, keepdims=True)
-            rows = (
-                jnp.where(lane_wide == COLS - 1, after, pltpu.roll(out[0:CP], COLS - 1, 1))
-                + out[CP : 2 * CP]
-                + jnp.where(lane_wide == 0, before, pltpu.roll(out[2 * CP :], 1, 1))
-            )
-            for q in range(quarters):
-                at = pl.multiple_of((r * quarters + q) * CP, 8)
-                dfield[pl.ds(at, CP), :] = rows[:, q * PP : (q + 1) * PP]
-        first = 2 * (step - 2) + 1
-        fields = [stack[pl.ds(first + i, 3)].reshape(taps, COLS) for i in range(2)]
-        owns = [dpre[first + i] for i in range(2)]
-        grad_ref[0:taps, :] += lax.dot_general(
-            jnp.concatenate(fields, axis=1),
-            jnp.concatenate(owns, axis=1),
-            (((1,), (1,)), ((), ())),
-            preferred_element_type=F32,
-        )
 
     @pl.when(step == ROWS // 2 + 1)
     def _():
@@ -454,7 +511,7 @@
             ship(k).wait()
 
 
-def conv_call(slots, part, field, top, bottom, own_west, own_east, far_west, far_east, cot, cot_top, cot_bottom, cot_cols, forward, backward, pick):
+def conv_call(slots, part, field, top, bottom, own_west, own_east, far_west, far_east, cot, forward, backward, pick):
     devices = pick.shape[0] // TILE
     reply_rows = part - TILE
     edges = [whole(x.shape) for x in (field, top, bottom, own_west, own_east, far_west, far_east)]
@@ -462,8 +519,8 @@
         functools.partial(conv_kernel, slots),
         grid=(ROWS // 2 + 2,),
         in_specs=edges
-        + [anywhere(), anywhere(), anywhere()]
-        + [whole(x.shape) for x in (cot_cols, forward, backward, pick)],
+        + [anywhere()]
+        + [whole(x.shape) for x in (forward, backward, pick)],
         out_specs=[anywhere(), whole((GRAD_ROWS, HID)), anywhere()],
         out_shape=[
             jax.ShapeDtypeStruct((ROWS, HID, COLS), BF16),
@@ -471,20 +528,21 @@
             jax.ShapeDtypeStruct((devices, reply_rows, PP), BF16),
         ],
         scratch_shapes=[
-            pltpu.VMEM((ROWS + 4, 3 * CP, COLS), BF16),
+            pltpu.VMEM((ROWS + 6, CP, COLS), BF16),
+            pltpu.VMEM((ROWS + 6, 3 * CP, COLS), BF16),
             pltpu.VMEM((ROWS + 2, HID, COLS), BF16),
             pltpu.VMEM((ROWS + 2, HID, COLS), BF16),
             pltpu.VMEM((ROWS + 2, HID, COLS), BF16),
             pltpu.VMEM((3 * CP, PP), F32),
             pltpu.VMEM((PIECES * CP, PP), F32),
             pltpu.VMEM((devices, reply_rows, PP), BF16),
-            pltpu.SemaphoreType.DMA((6,)),
+            pltpu.SemaphoreType.DMA((4,)),
             pltpu.SemaphoreType.DMA((4,)),
             pltpu.SemaphoreType.DMA((4,)),
         ],
         compiler_params=params(),
         name="conv_level",
-    )(field, top, bottom, own_west, own_east, far_west, far_east, cot, cot_top, cot_bottom, cot_cols, forward, backward, pick)
+    )(field, top, bottom, own_west, own_east, far_west, far_east, cot, forward, backward, pick)
 
 
 def return_kernel(slots, devices, place_ref, back_hbm, weight_hbm, out_ref, back, weights, back_f, out_f, back_sem, in_sem):
@@ -611,40 +669,32 @@
     )
     recv = lax.all_to_all(send.reshape(devices, part, PP), BOTH, split_axis=0, concat_axis=0, tiled=True)
 
-    taps = jnp.pad(conv_weight.reshape(3, 3, HID, C), ((0, 0), (0, 0), (0, 0), (0, CP - C)))
-    forward = taps.transpose(2, 0, 1, 3).reshape(HID, 9 * CP)
-    backward = taps[::-1].transpose(1, 3, 0, 2).reshape(3 * CP, 3 * HID)
+    forward, backward = taps_call(jnp.swapaxes(conv_weight, 1, 2))
     cot = jnp.swapaxes(cotangent[0], 0, 1)
-    cot_top = shift(cotangent[0, :, ROWS - 1, :], 0, 1)
-    cot_bottom = shift(cotangent[0, :, 0, :], 0, -1)
-
-    def rim(at, face_by):
-        column = cotangent[0, :, :, at]
-        above = shift(column[:, ROWS - 1 :], face_by, 1)
-        below = shift(column[:, :1], face_by, -1)
-        return [above, shift(column, face_by, 0), below]
-
-    gap = [jnp.zeros((HID, 64 - ROWS - 2), BF16)]
-    cot_cols = jnp.concatenate(rim(COLS - 1, 1) + gap + rim(0, -1) + gap, axis=1)
-    recv, forward, backward, cot, cot_top, cot_bottom, cot_cols = lax.optimization_barrier(
-        (recv, forward, backward, cot, cot_top, cot_bottom, cot_cols)
+    cot_first, cot_last = cotangent[0, :, 0, :], cotangent[0, :, ROWS - 1, :]
+    cot_west = jnp.pad(cotangent[0, :, :, 0], ((0, 0), (1, PP - ROWS - 1)))
+    cot_east = jnp.pad(cotangent[0, :, :, COLS - 1], ((0, 0), (1, PP - ROWS - 1)))
+    recv, forward, backward, cot, cot_first, cot_last, cot_west, cot_east = lax.optimization_barrier(
+        (recv, forward, backward, cot, cot_first, cot_last, cot_west, cot_east)
     )
 
-    field, low, high, west, east, pick = gather_call(recv, slots)
+    field, low, high, west, east, pick = gather_call(recv, cot_first, cot_last, slots)
     top = shift(high, 0, 1)
     bottom = shift(low, 0, -1)
-    west, east = columns_call(west, east, top, bottom)
+    west, east = columns_call(west, east, cot_west, cot_east, top, bottom)
     far_west = shift(east, 1, 0)
     far_east = shift(west, -1, 0)
     act, grad, reply = conv_call(
-        slots, part, field, top, bottom, west, east, far_west, far_east, cot, cot_top, cot_bottom, cot_cols, forward, backward, pick
+        slots, part, field, top, bottom, west, east, far_west, far_east, cot, forward, backward, pick
     )
-    activation = jnp.swapaxes(act, 0, 1)[None]
+    activation = with_layout_constraint(jnp.swapaxes(act, 0, 1), Layout((0, 1, 2)))
 
     back = lax.all_to_all(reply, BOTH, split_axis=0, concat_axis=0, tiled=True)
 
     halves = [("tile", 0)] + [("face", bit) for bit in range((faces - 1).bit_length())]
-    for axis, bit in halves:
+    grad = fold(grad, *halves[0])
+    grad, activation = lax.optimization_barrier((grad, activation))
+    for axis, bit in halves[1:]:
         grad = fold(grad, axis, bit)
     groups = [list(range(first, tiles, 2)) for first in range(2)]
     grad = lax.psum(grad, "tile", axis_index_groups=groups)
@@ -655,7 +705,7 @@
 
     back = back.reshape(devices * (part - TILE), PP)
     grad_lat = return_call(place, back, intersection_weight, devices, slots)
-    return (activation, grad_conv, jnp.swapaxes(grad_lat, 0, 1))
+    return (activation[None], grad_conv, jnp.swapaxes(grad_lat, 0, 1))
 
 
 def solution(mesh):

time: 328 us -> 318 us (0.970)
  starting transfers between devices: 56.2 us -> 30 us
  waiting for transfers between devices: 178 us -> 196 us
    all_to_all x1, waiting for transfers between devices: 20.4 us -> 96.2 us  [local(): lax.all_to_all(send.reshape(devices, part, PP), BOTH, split_axis=0, conca...]
    ppermute x12 -> x4, waiting for transfers between devices: 63.7 us -> 5.89 us  [shift(): return lax.ppermute(value, BOTH, pairs)]
    ppermute x12 -> x4, starting transfers between devices: 30.7 us -> 5.81 us  [shift(): return lax.ppermute(value, BOTH, pairs)]
    unnamed x23 -> x15, local copies, waits for them, and re-layouts: 18.4 us -> 11.3 us
    pallas_call x0 -> x1, local copies, waits for them, and re-layouts: none -> 6.54 us  [conv_call(): pl.pallas_call(functools.partial(conv_kernel, slots), grid=(ROWS // 2 + 2...]
    all_to_all x1, waiting for transfers between devices: 1.5 us -> 6.34 us  [local(): back = lax.all_to_all(reply, BOTH, split_axis=0, concat_axis=0, tiled=True)]
    ppermute x6, waiting for transfers between devices: 48.5 us -> 43.7 us  [swap(): lax.ppermute(value, axis, [(i, i ^ 1 << bit) for i in range(lax.axis_size...]
    pallas_call x1, Pallas kernels: 25.7 us -> 21.7 us  [conv_call(): pl.pallas_call(functools.partial(conv_kernel, slots), grid=(ROWS // 2 + 2...]
  transfers between devices with their start and end apart: 21 -> 13, of which waited for: 13 -> 12; matrix products, arithmetic and copies ran while one was open for 7% -> 8% of each run, Pallas kernels for 0% -> 1%
where the time goes in v3:
time: 318 us
  waiting for transfers between devices  196 us (62%)
  Pallas kernels  52.7 us (17%)
  starting transfers between devices  30 us (9%)
  local copies, waits for them, and re-layouts  22.7 us (7%)
  between operations  14.2 us (4%)
    all_to_all x1, waiting for transfers between devices, local(): lax.all_to_all(send.reshape(devices, part, PP), BOTH, split_axis=0, conca...  96.2 us
    ppermute x6, waiting for transfers between devices, swap(): lax.ppermute(value, axis, [(i, i ^ 1 << bit) for i in range(lax.axis_size...  43.7 us
    psum x1, waiting for transfers between devices, local(): grad = lax.psum(grad, 'tile', axis_index_groups=groups)  43.5 us
    pallas_call x1, Pallas kernels, conv_call(): pl.pallas_call(functools.partial(conv_kernel, slots), grid=(ROWS // 2 + 2...  21.7 us
    pallas_call x1, Pallas kernels, send_call(): pl.pallas_call(functools.partial(send_kernel, slots, part), in_specs=[sme...  11.8 us
    unnamed x15, local copies, waits for them, and re-layouts  11.3 us
    pallas_call x1, Pallas kernels, return_call(): pl.pallas_call(functools.partial(return_kernel, slots, devices), grid=(1,...  9.39 us
    ppermute x6, starting transfers between devices, swap(): lax.ppermute(value, axis, [(i, i ^ 1 << bit) for i in range(lax.axis_size...  8.39 us
  transfers between devices with their start and end apart: 13, of which 12 were waited for; matrix products, arithmetic and copies ran while one was open for 8% of the time, Pallas kernels for 1%

profile of v3, /device:TPU:0, one launch (start us, length us, event | category | flops | bytes accessed | tf_op | source)
XLA Modules:
  0.0 317.9 jit_solution(9764238133128530738)
XLA Ops:
  7.2 11.8 %block_products.1 = (bf16[19456,128]{1,0:T(8,128)(2,1)}, s32[256]{0:T(256)}) custom-call(s32[4,64]{1,0:T(4,128)} %bitcast.33, s32[4,64]{1,0:T(4,128)} %bitcast.34, s32[64]{0:T(128)} %counts_ref.1, bf16[74,64,128]{2,1,0:T(8,128)(2,1)} %bitcast.29, bf16[64,4,128,128]{3,2,1,0:T(8,128)(2,1)} %weight_hbm.3), custom_call_target="tpu_custom_call" | custom-call | tf_op jit(solution)/shard_map/block_products/pallas_call | solution.py:128
  19.0 7.4 %all-to-all-start = ((bf16[32,608,128]{2,1,0:T(8,128)(2,1)}), bf16[32,608,128]{2,1,0:T(8,128)(2,1)}, u32[]{:S(2)}, u32[]{:S(2)}) async-start(bf16[32,608,128]{2,1,0:T(8,128)(2,1)} %bitcast.25), calls=%async_computation | async-start | bytes 9961472 | tf_op jit(solution)/shard_map/all_to_all | solution.py:670
  26.4 6.7 %copy.22 = bf16[1,256,16,512]{3,1,2,0:T(8,128)(2,1)} copy(bf16[1,256,16,512]{3,2,1,0:T(8,128)(2,1)} %param.13) | data formatting | bytes 8388608 | tf_op args[6]
  33.7 1.6 copy.16
  35.3 1.6 copy.17
  38.3 1.9 taps.1
  40.3 1.9 slice_bitcast_fusion.1
  42.2 96.2 %all-to-all-done.recv_hbm = bf16[32,608,128]{2,1,0:T(8,128)(2,1)} async-done(((bf16[32,608,128]{2,1,0:T(8,128)(2,1)}), bf16[32,608,128]{2,1,0:T(8,128)(2,1)}, u32[]{:S(2)}, u32[]{:S(2)}) %all-to-all-start) | async-done | bytes 4980768 | tf_op jit(solution)/shard_map/all_to_all | solution.py:670
  138.3 5.8 %field_sum.1 = (bf16[16,80,512]{2,1,0:T(8,128)(2,1)}, bf16[416,512]{1,0:T(8,128)(2,1)}, bf16[416,512]{1,0:T(8,128)(2,1)}, bf16[80,128]{1,0:T(8,128)(2,1)}, bf16[...) custom-call(bf16[32,608,128]{2,1,0:T(8,128)(2,1)} %all-to-all-done.recv_hbm, bf16[256,512]{1,0:T(8,128)(2,1)} %get-tuple-element.32.first_ref, ...), custom_call_target="tpu_custom_call" | custom-call | tf_op jit(solution)/shard_map/field_sum/pallas_call | solution.py:253
  144.1 1.6 collective-permute-start
  145.7 1.3 collective-permute-start.1
  147.3 2.3 collective-permute-done.1.bottom_ref
  150.3 2.2 edge_columns.1
  152.5 1.3 collective-permute-start.2
  153.8 1.6 collective-permute-start.3
  155.4 2.7 collective-permute-done.2.far_west
  159.4 21.7 %conv_level.1 = (bf16[16,256,512]{2,1,0:T(8,128)(2,1)}, f32[768,256]{1,0:T(8,128)}, bf16[32,592,128]{2,1,0:T(8,128)(2,1)}) custom-call(bf16[16,80,512]{2,1,0:T(8,128)(2,1)} %get-tuple-element.34.field_ref, bf16[416,512]{1,0:T(8,128)(2,1)} %copy-done.1, bf16[416,512]{1,0:T(8,128)(2,1)} %copy-done.2, bf16[336,128]{1,0:T(8,128)(2,1)} %get-tuple-element.41.own_west, ...), custom_call_target="tpu_custom_call" | custom-call | tf_op jit(solution)/shard_map/conv_level/pallas_call | solution.py:518
  181.1 8.3 %all-to-all-start.1 = ((bf16[32,592,128]{2,1,0:T(8,128)(2,1)}), bf16[32,592,128]{2,1,0:T(8,128)(2,1)}, u32[]{:S(2)}, u32[]{:S(2)}) async-start(bf16[32,592,128]{2,1,0:T(8,128)(2,1)} %get-tuple-element.52), calls=%async_computation.1 | async-start | bytes 9699328 | tf_op jit(solution)/shard_map/all_to_all | solution.py:692
  189.8 6.5 %copy.21 = bf16[16,256,512]{2,0,1:T(8,128)(2,1)} copy(bf16[16,256,512]{2,1,0:T(8,128)(2,1)} %get-tuple-element.48) | data formatting | bytes 8388608 | tf_op jit(solution)/shard_map/conv_level/pallas_call | solution.py:518
  196.4 1.7 collective-permute-start.5
  198.1 29.5 %collective-permute-done.5 = f32[192,256]{1,0:T(8,128)S(1)} collective-permute-done((f32[192,256]{1,0:T(8,128)S(1)}, f32[192,256]{1,0:T(8,128)S(1)}, u32[]{:S(2)}, u32[]{:S(2)}) %collective-permute-start.5) | collective-permute-done | bytes 196640 | tf_op jit(solution)/shard_map/ppermute | solution.py:638
  227.7 1.5 collective-permute-start.6
  229.2 4.7 %collective-permute-done.6 = f32[96,256]{1,0:T(8,128)S(1)} collective-permute-done((f32[96,256]{1,0:T(8,128)S(1)}, f32[96,256]{1,0:T(8,128)S(1)}, u32[]{:S(2)}, u32[]{:S(2)}) %collective-permute-start.6) | collective-permute-done | bytes 98336 | tf_op jit(solution)/shard_map/ppermute | solution.py:638
  234.6 43.5 %all-reduce.4.cloned.1.call-done = f32[96,256]{1,0:T(8,128)} async-done(((f32[96,256]{1,0:T(8,128)}), f32[96,256]{1,0:T(8,128)}) %all-reduce.4.cloned.1.call-update) | async-done | bytes 98320 | tf_op jit(solution)/shard_map/psum | solution.py:700
  278.9 2.1 collective-permute-start.7
  281.0 2.6 collective-permute-done.7
  284.5 2.7 collective-permute-start.8
  287.3 5.2 %collective-permute-done.8 = f32[192,256]{1,0:T(8,128)S(1)} collective-permute-done((f32[192,256]{1,0:T(8,128)S(1)}, f32[192,256]{1,0:T(8,128)S(1)}, u32[]{:S(2)}, u32[]{:S(2)}) %collective-permute-start.8) | collective-permute-done | bytes 196640 | tf_op jit(solution)/shard_map/ppermute | solution.py:638
  292.6 1.7 collective-permute-done.9
  294.4 0.9 slice_bitcast_fusion
  295.3 6.3 %all-to-all-done.1 = bf16[32,592,128]{2,1,0:T(8,128)(2,1)} async-done(((bf16[32,592,128]{2,1,0:T(8,128)(2,1)}), bf16[32,592,128]{2,1,0:T(8,128)(2,1)}, u32[]{:S(2)}, u32[]{:S(2)}) %all-to-all-start.1) | async-done | bytes 4849696 | tf_op jit(solution)/shard_map/all_to_all | solution.py:692
  301.7 9.4 %block_gradients.1 = bf16[74,64,128]{2,1,0:T(8,128)(2,1)} custom-call(s32[256]{0:T(256)} %get-tuple-element.51.place_ref, bf16[18944,128]{1,0:T(8,128)(2,1)} %bitcast.15.back_hbm, bf16[64,4,128,128]{3,2,1,0:T(8,128)(2,1)} %weight_hbm.3), custom_call_target="tpu_custom_call" | custom-call | tf_op jit(solution)/shard_map/block_gradients/pallas_call | solution.py:607
  (35 shorter events, 7.5 us)
Async XLA Ops:
  19.0 119.3 %all-to-all-start = ((bf16[32,608,128]{2,1,0:T(8,128)(2,1)}), bf16[32,608,128]{2,1,0:T(8,128)(2,1)}, u32[]{:S(2)}, u32[]{:S(2)}) async-start(bf16[32,608,128]{2,1,0:T(8,128)(2,1)} %bitcast.25), calls=%async_computation | async-start | bytes 9961472 | tf_op jit(solution)/shard_map/all_to_all | solution.py:670
  26.4 6.7 %copy-start = (bf16[1,256,16,512]{3,2,1,0:T(8,128)(2,1)S(1)}, bf16[1,256,16,512]{3,2,1,0:T(8,128)(2,1)}, u32[]{:S(2)}) copy-start(bf16[1,256,16,512]{3,2,1,0:T(8,128)(2,1)} %param.13) | copy-start | bytes 12582916
  144.1 3.2 collective-permute-start
  145.7 3.9 %collective-permute-start.1 = (bf16[416,512]{1,0:T(8,128)(2,1)}, bf16[416,512]{1,0:T(8,128)(2,1)S(1)}, u32[]{:S(2)}, u32[]{:S(2)}) collective-permute-start(bf16[416,512]{1,0:T(8,128)(2,1)} %get-tuple-element.36), channel_id=1, source_target_pairs={{1,0},{2,1},{3,2},{4,3},{5,4},{6,5},{7,6},{9,8},{10,9},{11,10},{12... | collective-permute-start | bytes 1277960 | tf_op jit(solution)/shard_map/ppermute | solution.py:634
  147.3 2.3 copy-start.1
  149.6 0.8 copy-start.2
  152.5 5.6 %collective-permute-start.2 = (bf16[336,128]{1,0:T(8,128)(2,1)}, bf16[336,128]{1,0:T(8,128)(2,1)S(1)}, u32[]{:S(2)}, u32[]{:S(2)}) collective-permute-start(bf16[336,128]{1,0:T(8,128)(2,1)} %get-tuple-element.42.own_east), channel_id=1, source_target_pairs={{0,8},{1,9},{2,10},{3,11},{4,12},{5,13},{6,14},{7,15},{8,16},{9,17... | collective-permute-start | bytes 258056 | tf_op jit(solution)/shard_map/ppermute | solution.py:634
  153.8 4.9 %collective-permute-start.3 = (bf16[336,128]{1,0:T(8,128)(2,1)}, bf16[336,128]{1,0:T(8,128)(2,1)S(1)}, u32[]{:S(2)}, u32[]{:S(2)}) collective-permute-start(bf16[336,128]{1,0:T(8,128)(2,1)} %get-tuple-element.41.own_west), channel_id=1, source_target_pairs={{0,24},{1,25},{2,26},{3,27},{4,28},{5,29},{6,30},{7,31},{8,0},{9,1... | collective-permute-start | bytes 258056 | tf_op jit(solution)/shard_map/ppermute | solution.py:634
  158.1 0.7 copy-start.4
  158.7 0.6 copy-start.5
  181.1 8.4 %copy-start.3 = (f32[768,256]{1,0:T(8,128)S(1)}, f32[768,256]{1,0:T(8,128)}, u32[]{:S(2)}) copy-start(f32[768,256]{1,0:T(8,128)} %get-tuple-element.47) | copy-start | bytes 2359300
  181.1 120.6 %all-to-all-start.1 = ((bf16[32,592,128]{2,1,0:T(8,128)(2,1)}), bf16[32,592,128]{2,1,0:T(8,128)(2,1)}, u32[]{:S(2)}, u32[]{:S(2)}) async-start(bf16[32,592,128]{2,1,0:T(8,128)(2,1)} %get-tuple-element.52), calls=%async_computation.1 | async-start | bytes 9699328 | tf_op jit(solution)/shard_map/all_to_all | solution.py:692
  189.4 88.6 %all-reduce.4.cloned.1.call-start = ((), (), s32[]{:S(2)}) async-start(), calls=%async_computation.2 | async-start | bytes 196608 | tf_op jit(solution)/shard_map/psum | solution.py:700
  189.5 6.8 %collective-permute-start.4 = (f32[384,256]{1,0:T(8,128)S(1)}, f32[384,256]{1,0:T(8,128)S(1)}, u32[]{:S(2)}, u32[]{:S(2)}) collective-permute-start(f32[384,256]{1,0:T(8,128)S(1)} %constant_dynamic-slice_fusion.2), channel_id=1, source_target_pairs={{0,1},{1,0},{2,3},{3,2},{4,5},{5,4},{6,7},{7,6},{8,9},{9,8},{10,11... | collective-permute-start | bytes 1179656 | tf_op jit(solution)/shard_map/ppermute | solution.py:638
  196.4 31.2 %collective-permute-start.5 = (f32[192,256]{1,0:T(8,128)S(1)}, f32[192,256]{1,0:T(8,128)S(1)}, u32[]{:S(2)}, u32[]{:S(2)}) collective-permute-start(f32[192,256]{1,0:T(8,128)S(1)} %constant_dynamic-slice_fusion.1), channel_id=1, source_target_pairs={{0,8},{8,0},{16,24},{24,16},{1,9},{9,1},{17,25},{25,17},{2,10},{10... | collective-permute-start | bytes 589832 | tf_op jit(solution)/shard_map/ppermute | solution.py:638
  227.7 6.2 %collective-permute-start.6 = (f32[96,256]{1,0:T(8,128)S(1)}, f32[96,256]{1,0:T(8,128)S(1)}, u32[]{:S(2)}, u32[]{:S(2)}) collective-permute-start(f32[96,256]{1,0:T(8,128)S(1)} %constant_dynamic-slice_fusion), channel_id=1, source_target_pairs={{0,16},{8,24},{16,0},{24,8},{1,17},{9,25},{17,1},{25,9},{2,18},{10... | collective-permute-start | bytes 294920 | tf_op jit(solution)/shard_map/ppermute | solution.py:638
  278.9 4.7 %collective-permute-start.7 = (f32[96,256]{1,0:T(8,128)S(1)}, f32[96,256]{1,0:T(8,128)S(1)}, u32[]{:S(2)}, u32[]{:S(2)}) collective-permute-start(f32[96,256]{1,0:T(8,128)S(1)} %broadcast_multiply_fusion), channel_id=1, source_target_pairs={{0,16},{8,24},{16,0},{24,8},{1,17},{9,25},{17,1},{25,9},{2,18},{10... | collective-permute-start | bytes 294920 | tf_op jit(solution)/shard_map/ppermute | solution.py:638
  284.5 7.9 %collective-permute-start.8 = (f32[192,256]{1,0:T(8,128)S(1)}, f32[192,256]{1,0:T(8,128)S(1)}, u32[]{:S(2)}, u32[]{:S(2)}) collective-permute-start(f32[192,256]{1,0:T(8,128)S(1)} %pad_maximum_fusion.2), channel_id=1, source_target_pairs={{0,8},{8,0},{16,24},{24,16},{1,9},{9,1},{17,25},{25,17},{2,10},{10... | collective-permute-start | bytes 589832 | tf_op jit(solution)/shard_map/ppermute | solution.py:638
  292.5 1.8 collective-permute-start.9
Sparse Core Ops, SparseCore 0:
  234.7 43.2 all-reduce.3

commit v4 on v3

--- a/solution.py
+++ b/solution.py
@@ -180,7 +180,7 @@
     )(weight)
 
 
-def gather_kernel(slots, recv_hbm, first_ref, last_ref, field_ref, low_ref, high_ref, west_ref, east_ref, pick_ref, recv_ref, total, sem):
+def gather_kernel(slots, recv_hbm, field_ref, low_ref, high_ref, west_ref, east_ref, pick_ref, recv_ref, total, sem):
     devices, part = recv_ref.shape[0], recv_ref.shape[1]
     per = TILE // slots
     tiles = part // TILE - 1
@@ -241,19 +241,17 @@
                 east = put_columns(east, r + 2, lane, block[:, PP - 2 : PP - 1], block[:, PP - 1 : PP])
     west_ref[...] = west.astype(BF16)
     east_ref[...] = east.astype(BF16)
-    low_ref[2 * CP :, :] = first_ref[...]
-    high_ref[2 * CP :, :] = last_ref[...]
-
-
-def gather_call(recv, first, last, slots):
+
+
+def gather_call(recv, slots):
     devices = recv.shape[0]
     wide = TILE // slots * PIECES
-    edge = (2 * CP + HID, COLS)
+    edge = (2 * CP, COLS)
     shapes = [(ROWS, CP, COLS), edge, edge, (CP, PP), (CP, PP), (devices * TILE, wide)]
     return pl.pallas_call(
         functools.partial(gather_kernel, slots),
         grid=(1,),
-        in_specs=[anywhere(), whole(first.shape), whole(last.shape)],
+        in_specs=[anywhere()],
         out_specs=[whole(s) for s in shapes],
         out_shape=[jax.ShapeDtypeStruct(s, BF16) for s in shapes],
         scratch_shapes=[
@@ -263,10 +261,10 @@
         ],
         compiler_params=params(),
         name="field_sum",
-    )(recv, first, last)
-
-
-def columns_kernel(west0, east0, cot_west, cot_east, top_ref, bottom_ref, west_ref, east_ref):
+    )(recv)
+
+
+def columns_kernel(west0, east0, cot_west, cot_east, top_ref, bottom_ref, cot_top, cot_bottom, west_ref, east_ref):
     lane = lane_of((CP, PP))
     west = west0[...].astype(F32)
     east = east0[...].astype(F32)
@@ -280,19 +278,19 @@
     lane = lane_of((HID, PP))
     west = cot_west[...].astype(F32)
     east = cot_east[...].astype(F32)
-    for row, ref in ((0, top_ref), (ROWS + 1, bottom_ref)):
-        west = jnp.where(lane == row, ref[2 * CP :, 0:PP].astype(F32)[:, 0:1], west)
-        east = jnp.where(lane == row, ref[2 * CP :, COLS - PP : COLS].astype(F32)[:, PP - 1 : PP], east)
+    for row, ref in ((0, cot_top), (ROWS + 1, cot_bottom)):
+        west = jnp.where(lane == row, ref[:, 0:PP].astype(F32)[:, 0:1], west)
+        east = jnp.where(lane == row, ref[:, COLS - PP : COLS].astype(F32)[:, PP - 1 : PP], east)
     west_ref[CP:, :] = west.astype(BF16)
     east_ref[CP:, :] = east.astype(BF16)
 
 
-def columns_call(west, east, cot_west, cot_east, top, bottom):
+def columns_call(west, east, cot_west, cot_east, top, bottom, cot_top, cot_bottom):
     return pl.pallas_call(
         columns_kernel,
         out_shape=[jax.ShapeDtypeStruct((CP + HID, PP), BF16)] * 2,
         name="edge_columns",
-    )(west, east, cot_west, cot_east, top, bottom)
+    )(west, east, cot_west, cot_east, top, bottom, cot_top, cot_bottom)
 
 
 def gelu_parts(value):
@@ -314,6 +312,8 @@
     far_west,
     far_east,
     cot_hbm,
+    cot_top,
+    cot_bottom,
     forward_ref,
     backward_ref,
     pick_ref,
@@ -418,8 +418,8 @@
             rims[i] = top_ref[i * CP : (i + 1) * CP, :]
             rims[ROWS + 2 + i] = bottom_ref[i * CP : (i + 1) * CP, :]
         rims[2 : ROWS + 2] = field_ref[...]
-        cots[0] = top_ref[2 * CP :, :]
-        cots[ROWS + 1] = bottom_ref[2 * CP :, :]
+        cots[0] = cot_top[...]
+        cots[ROWS + 1] = cot_bottom[...]
         rims[ROWS + 4 : ROWS + 6] = jnp.zeros((2, CP, COLS), BF16)
         for row in range(4):
             stack[row] = build(row)
@@ -511,7 +511,7 @@
             ship(k).wait()
 
 
-def conv_call(slots, part, field, top, bottom, own_west, own_east, far_west, far_east, cot, forward, backward, pick):
+def conv_call(slots, part, field, top, bottom, own_west, own_east, far_west, far_east, cot, cot_top, cot_bottom, forward, backward, pick):
     devices = pick.shape[0] // TILE
     reply_rows = part - TILE
     edges = [whole(x.shape) for x in (field, top, bottom, own_west, own_east, far_west, far_east)]
@@ -520,7 +520,7 @@
         grid=(ROWS // 2 + 2,),
         in_specs=edges
         + [anywhere()]
-        + [whole(x.shape) for x in (forward, backward, pick)],
+        + [whole(x.shape) for x in (cot_top, cot_bottom, forward, backward, pick)],
         out_specs=[anywhere(), whole((GRAD_ROWS, HID)), anywhere()],
         out_shape=[
             jax.ShapeDtypeStruct((ROWS, HID, COLS), BF16),
@@ -542,7 +542,7 @@
         ],
         compiler_params=params(),
         name="conv_level",
-    )(field, top, bottom, own_west, own_east, far_west, far_east, cot, forward, backward, pick)
+    )(field, top, bottom, own_west, own_east, far_west, far_east, cot, cot_top, cot_bottom, forward, backward, pick)
 
 
 def return_kernel(slots, devices, place_ref, back_hbm, weight_hbm, out_ref, back, weights, back_f, out_f, back_sem, in_sem):
@@ -671,21 +671,22 @@
 
     forward, backward = taps_call(jnp.swapaxes(conv_weight, 1, 2))
     cot = jnp.swapaxes(cotangent[0], 0, 1)
-    cot_first, cot_last = cotangent[0, :, 0, :], cotangent[0, :, ROWS - 1, :]
+    cot_top = shift(cotangent[0, :, ROWS - 1, :], 0, 1)
+    cot_bottom = shift(cotangent[0, :, 0, :], 0, -1)
     cot_west = jnp.pad(cotangent[0, :, :, 0], ((0, 0), (1, PP - ROWS - 1)))
     cot_east = jnp.pad(cotangent[0, :, :, COLS - 1], ((0, 0), (1, PP - ROWS - 1)))
-    recv, forward, backward, cot, cot_first, cot_last, cot_west, cot_east = lax.optimization_barrier(
-        (recv, forward, backward, cot, cot_first, cot_last, cot_west, cot_east)
+    recv, forward, backward, cot, cot_west, cot_east = lax.optimization_barrier(
+        (recv, forward, backward, cot, cot_west, cot_east)
     )
 
-    field, low, high, west, east, pick = gather_call(recv, cot_first, cot_last, slots)
+    field, low, high, west, east, pick = gather_call(recv, slots)
     top = shift(high, 0, 1)
     bottom = shift(low, 0, -1)
-    west, east = columns_call(west, east, cot_west, cot_east, top, bottom)
+    west, east = columns_call(west, east, cot_west, cot_east, top, bottom, cot_top, cot_bottom)
     far_west = shift(east, 1, 0)
     far_east = shift(west, -1, 0)
     act, grad, reply = conv_call(
-        slots, part, field, top, bottom, west, east, far_west, far_east, cot, forward, backward, pick
+        slots, part, field, top, bottom, west, east, far_west, far_east, cot, cot_top, cot_bottom, forward, backward, pick
     )
     activation = with_layout_constraint(jnp.swapaxes(act, 0, 1), Layout((0, 1, 2)))
 

time: 318 us -> 314 us (0.987)
    ppermute x4 -> x6, starting transfers between devices: 5.81 us -> 9.19 us  [shift(): return lax.ppermute(value, BOTH, pairs)]
    unnamed x15 -> x21, local copies, waits for them, and re-layouts: 11.3 us -> 11.2 us
  transfers between devices with their start and end apart: 13 -> 15, of which waited for: 12 -> 11; matrix products, arithmetic and copies ran while one was open for 8% -> 6% of each run, Pallas kernels for 1% -> 2%
where the time goes in v4:
time: 314 us
  waiting for transfers between devices  194 us (62%)
  Pallas kernels  51.6 us (16%)
  starting transfers between devices  30.9 us (10%)
  local copies, waits for them, and re-layouts  20.8 us (7%)
  between operations  14.3 us (5%)
    all_to_all x1, waiting for transfers between devices, local(): lax.all_to_all(send.reshape(devices, part, PP), BOTH, split_axis=0, conca...  94.6 us
    ppermute x6, waiting for transfers between devices, swap(): lax.ppermute(value, axis, [(i, i ^ 1 << bit) for i in range(lax.axis_size...  43.7 us
    psum x1, waiting for transfers between devices, local(): grad = lax.psum(grad, 'tile', axis_index_groups=groups)  43.5 us
    pallas_call x1, Pallas kernels, conv_call(): pl.pallas_call(functools.partial(conv_kernel, slots), grid=(ROWS // 2 + 2...  21.7 us
    pallas_call x1, Pallas kernels, send_call(): pl.pallas_call(functools.partial(send_kernel, slots, part), in_specs=[sme...  11.8 us
    unnamed x21, local copies, waits for them, and re-layouts  11.2 us
    pallas_call x1, Pallas kernels, return_call(): pl.pallas_call(functools.partial(return_kernel, slots, devices), grid=(1,...  9.39 us
    ppermute x6, starting transfers between devices, shift(): return lax.ppermute(value, BOTH, pairs)  9.19 us
  transfers between devices with their start and end apart: 15, of which 11 were waited for; matrix products, arithmetic and copies ran while one was open for 6% of the time, Pallas kernels for 2%

profile of v4, /device:TPU:0, one launch (start us, length us, event | category | flops | bytes accessed | tf_op | source)
XLA Modules:
  0.0 313.8 jit_solution(10512512752870357301)
XLA Ops:
  7.2 11.8 %block_products.1 = (bf16[19456,128]{1,0:T(8,128)(2,1)}, s32[256]{0:T(256)}) custom-call(s32[4,64]{1,0:T(4,128)} %bitcast.33, s32[4,64]{1,0:T(4,128)} %bitcast.34, s32[64]{0:T(128)} %counts_ref.1, bf16[74,64,128]{2,1,0:T(8,128)(2,1)} %bitcast.29, bf16[64,4,128,128]{3,2,1,0:T(8,128)(2,1)} %weight_hbm.3), custom_call_target="tpu_custom_call" | custom-call | tf_op jit(solution)/shard_map/block_products/pallas_call | solution.py:128
  19.0 7.4 %all-to-all-start = ((bf16[32,608,128]{2,1,0:T(8,128)(2,1)}), bf16[32,608,128]{2,1,0:T(8,128)(2,1)}, u32[]{:S(2)}, u32[]{:S(2)}) async-start(bf16[32,608,128]{2,1,0:T(8,128)(2,1)} %bitcast.25), calls=%async_computation | async-start | bytes 9961472 | tf_op jit(solution)/shard_map/all_to_all | solution.py:670
  26.4 4.7 %copy.22 = bf16[1,256,16,512]{3,1,2,0:T(8,128)(2,1)S(1)} copy(bf16[1,256,16,512]{3,2,1,0:T(8,128)(2,1)} %param.13) | data formatting | bytes 8388608 | tf_op args[6]
  31.1 2.0 copy-done
  33.1 2.1 collective-permute-start.2
  37.1 1.6 copy.16
  38.7 1.6 copy.17
  41.8 1.9 taps.1
  43.7 94.6 %all-to-all-done.recv_hbm = bf16[32,608,128]{2,1,0:T(8,128)(2,1)} async-done(((bf16[32,608,128]{2,1,0:T(8,128)(2,1)}), bf16[32,608,128]{2,1,0:T(8,128)(2,1)}, u32[]{:S(2)}, u32[]{:S(2)}) %all-to-all-start) | async-done | bytes 4980768 | tf_op jit(solution)/shard_map/all_to_all | solution.py:670
  138.3 4.6 %field_sum.1 = (bf16[16,80,512]{2,1,0:T(8,128)(2,1)}, bf16[160,512]{1,0:T(8,128)(2,1)}, bf16[160,512]{1,0:T(8,128)(2,1)}, bf16[80,128]{1,0:T(8,128)(2,1)}, bf16[...) custom-call(bf16[32,608,128]{2,1,0:T(8,128)(2,1)} %all-to-all-done.recv_hbm), custom_call_target="tpu_custom_call" | custom-call | tf_op jit(solution)/shard_map/field_sum/pallas_call | solution.py:251
  142.9 1.6 collective-permute-start
  144.4 1.3 collective-permute-start.1
  145.8 2.1 collective-permute-done.1.bottom_ref
  148.6 2.2 edge_columns.1
  150.8 1.3 collective-permute-start.4
  152.1 1.6 collective-permute-start.5
  153.7 2.7 collective-permute-done.4.far_west
  157.7 21.7 %conv_level.1 = (bf16[16,256,512]{2,1,0:T(8,128)(2,1)}, f32[768,256]{1,0:T(8,128)}, bf16[32,592,128]{2,1,0:T(8,128)(2,1)}) custom-call(bf16[16,80,512]{2,1,0:T(8,128)(2,1)} %get-tuple-element.30.field_ref, bf16[160,512]{1,0:T(8,128)(2,1)} %copy-done.5, bf16[160,512]{1,0:T(8,128)(2,1)} %copy-done.6, bf16[336,128]{1,0:T(8,128)(2,1)} %get-tuple-element.37.own_west, ...), custom_call_target="tpu_custom_call" | custom-call | tf_op jit(solution)/shard_map/conv_level/pallas_call | solution.py:518
  179.4 5.9 %all-to-all-start.1 = ((bf16[32,592,128]{2,1,0:T(8,128)(2,1)}), bf16[32,592,128]{2,1,0:T(8,128)(2,1)}, u32[]{:S(2)}, u32[]{:S(2)}) async-start(bf16[32,592,128]{2,1,0:T(8,128)(2,1)} %get-tuple-element.48), calls=%async_computation.1 | async-start | bytes 9699328 | tf_op jit(solution)/shard_map/all_to_all | solution.py:693
  185.7 6.5 %copy.21 = bf16[16,256,512]{2,0,1:T(8,128)(2,1)} copy(bf16[16,256,512]{2,1,0:T(8,128)(2,1)} %get-tuple-element.44) | data formatting | bytes 8388608 | tf_op jit(solution)/shard_map/conv_level/pallas_call | solution.py:518
  192.3 1.7 collective-permute-start.7
  194.0 29.5 %collective-permute-done.7 = f32[192,256]{1,0:T(8,128)S(1)} collective-permute-done((f32[192,256]{1,0:T(8,128)S(1)}, f32[192,256]{1,0:T(8,128)S(1)}, u32[]{:S(2)}, u32[]{:S(2)}) %collective-permute-start.7) | collective-permute-done | bytes 196640 | tf_op jit(solution)/shard_map/ppermute | solution.py:638
  223.6 1.5 collective-permute-start.8
  225.1 4.7 %collective-permute-done.8 = f32[96,256]{1,0:T(8,128)S(1)} collective-permute-done((f32[96,256]{1,0:T(8,128)S(1)}, f32[96,256]{1,0:T(8,128)S(1)}, u32[]{:S(2)}, u32[]{:S(2)}) %collective-permute-start.8) | collective-permute-done | bytes 98336 | tf_op jit(solution)/shard_map/ppermute | solution.py:638
  230.5 43.5 %all-reduce.4.cloned.1.call-done = f32[96,256]{1,0:T(8,128)} async-done(((f32[96,256]{1,0:T(8,128)}), f32[96,256]{1,0:T(8,128)}) %all-reduce.4.cloned.1.call-update) | async-done | bytes 98320 | tf_op jit(solution)/shard_map/psum | solution.py:701
  274.8 2.1 collective-permute-start.9
  276.9 2.6 collective-permute-done.9
  280.5 2.7 collective-permute-start.10
  283.2 5.2 %collective-permute-done.10 = f32[192,256]{1,0:T(8,128)S(1)} collective-permute-done((f32[192,256]{1,0:T(8,128)S(1)}, f32[192,256]{1,0:T(8,128)S(1)}, u32[]{:S(2)}, u32[]{:S(2)}) %collective-permute-start.10) | collective-permute-done | bytes 196640 | tf_op jit(solution)/shard_map/ppermute | solution.py:638
  288.5 1.7 collective-permute-done.11
  291.2 6.3 %all-to-all-done.1 = bf16[32,592,128]{2,1,0:T(8,128)(2,1)} async-done(((bf16[32,592,128]{2,1,0:T(8,128)(2,1)}), bf16[32,592,128]{2,1,0:T(8,128)(2,1)}, u32[]{:S(2)}, u32[]{:S(2)}) %all-to-all-start.1) | async-done | bytes 4849696 | tf_op jit(solution)/shard_map/all_to_all | solution.py:693
  297.6 9.4 %block_gradients.1 = bf16[74,64,128]{2,1,0:T(8,128)(2,1)} custom-call(s32[256]{0:T(256)} %get-tuple-element.47.place_ref, bf16[18944,128]{1,0:T(8,128)(2,1)} %bitcast.15.back_hbm, bf16[64,4,128,128]{3,2,1,0:T(8,128)(2,1)} %weight_hbm.3), custom_call_target="tpu_custom_call" | custom-call | tf_op jit(solution)/shard_map/block_gradients/pallas_call | solution.py:607
  (45 shorter events, 9.4 us)
Async XLA Ops:
  19.0 119.3 %all-to-all-start = ((bf16[32,608,128]{2,1,0:T(8,128)(2,1)}), bf16[32,608,128]{2,1,0:T(8,128)(2,1)}, u32[]{:S(2)}, u32[]{:S(2)}) async-start(bf16[32,608,128]{2,1,0:T(8,128)(2,1)} %bitcast.25), calls=%async_computation | async-start | bytes 9961472 | tf_op jit(solution)/shard_map/all_to_all | solution.py:670
  26.4 10.2 %copy-start.1 = (bf16[1,256,16,512]{3,2,1,0:T(8,128)(2,1)S(1)}, bf16[1,256,16,512]{3,2,1,0:T(8,128)(2,1)}, u32[]{:S(2)}) copy-start(bf16[1,256,16,512]{3,2,1,0:T(8,128)(2,1)} %param.13) | copy-start | bytes 12582916
  31.1 2.0 copy-start
  33.1 112.6 %collective-permute-start.2 = (bf16[256,512]{1,0:T(8,128)(2,1)S(1)}, bf16[256,512]{1,0:T(8,128)(2,1)S(1)}, u32[]{:S(2)}, u32[]{:S(2)}) collective-permute-start(bf16[256,512]{1,0:T(8,128)(2,1)S(1)} %get-tuple-element.50), channel_id=1, source_target_pairs={{0,1},{1,2},{2,3},{3,4},{4,5},{5,6},{6,7},{8,9},{9,10},{10,11},{11... | collective-permute-start | bytes 786440 | tf_op jit(solution)/shard_map/ppermute | solution.py:634
  35.2 110.5 %collective-permute-start.3 = (bf16[256,512]{1,0:T(8,128)(2,1)S(1)}, bf16[256,512]{1,0:T(8,128)(2,1)S(1)}, u32[]{:S(2)}, u32[]{:S(2)}) collective-permute-start(bf16[256,512]{1,0:T(8,128)(2,1)S(1)} %get-tuple-element.49), channel_id=1, source_target_pairs={{1,0},{2,1},{3,2},{4,3},{5,4},{6,5},{7,6},{9,8},{10,9},{11,10},{12... | collective-permute-start | bytes 786440 | tf_op jit(solution)/shard_map/ppermute | solution.py:634
  142.9 2.9 collective-permute-start
  144.4 3.5 %collective-permute-start.1 = (bf16[160,512]{1,0:T(8,128)(2,1)}, bf16[160,512]{1,0:T(8,128)(2,1)S(1)}, u32[]{:S(2)}, u32[]{:S(2)}) collective-permute-start(bf16[160,512]{1,0:T(8,128)(2,1)} %get-tuple-element.32), channel_id=1, source_target_pairs={{1,0},{2,1},{3,2},{4,3},{5,4},{6,5},{7,6},{9,8},{10,9},{11,10},{12... | collective-permute-start | bytes 491528 | tf_op jit(solution)/shard_map/ppermute | solution.py:634
  145.7 2.2 copy-start.2
  145.8 2.2 copy-start.3
  145.8 2.2 copy-start.5
  147.9 0.7 copy-start.6
  150.8 5.6 %collective-permute-start.4 = (bf16[336,128]{1,0:T(8,128)(2,1)}, bf16[336,128]{1,0:T(8,128)(2,1)S(1)}, u32[]{:S(2)}, u32[]{:S(2)}) collective-permute-start(bf16[336,128]{1,0:T(8,128)(2,1)} %get-tuple-element.38.own_east), channel_id=1, source_target_pairs={{0,8},{1,9},{2,10},{3,11},{4,12},{5,13},{6,14},{7,15},{8,16},{9,17... | collective-permute-start | bytes 258056 | tf_op jit(solution)/shard_map/ppermute | solution.py:634
  152.1 4.9 %collective-permute-start.5 = (bf16[336,128]{1,0:T(8,128)(2,1)}, bf16[336,128]{1,0:T(8,128)(2,1)S(1)}, u32[]{:S(2)}, u32[]{:S(2)}) collective-permute-start(bf16[336,128]{1,0:T(8,128)(2,1)} %get-tuple-element.37.own_west), channel_id=1, source_target_pairs={{0,24},{1,25},{2,26},{3,27},{4,28},{5,29},{6,30},{7,31},{8,0},{9,1... | collective-permute-start | bytes 258056 | tf_op jit(solution)/shard_map/ppermute | solution.py:634
  156.4 0.7 copy-start.7
  157.0 0.6 copy-start.8
  179.4 6.0 %copy-start.4 = (f32[768,256]{1,0:T(8,128)S(1)}, f32[768,256]{1,0:T(8,128)}, u32[]{:S(2)}) copy-start(f32[768,256]{1,0:T(8,128)} %get-tuple-element.43) | copy-start | bytes 2359300
  179.4 118.1 %all-to-all-start.1 = ((bf16[32,592,128]{2,1,0:T(8,128)(2,1)}), bf16[32,592,128]{2,1,0:T(8,128)(2,1)}, u32[]{:S(2)}, u32[]{:S(2)}) async-start(bf16[32,592,128]{2,1,0:T(8,128)(2,1)} %get-tuple-element.48), calls=%async_computation.1 | async-start | bytes 9699328 | tf_op jit(solution)/shard_map/all_to_all | solution.py:693
  185.3 88.6 %all-reduce.4.cloned.1.call-start = ((), (), s32[]{:S(2)}) async-start(), calls=%async_computation.2 | async-start | bytes 196608 | tf_op jit(solution)/shard_map/psum | solution.py:701
  185.4 6.8 %collective-permute-start.6 = (f32[384,256]{1,0:T(8,128)S(1)}, f32[384,256]{1,0:T(8,128)S(1)}, u32[]{:S(2)}, u32[]{:S(2)}) collective-permute-start(f32[384,256]{1,0:T(8,128)S(1)} %constant_dynamic-slice_fusion.2), channel_id=1, source_target_pairs={{0,1},{1,0},{2,3},{3,2},{4,5},{5,4},{6,7},{7,6},{8,9},{9,8},{10,11... | collective-permute-start | bytes 1179656 | tf_op jit(solution)/shard_map/ppermute | solution.py:638
  192.3 31.2 %collective-permute-start.7 = (f32[192,256]{1,0:T(8,128)S(1)}, f32[192,256]{1,0:T(8,128)S(1)}, u32[]{:S(2)}, u32[]{:S(2)}) collective-permute-start(f32[192,256]{1,0:T(8,128)S(1)} %constant_dynamic-slice_fusion.1), channel_id=1, source_target_pairs={{0,8},{8,0},{16,24},{24,16},{1,9},{9,1},{17,25},{25,17},{2,10},{10... | collective-permute-start | bytes 589832 | tf_op jit(solution)/shard_map/ppermute | solution.py:638
  223.6 6.2 %collective-permute-start.8 = (f32[96,256]{1,0:T(8,128)S(1)}, f32[96,256]{1,0:T(8,128)S(1)}, u32[]{:S(2)}, u32[]{:S(2)}) collective-permute-start(f32[96,256]{1,0:T(8,128)S(1)} %constant_dynamic-slice_fusion), channel_id=1, source_target_pairs={{0,16},{8,24},{16,0},{24,8},{1,17},{9,25},{17,1},{25,9},{2,18},{10... | collective-permute-start | bytes 294920 | tf_op jit(solution)/shard_map/ppermute | solution.py:638
  274.8 4.7 %collective-permute-start.9 = (f32[96,256]{1,0:T(8,128)S(1)}, f32[96,256]{1,0:T(8,128)S(1)}, u32[]{:S(2)}, u32[]{:S(2)}) collective-permute-start(f32[96,256]{1,0:T(8,128)S(1)} %broadcast_multiply_fusion), channel_id=1, source_target_pairs={{0,16},{8,24},{16,0},{24,8},{1,17},{9,25},{17,1},{25,9},{2,18},{10... | collective-permute-start | bytes 294920 | tf_op jit(solution)/shard_map/ppermute | solution.py:638
  280.5 7.9 %collective-permute-start.10 = (f32[192,256]{1,0:T(8,128)S(1)}, f32[192,256]{1,0:T(8,128)S(1)}, u32[]{:S(2)}, u32[]{:S(2)}) collective-permute-start(f32[192,256]{1,0:T(8,128)S(1)} %pad_maximum_fusion.2), channel_id=1, source_target_pairs={{0,8},{8,0},{16,24},{24,16},{1,9},{9,1},{17,25},{25,17},{2,10},{10... | collective-permute-start | bytes 589832 | tf_op jit(solution)/shard_map/ppermute | solution.py:638
  288.4 1.8 collective-permute-start.11
Sparse Core Ops, SparseCore 0:
  230.6 43.2 all-reduce.3

commit v5 on v4

--- a/solution.py
+++ b/solution.py
@@ -141,7 +141,7 @@
             pltpu.VMEM((devices * part, PP), BF16),
             pltpu.SMEM((devices,), jnp.int32),
             pltpu.SemaphoreType.DMA,
-            pltpu.SemaphoreType.DMA((4,)),
+            pltpu.SemaphoreType.DMA((2,)),
             pltpu.SemaphoreType.DMA((8,)),
         ],
         compiler_params=params(),
@@ -264,33 +264,45 @@
     )(recv)
 
 
-def columns_kernel(west0, east0, cot_west, cot_east, top_ref, bottom_ref, cot_top, cot_bottom, west_ref, east_ref):
+def columns_kernel(west0, east0, cot_west, cot_east, *refs):
+    top_left, top_right, bottom_left, bottom_right = refs[0:4]
+    cot_top_left, cot_top_right, cot_bottom_left, cot_bottom_right = refs[4:8]
+    west_ref, east_ref = refs[8:]
     lane = lane_of((CP, PP))
     west = west0[...].astype(F32)
     east = east0[...].astype(F32)
-    for row, ref, i in ((0, top_ref, 0), (1, top_ref, 1), (ROWS + 2, bottom_ref, 0), (ROWS + 3, bottom_ref, 1)):
-        left = ref[i * CP : (i + 1) * CP, 0:PP].astype(F32)
-        right = ref[i * CP : (i + 1) * CP, COLS - PP : COLS].astype(F32)
-        west = put_columns(west, row, lane, left[:, 0:1], left[:, 1:2])
-        east = put_columns(east, row, lane, right[:, PP - 2 : PP - 1], right[:, PP - 1 : PP])
+    for first, left_ref, right_ref in ((0, top_left, top_right), (ROWS + 2, bottom_left, bottom_right)):
+        for i in range(2):
+            left = left_ref[i * CP : (i + 1) * CP, :].astype(F32)
+            right = right_ref[i * CP : (i + 1) * CP, :].astype(F32)
+            west = put_columns(west, first + i, lane, left[:, 0:1], left[:, 1:2])
+            east = put_columns(east, first + i, lane, right[:, PP - 2 : PP - 1], right[:, PP - 1 : PP])
     west_ref[0:CP, :] = west.astype(BF16)
     east_ref[0:CP, :] = east.astype(BF16)
     lane = lane_of((HID, PP))
     west = cot_west[...].astype(F32)
     east = cot_east[...].astype(F32)
-    for row, ref in ((0, cot_top), (ROWS + 1, cot_bottom)):
-        west = jnp.where(lane == row, ref[:, 0:PP].astype(F32)[:, 0:1], west)
-        east = jnp.where(lane == row, ref[:, COLS - PP : COLS].astype(F32)[:, PP - 1 : PP], east)
+    for row, left_ref, right_ref in (
+        (0, cot_top_left, cot_top_right),
+        (ROWS + 1, cot_bottom_left, cot_bottom_right),
+    ):
+        west = jnp.where(lane == row, left_ref[...].astype(F32)[:, 0:1], west)
+        east = jnp.where(lane == row, right_ref[...].astype(F32)[:, PP - 1 : PP], east)
     west_ref[CP:, :] = west.astype(BF16)
     east_ref[CP:, :] = east.astype(BF16)
 
 
-def columns_call(west, east, cot_west, cot_east, top, bottom, cot_top, cot_bottom):
+def columns_call(west, east, cot_west, cot_east, *edges):
+    ends = [pl.BlockSpec((x.shape[0], PP), lambda _, at=at: (0, at)) for x in edges for at in (0, COLS // PP - 1)]
+    shape = (CP + HID, PP)
     return pl.pallas_call(
         columns_kernel,
-        out_shape=[jax.ShapeDtypeStruct((CP + HID, PP), BF16)] * 2,
+        grid=(1,),
+        in_specs=[whole(x.shape) for x in (west, east, cot_west, cot_east)] + ends,
+        out_specs=[whole(shape)] * 2,
+        out_shape=[jax.ShapeDtypeStruct(shape, BF16)] * 2,
         name="edge_columns",
-    )(west, east, cot_west, cot_east, top, bottom, cot_top, cot_bottom)
+    )(west, east, cot_west, cot_east, *[x for x in edges for _ in range(2)])
 
 
 def gelu_parts(value):

time: 314 us -> 313 us (level)
  no operation moved by 1% of the time
where the time goes in v5:
time: 313 us
  waiting for transfers between devices  194 us (62%)
  Pallas kernels  50.7 us (16%)
  starting transfers between devices  30.9 us (10%)
  local copies, waits for them, and re-layouts  20.8 us (7%)
  between operations  14.3 us (5%)
    all_to_all x1, waiting for transfers between devices, local(): lax.all_to_all(send.reshape(devices, part, PP), BOTH, split_axis=0, conca...  94.6 us
    ppermute x6, waiting for transfers between devices, swap(): lax.ppermute(value, axis, [(i, i ^ 1 << bit) for i in range(lax.axis_size...  43.7 us
    psum x1, waiting for transfers between devices, local(): grad = lax.psum(grad, 'tile', axis_index_groups=groups)  43.5 us
    pallas_call x1, Pallas kernels, conv_call(): pl.pallas_call(functools.partial(conv_kernel, slots), grid=(ROWS // 2 + 2...  21.8 us
    unnamed x21, local copies, waits for them, and re-layouts  11.2 us
    pallas_call x1, Pallas kernels, send_call(): pl.pallas_call(functools.partial(send_kernel, slots, part), in_specs=[sme...  11 us
    pallas_call x1, Pallas kernels, return_call(): pl.pallas_call(functools.partial(return_kernel, slots, devices), grid=(1,...  9.4 us
    ppermute x6, starting transfers between devices, shift(): return lax.ppermute(value, BOTH, pairs)  9.19 us
  transfers between devices with their start and end apart: 15, of which 11 were waited for; matrix products, arithmetic and copies ran while one was open for 6% of the time, Pallas kernels for 2%

profile of v5, /device:TPU:0, one launch (start us, length us, event | category | flops | bytes accessed | tf_op | source)
XLA Modules:
  0.0 312.9 jit_solution(419741691175736997)
XLA Ops:
  7.2 11.0 %block_products.1 = (bf16[19456,128]{1,0:T(8,128)(2,1)}, s32[256]{0:T(256)}) custom-call(s32[4,64]{1,0:T(4,128)} %bitcast.33, s32[4,64]{1,0:T(4,128)} %bitcast.34, s32[64]{0:T(128)} %counts_ref.1, bf16[74,64,128]{2,1,0:T(8,128)(2,1)} %bitcast.29, bf16[64,4,128,128]{3,2,1,0:T(8,128)(2,1)} %weight_hbm.3), custom_call_target="tpu_custom_call" | custom-call | tf_op jit(solution)/shard_map/block_products/pallas_call | solution.py:128
  18.1 7.4 %all-to-all-start = ((bf16[32,608,128]{2,1,0:T(8,128)(2,1)}), bf16[32,608,128]{2,1,0:T(8,128)(2,1)}, u32[]{:S(2)}, u32[]{:S(2)}) async-start(bf16[32,608,128]{2,1,0:T(8,128)(2,1)} %bitcast.25), calls=%async_computation | async-start | bytes 9961472 | tf_op jit(solution)/shard_map/all_to_all | solution.py:682
  25.5 4.7 %copy.22 = bf16[1,256,16,512]{3,1,2,0:T(8,128)(2,1)S(1)} copy(bf16[1,256,16,512]{3,2,1,0:T(8,128)(2,1)} %param.13) | data formatting | bytes 8388608 | tf_op args[6]
  30.2 2.0 copy-done
  32.3 2.1 collective-permute-start.2
  34.4 1.3 collective-permute-start.3
  36.3 1.6 copy.16
  37.9 1.6 copy.17
  40.9 1.9 taps.1
  42.8 94.6 %all-to-all-done.recv_hbm = bf16[32,608,128]{2,1,0:T(8,128)(2,1)} async-done(((bf16[32,608,128]{2,1,0:T(8,128)(2,1)}), bf16[32,608,128]{2,1,0:T(8,128)(2,1)}, u32[]{:S(2)}, u32[]{:S(2)}) %all-to-all-start) | async-done | bytes 4980768 | tf_op jit(solution)/shard_map/all_to_all | solution.py:682
  137.4 4.6 %field_sum.1 = (bf16[16,80,512]{2,1,0:T(8,128)(2,1)}, bf16[160,512]{1,0:T(8,128)(2,1)}, bf16[160,512]{1,0:T(8,128)(2,1)}, bf16[80,128]{1,0:T(8,128)(2,1)}, bf16[...) custom-call(bf16[32,608,128]{2,1,0:T(8,128)(2,1)} %all-to-all-done.recv_hbm), custom_call_target="tpu_custom_call" | custom-call | tf_op jit(solution)/shard_map/field_sum/pallas_call | solution.py:251
  142.0 1.6 collective-permute-start
  145.0 2.1 collective-permute-done.1.refs_2_.refs_3_.bottom_ref
  147.8 2.0 edge_columns.1
  149.8 1.3 collective-permute-start.4
  151.1 1.6 collective-permute-start.5
  152.7 2.7 collective-permute-done.4.far_west
  156.7 21.8 %conv_level.1 = (bf16[16,256,512]{2,1,0:T(8,128)(2,1)}, f32[768,256]{1,0:T(8,128)}, bf16[32,592,128]{2,1,0:T(8,128)(2,1)}) custom-call(bf16[16,80,512]{2,1,0:T(8,128)(2,1)} %get-tuple-element.30.field_ref, bf16[160,512]{1,0:T(8,128)(2,1)} %copy-done.4, bf16[160,512]{1,0:T(8,128)(2,1)} %copy-done.5, bf16[336,128]{1,0:T(8,128)(2,1)} %get-tuple-element.37.own_west, ...), custom_call_target="tpu_custom_call" | custom-call | tf_op jit(solution)/shard_map/conv_level/pallas_call | solution.py:530
  178.5 5.9 %all-to-all-start.1 = ((bf16[32,592,128]{2,1,0:T(8,128)(2,1)}), bf16[32,592,128]{2,1,0:T(8,128)(2,1)}, u32[]{:S(2)}, u32[]{:S(2)}) async-start(bf16[32,592,128]{2,1,0:T(8,128)(2,1)} %get-tuple-element.48), calls=%async_computation.1 | async-start | bytes 9699328 | tf_op jit(solution)/shard_map/all_to_all | solution.py:705
  184.7 6.5 %copy.21 = bf16[16,256,512]{2,0,1:T(8,128)(2,1)} copy(bf16[16,256,512]{2,1,0:T(8,128)(2,1)} %get-tuple-element.44) | data formatting | bytes 8388608 | tf_op jit(solution)/shard_map/conv_level/pallas_call | solution.py:530
  191.3 1.7 collective-permute-start.7
  193.1 29.5 %collective-permute-done.7 = f32[192,256]{1,0:T(8,128)S(1)} collective-permute-done((f32[192,256]{1,0:T(8,128)S(1)}, f32[192,256]{1,0:T(8,128)S(1)}, u32[]{:S(2)}, u32[]{:S(2)}) %collective-permute-start.7) | collective-permute-done | bytes 196640 | tf_op jit(solution)/shard_map/ppermute | solution.py:650
  222.6 1.5 collective-permute-start.8
  224.1 4.7 %collective-permute-done.8 = f32[96,256]{1,0:T(8,128)S(1)} collective-permute-done((f32[96,256]{1,0:T(8,128)S(1)}, f32[96,256]{1,0:T(8,128)S(1)}, u32[]{:S(2)}, u32[]{:S(2)}) %collective-permute-start.8) | collective-permute-done | bytes 98336 | tf_op jit(solution)/shard_map/ppermute | solution.py:650
  229.5 43.5 %all-reduce.4.cloned.1.call-done = f32[96,256]{1,0:T(8,128)} async-done(((f32[96,256]{1,0:T(8,128)}), f32[96,256]{1,0:T(8,128)}) %all-reduce.4.cloned.1.call-update) | async-done | bytes 98320 | tf_op jit(solution)/shard_map/psum | solution.py:713
  273.9 2.1 collective-permute-start.9
  276.0 2.6 collective-permute-done.9
  279.5 2.7 collective-permute-start.10
  282.2 5.2 %collective-permute-done.10 = f32[192,256]{1,0:T(8,128)S(1)} collective-permute-done((f32[192,256]{1,0:T(8,128)S(1)}, f32[192,256]{1,0:T(8,128)S(1)}, u32[]{:S(2)}, u32[]{:S(2)}) %collective-permute-start.10) | collective-permute-done | bytes 196640 | tf_op jit(solution)/shard_map/ppermute | solution.py:650
  287.5 1.7 collective-permute-done.11
  290.3 6.3 %all-to-all-done.1 = bf16[32,592,128]{2,1,0:T(8,128)(2,1)} async-done(((bf16[32,592,128]{2,1,0:T(8,128)(2,1)}), bf16[32,592,128]{2,1,0:T(8,128)(2,1)}, u32[]{:S(2)}, u32[]{:S(2)}) %all-to-all-start.1) | async-done | bytes 4849696 | tf_op jit(solution)/shard_map/all_to_all | solution.py:705
  296.6 9.4 %block_gradients.1 = bf16[74,64,128]{2,1,0:T(8,128)(2,1)} custom-call(s32[256]{0:T(256)} %get-tuple-element.47.place_ref, bf16[18944,128]{1,0:T(8,128)(2,1)} %bitcast.15.back_hbm, bf16[64,4,128,128]{3,2,1,0:T(8,128)(2,1)} %weight_hbm.3), custom_call_target="tpu_custom_call" | custom-call | tf_op jit(solution)/shard_map/block_gradients/pallas_call | solution.py:619
  (45 shorter events, 9.4 us)
Async XLA Ops:
  18.1 119.3 %all-to-all-start = ((bf16[32,608,128]{2,1,0:T(8,128)(2,1)}), bf16[32,608,128]{2,1,0:T(8,128)(2,1)}, u32[]{:S(2)}, u32[]{:S(2)}) async-start(bf16[32,608,128]{2,1,0:T(8,128)(2,1)} %bitcast.25), calls=%async_computation | async-start | bytes 9961472 | tf_op jit(solution)/shard_map/all_to_all | solution.py:682
  25.5 10.2 %copy-start.1 = (bf16[1,256,16,512]{3,2,1,0:T(8,128)(2,1)S(1)}, bf16[1,256,16,512]{3,2,1,0:T(8,128)(2,1)}, u32[]{:S(2)}) copy-start(bf16[1,256,16,512]{3,2,1,0:T(8,128)(2,1)} %param.13) | copy-start | bytes 12582916
  30.2 2.0 copy-start
  32.3 112.6 %collective-permute-start.2 = (bf16[256,512]{1,0:T(8,128)(2,1)S(1)}, bf16[256,512]{1,0:T(8,128)(2,1)S(1)}, u32[]{:S(2)}, u32[]{:S(2)}) collective-permute-start(bf16[256,512]{1,0:T(8,128)(2,1)S(1)} %get-tuple-element.50), channel_id=1, source_target_pairs={{0,1},{1,2},{2,3},{3,4},{4,5},{5,6},{6,7},{8,9},{9,10},{10,11},{11... | collective-permute-start | bytes 786440 | tf_op jit(solution)/shard_map/ppermute | solution.py:646
  34.4 110.5 %collective-permute-start.3 = (bf16[256,512]{1,0:T(8,128)(2,1)S(1)}, bf16[256,512]{1,0:T(8,128)(2,1)S(1)}, u32[]{:S(2)}, u32[]{:S(2)}) collective-permute-start(bf16[256,512]{1,0:T(8,128)(2,1)S(1)} %get-tuple-element.49), channel_id=1, source_target_pairs={{1,0},{2,1},{3,2},{4,3},{5,4},{6,5},{7,6},{9,8},{10,9},{11,10},{12... | collective-permute-start | bytes 786440 | tf_op jit(solution)/shard_map/ppermute | solution.py:646
  142.0 2.9 collective-permute-start
  143.6 3.5 %collective-permute-start.1 = (bf16[160,512]{1,0:T(8,128)(2,1)}, bf16[160,512]{1,0:T(8,128)(2,1)S(1)}, u32[]{:S(2)}, u32[]{:S(2)}) collective-permute-start(bf16[160,512]{1,0:T(8,128)(2,1)} %get-tuple-element.32), channel_id=1, source_target_pairs={{1,0},{2,1},{3,2},{4,3},{5,4},{6,5},{7,6},{9,8},{10,9},{11,10},{12... | collective-permute-start | bytes 491528 | tf_op jit(solution)/shard_map/ppermute | solution.py:646
  144.9 2.2 copy-start.2
  144.9 2.2 copy-start.3
  144.9 2.2 copy-start.4
  147.1 0.7 copy-start.5
  149.8 5.6 %collective-permute-start.4 = (bf16[336,128]{1,0:T(8,128)(2,1)}, bf16[336,128]{1,0:T(8,128)(2,1)S(1)}, u32[]{:S(2)}, u32[]{:S(2)}) collective-permute-start(bf16[336,128]{1,0:T(8,128)(2,1)} %get-tuple-element.38.own_east), channel_id=1, source_target_pairs={{0,8},{1,9},{2,10},{3,11},{4,12},{5,13},{6,14},{7,15},{8,16},{9,17... | collective-permute-start | bytes 258056 | tf_op jit(solution)/shard_map/ppermute | solution.py:646
  151.1 4.9 %collective-permute-start.5 = (bf16[336,128]{1,0:T(8,128)(2,1)}, bf16[336,128]{1,0:T(8,128)(2,1)S(1)}, u32[]{:S(2)}, u32[]{:S(2)}) collective-permute-start(bf16[336,128]{1,0:T(8,128)(2,1)} %get-tuple-element.37.own_west), channel_id=1, source_target_pairs={{0,24},{1,25},{2,26},{3,27},{4,28},{5,29},{6,30},{7,31},{8,0},{9,1... | collective-permute-start | bytes 258056 | tf_op jit(solution)/shard_map/ppermute | solution.py:646
  155.4 0.7 copy-start.7
  156.0 0.6 copy-start.8
  178.5 5.9 %copy-start.6 = (f32[768,256]{1,0:T(8,128)S(1)}, f32[768,256]{1,0:T(8,128)}, u32[]{:S(2)}) copy-start(f32[768,256]{1,0:T(8,128)} %get-tuple-element.43) | copy-start | bytes 2359300
  178.5 118.1 %all-to-all-start.1 = ((bf16[32,592,128]{2,1,0:T(8,128)(2,1)}), bf16[32,592,128]{2,1,0:T(8,128)(2,1)}, u32[]{:S(2)}, u32[]{:S(2)}) async-start(bf16[32,592,128]{2,1,0:T(8,128)(2,1)} %get-tuple-element.48), calls=%async_computation.1 | async-start | bytes 9699328 | tf_op jit(solution)/shard_map/all_to_all | solution.py:705
  184.3 88.6 %all-reduce.4.cloned.1.call-start = ((), (), s32[]{:S(2)}) async-start(), calls=%async_computation.2 | async-start | bytes 196608 | tf_op jit(solution)/shard_map/psum | solution.py:713
  184.5 6.8 %collective-permute-start.6 = (f32[384,256]{1,0:T(8,128)S(1)}, f32[384,256]{1,0:T(8,128)S(1)}, u32[]{:S(2)}, u32[]{:S(2)}) collective-permute-start(f32[384,256]{1,0:T(8,128)S(1)} %constant_dynamic-slice_fusion.2), channel_id=1, source_target_pairs={{0,1},{1,0},{2,3},{3,2},{4,5},{5,4},{6,7},{7,6},{8,9},{9,8},{10,11... | collective-permute-start | bytes 1179656 | tf_op jit(solution)/shard_map/ppermute | solution.py:650
  191.3 31.2 %collective-permute-start.7 = (f32[192,256]{1,0:T(8,128)S(1)}, f32[192,256]{1,0:T(8,128)S(1)}, u32[]{:S(2)}, u32[]{:S(2)}) collective-permute-start(f32[192,256]{1,0:T(8,128)S(1)} %constant_dynamic-slice_fusion.1), channel_id=1, source_target_pairs={{0,8},{8,0},{16,24},{24,16},{1,9},{9,1},{17,25},{25,17},{2,10},{10... | collective-permute-start | bytes 589832 | tf_op jit(solution)/shard_map/ppermute | solution.py:650
  222.6 6.2 %collective-permute-start.8 = (f32[96,256]{1,0:T(8,128)S(1)}, f32[96,256]{1,0:T(8,128)S(1)}, u32[]{:S(2)}, u32[]{:S(2)}) collective-permute-start(f32[96,256]{1,0:T(8,128)S(1)} %constant_dynamic-slice_fusion), channel_id=1, source_target_pairs={{0,16},{8,24},{16,0},{24,8},{1,17},{9,25},{17,1},{25,9},{2,18},{10... | collective-permute-start | bytes 294920 | tf_op jit(solution)/shard_map/ppermute | solution.py:650
  273.9 4.7 %collective-permute-start.9 = (f32[96,256]{1,0:T(8,128)S(1)}, f32[96,256]{1,0:T(8,128)S(1)}, u32[]{:S(2)}, u32[]{:S(2)}) collective-permute-start(f32[96,256]{1,0:T(8,128)S(1)} %broadcast_multiply_fusion), channel_id=1, source_target_pairs={{0,16},{8,24},{16,0},{24,8},{1,17},{9,25},{17,1},{25,9},{2,18},{10... | collective-permute-start | bytes 294920 | tf_op jit(solution)/shard_map/ppermute | solution.py:650
  279.5 7.9 %collective-permute-start.10 = (f32[192,256]{1,0:T(8,128)S(1)}, f32[192,256]{1,0:T(8,128)S(1)}, u32[]{:S(2)}, u32[]{:S(2)}) collective-permute-start(f32[192,256]{1,0:T(8,128)S(1)} %pad_maximum_fusion.2), channel_id=1, source_target_pairs={{0,8},{8,0},{16,24},{24,16},{1,9},{9,1},{17,25},{25,17},{2,10},{10... | collective-permute-start | bytes 589832 | tf_op jit(solution)/shard_map/ppermute | solution.py:650
  287.4 1.8 collective-permute-start.11
Sparse Core Ops, SparseCore 0:
  229.6 43.2 all-reduce.3

commit v6 on v5

--- a/solution.py
+++ b/solution.py
@@ -107,7 +107,10 @@
         def pack(d, carry):
             used = tally[k * share + d]
             at = pl.multiple_of((k * share + d) * part, TILE)
-            values = jnp.where(slot_of(codes) < used, store[pl.ds(at, codes), :], 0.0)
+            filled = slot_of(codes) < used
+            if codes > C * slots:
+                filled = filled & (lax.broadcasted_iota(jnp.int32, (codes, PP), 0) < C * slots)
+            values = jnp.where(filled, store[pl.ds(at, codes), :], 0.0)
             packed[pl.ds(at, codes), :] = values.astype(BF16)
             subtiles = jnp.where(slot_of(TILE) < used, store[pl.ds(at + codes, TILE), :], -1.0)
             packed[pl.ds(at + codes, TILE), :] = subtiles.astype(BF16)

time: 313 us -> 313 us (level)
  no operation moved by 1% of the time
where the time goes in v6:
time: 313 us
  waiting for transfers between devices  194 us (62%)
  Pallas kernels  50.6 us (16%)
  starting transfers between devices  30.9 us (10%)
  local copies, waits for them, and re-layouts  20.8 us (7%)
  between operations  14.3 us (5%)
    all_to_all x1, waiting for transfers between devices, local(): lax.all_to_all(send.reshape(devices, part, PP), BOTH, split_axis=0, conca...  94.6 us
    ppermute x6, waiting for transfers between devices, swap(): lax.ppermute(value, axis, [(i, i ^ 1 << bit) for i in range(lax.axis_size...  43.7 us
    psum x1, waiting for transfers between devices, local(): grad = lax.psum(grad, 'tile', axis_index_groups=groups)  43.5 us
    pallas_call x1, Pallas kernels, conv_call(): pl.pallas_call(functools.partial(conv_kernel, slots), grid=(ROWS // 2 + 2...  21.7 us
    unnamed x21, local copies, waits for them, and re-layouts  11.2 us
    pallas_call x1, Pallas kernels, send_call(): pl.pallas_call(functools.partial(send_kernel, slots, part), in_specs=[sme...  11 us
    pallas_call x1, Pallas kernels, return_call(): pl.pallas_call(functools.partial(return_kernel, slots, devices), grid=(1,...  9.39 us
    ppermute x6, starting transfers between devices, shift(): return lax.ppermute(value, BOTH, pairs)  9.2 us
  transfers between devices with their start and end apart: 15, of which 11 were waited for; matrix products, arithmetic and copies ran while one was open for 6% of the time, Pallas kernels for 2%

profile of v6, /device:TPU:0, one launch (start us, length us, event | category | flops | bytes accessed | tf_op | source)
XLA Modules:
  0.0 312.8 jit_solution(419741691175736997)
XLA Ops:
  7.2 11.0 %block_products.1 = (bf16[19456,128]{1,0:T(8,128)(2,1)}, s32[256]{0:T(256)}) custom-call(s32[4,64]{1,0:T(4,128)} %bitcast.33, s32[4,64]{1,0:T(4,128)} %bitcast.34, s32[64]{0:T(128)} %counts_ref.1, bf16[74,64,128]{2,1,0:T(8,128)(2,1)} %bitcast.29, bf16[64,4,128,128]{3,2,1,0:T(8,128)(2,1)} %weight_hbm.3), custom_call_target="tpu_custom_call" | custom-call | tf_op jit(solution)/shard_map/block_products/pallas_call | solution.py:131
  18.1 7.4 %all-to-all-start = ((bf16[32,608,128]{2,1,0:T(8,128)(2,1)}), bf16[32,608,128]{2,1,0:T(8,128)(2,1)}, u32[]{:S(2)}, u32[]{:S(2)}) async-start(bf16[32,608,128]{2,1,0:T(8,128)(2,1)} %bitcast.25), calls=%async_computation | async-start | bytes 9961472 | tf_op jit(solution)/shard_map/all_to_all | solution.py:685
  25.6 4.7 %copy.22 = bf16[1,256,16,512]{3,1,2,0:T(8,128)(2,1)S(1)} copy(bf16[1,256,16,512]{3,2,1,0:T(8,128)(2,1)} %param.13) | data formatting | bytes 8388608 | tf_op args[6]
  30.3 2.0 copy-done
  32.3 2.1 collective-permute-start.2
  34.4 1.3 collective-permute-start.3
  36.3 1.6 copy.16
  37.9 1.6 copy.17
  40.9 1.9 taps.1
  42.9 94.6 %all-to-all-done.recv_hbm = bf16[32,608,128]{2,1,0:T(8,128)(2,1)} async-done(((bf16[32,608,128]{2,1,0:T(8,128)(2,1)}), bf16[32,608,128]{2,1,0:T(8,128)(2,1)}, u32[]{:S(2)}, u32[]{:S(2)}) %all-to-all-start) | async-done | bytes 4980768 | tf_op jit(solution)/shard_map/all_to_all | solution.py:685
  137.4 4.6 %field_sum.1 = (bf16[16,80,512]{2,1,0:T(8,128)(2,1)}, bf16[160,512]{1,0:T(8,128)(2,1)}, bf16[160,512]{1,0:T(8,128)(2,1)}, bf16[80,128]{1,0:T(8,128)(2,1)}, bf16[...) custom-call(bf16[32,608,128]{2,1,0:T(8,128)(2,1)} %all-to-all-done.recv_hbm), custom_call_target="tpu_custom_call" | custom-call | tf_op jit(solution)/shard_map/field_sum/pallas_call | solution.py:254
  142.0 1.6 collective-permute-start
  145.0 2.1 collective-permute-done.1.refs_2_.refs_3_.bottom_ref
  147.8 2.0 edge_columns.1
  149.8 1.3 collective-permute-start.4
  151.1 1.6 collective-permute-start.5
  152.7 2.7 collective-permute-done.4.far_west
  156.7 21.7 %conv_level.1 = (bf16[16,256,512]{2,1,0:T(8,128)(2,1)}, f32[768,256]{1,0:T(8,128)}, bf16[32,592,128]{2,1,0:T(8,128)(2,1)}) custom-call(bf16[16,80,512]{2,1,0:T(8,128)(2,1)} %get-tuple-element.30.field_ref, bf16[160,512]{1,0:T(8,128)(2,1)} %copy-done.4, bf16[160,512]{1,0:T(8,128)(2,1)} %copy-done.5, bf16[336,128]{1,0:T(8,128)(2,1)} %get-tuple-element.37.own_west, ...), custom_call_target="tpu_custom_call" | custom-call | tf_op jit(solution)/shard_map/conv_level/pallas_call | solution.py:533
  178.4 5.9 %all-to-all-start.1 = ((bf16[32,592,128]{2,1,0:T(8,128)(2,1)}), bf16[32,592,128]{2,1,0:T(8,128)(2,1)}, u32[]{:S(2)}, u32[]{:S(2)}) async-start(bf16[32,592,128]{2,1,0:T(8,128)(2,1)} %get-tuple-element.48), calls=%async_computation.1 | async-start | bytes 9699328 | tf_op jit(solution)/shard_map/all_to_all | solution.py:708
  184.7 6.5 %copy.21 = bf16[16,256,512]{2,0,1:T(8,128)(2,1)} copy(bf16[16,256,512]{2,1,0:T(8,128)(2,1)} %get-tuple-element.44) | data formatting | bytes 8388608 | tf_op jit(solution)/shard_map/conv_level/pallas_call | solution.py:533
  191.3 1.7 collective-permute-start.7
  193.0 29.5 %collective-permute-done.7 = f32[192,256]{1,0:T(8,128)S(1)} collective-permute-done((f32[192,256]{1,0:T(8,128)S(1)}, f32[192,256]{1,0:T(8,128)S(1)}, u32[]{:S(2)}, u32[]{:S(2)}) %collective-permute-start.7) | collective-permute-done | bytes 196640 | tf_op jit(solution)/shard_map/ppermute | solution.py:653
  222.6 1.5 collective-permute-start.8
  224.1 4.7 %collective-permute-done.8 = f32[96,256]{1,0:T(8,128)S(1)} collective-permute-done((f32[96,256]{1,0:T(8,128)S(1)}, f32[96,256]{1,0:T(8,128)S(1)}, u32[]{:S(2)}, u32[]{:S(2)}) %collective-permute-start.8) | collective-permute-done | bytes 98336 | tf_op jit(solution)/shard_map/ppermute | solution.py:653
  229.5 43.5 %all-reduce.4.cloned.1.call-done = f32[96,256]{1,0:T(8,128)} async-done(((f32[96,256]{1,0:T(8,128)}), f32[96,256]{1,0:T(8,128)}) %all-reduce.4.cloned.1.call-update) | async-done | bytes 98320 | tf_op jit(solution)/shard_map/psum | solution.py:716
  273.8 2.1 collective-permute-start.9
  275.9 2.6 collective-permute-done.9
  279.5 2.7 collective-permute-start.10
  282.2 5.2 %collective-permute-done.10 = f32[192,256]{1,0:T(8,128)S(1)} collective-permute-done((f32[192,256]{1,0:T(8,128)S(1)}, f32[192,256]{1,0:T(8,128)S(1)}, u32[]{:S(2)}, u32[]{:S(2)}) %collective-permute-start.10) | collective-permute-done | bytes 196640 | tf_op jit(solution)/shard_map/ppermute | solution.py:653
  287.5 1.7 collective-permute-done.11
  290.2 6.3 %all-to-all-done.1 = bf16[32,592,128]{2,1,0:T(8,128)(2,1)} async-done(((bf16[32,592,128]{2,1,0:T(8,128)(2,1)}), bf16[32,592,128]{2,1,0:T(8,128)(2,1)}, u32[]{:S(2)}, u32[]{:S(2)}) %all-to-all-start.1) | async-done | bytes 4849696 | tf_op jit(solution)/shard_map/all_to_all | solution.py:708
  296.6 9.4 %block_gradients.1 = bf16[74,64,128]{2,1,0:T(8,128)(2,1)} custom-call(s32[256]{0:T(256)} %get-tuple-element.47.place_ref, bf16[18944,128]{1,0:T(8,128)(2,1)} %bitcast.15.back_hbm, bf16[64,4,128,128]{3,2,1,0:T(8,128)(2,1)} %weight_hbm.3), custom_call_target="tpu_custom_call" | custom-call | tf_op jit(solution)/shard_map/block_gradients/pallas_call | solution.py:622
  (45 shorter events, 9.4 us)
Async XLA Ops:
  18.1 119.3 %all-to-all-start = ((bf16[32,608,128]{2,1,0:T(8,128)(2,1)}), bf16[32,608,128]{2,1,0:T(8,128)(2,1)}, u32[]{:S(2)}, u32[]{:S(2)}) async-start(bf16[32,608,128]{2,1,0:T(8,128)(2,1)} %bitcast.25), calls=%async_computation | async-start | bytes 9961472 | tf_op jit(solution)/shard_map/all_to_all | solution.py:685
  25.5 10.2 %copy-start.1 = (bf16[1,256,16,512]{3,2,1,0:T(8,128)(2,1)S(1)}, bf16[1,256,16,512]{3,2,1,0:T(8,128)(2,1)}, u32[]{:S(2)}) copy-start(bf16[1,256,16,512]{3,2,1,0:T(8,128)(2,1)} %param.13) | copy-start | bytes 12582916
  30.2 2.0 copy-start
  32.3 112.6 %collective-permute-start.2 = (bf16[256,512]{1,0:T(8,128)(2,1)S(1)}, bf16[256,512]{1,0:T(8,128)(2,1)S(1)}, u32[]{:S(2)}, u32[]{:S(2)}) collective-permute-start(bf16[256,512]{1,0:T(8,128)(2,1)S(1)} %get-tuple-element.50), channel_id=1, source_target_pairs={{0,1},{1,2},{2,3},{3,4},{4,5},{5,6},{6,7},{8,9},{9,10},{10,11},{11... | collective-permute-start | bytes 786440 | tf_op jit(solution)/shard_map/ppermute | solution.py:649
  34.4 110.5 %collective-permute-start.3 = (bf16[256,512]{1,0:T(8,128)(2,1)S(1)}, bf16[256,512]{1,0:T(8,128)(2,1)S(1)}, u32[]{:S(2)}, u32[]{:S(2)}) collective-permute-start(bf16[256,512]{1,0:T(8,128)(2,1)S(1)} %get-tuple-element.49), channel_id=1, source_target_pairs={{1,0},{2,1},{3,2},{4,3},{5,4},{6,5},{7,6},{9,8},{10,9},{11,10},{12... | collective-permute-start | bytes 786440 | tf_op jit(solution)/shard_map/ppermute | solution.py:649
  142.0 2.9 collective-permute-start
  143.6 3.5 %collective-permute-start.1 = (bf16[160,512]{1,0:T(8,128)(2,1)}, bf16[160,512]{1,0:T(8,128)(2,1)S(1)}, u32[]{:S(2)}, u32[]{:S(2)}) collective-permute-start(bf16[160,512]{1,0:T(8,128)(2,1)} %get-tuple-element.32), channel_id=1, source_target_pairs={{1,0},{2,1},{3,2},{4,3},{5,4},{6,5},{7,6},{9,8},{10,9},{11,10},{12... | collective-permute-start | bytes 491528 | tf_op jit(solution)/shard_map/ppermute | solution.py:649
  144.9 2.2 copy-start.2
  144.9 2.2 copy-start.3
  145.0 2.2 copy-start.4
  147.1 0.7 copy-start.5
  149.8 5.6 %collective-permute-start.4 = (bf16[336,128]{1,0:T(8,128)(2,1)}, bf16[336,128]{1,0:T(8,128)(2,1)S(1)}, u32[]{:S(2)}, u32[]{:S(2)}) collective-permute-start(bf16[336,128]{1,0:T(8,128)(2,1)} %get-tuple-element.38.own_east), channel_id=1, source_target_pairs={{0,8},{1,9},{2,10},{3,11},{4,12},{5,13},{6,14},{7,15},{8,16},{9,17... | collective-permute-start | bytes 258056 | tf_op jit(solution)/shard_map/ppermute | solution.py:649
  151.1 4.9 %collective-permute-start.5 = (bf16[336,128]{1,0:T(8,128)(2,1)}, bf16[336,128]{1,0:T(8,128)(2,1)S(1)}, u32[]{:S(2)}, u32[]{:S(2)}) collective-permute-start(bf16[336,128]{1,0:T(8,128)(2,1)} %get-tuple-element.37.own_west), channel_id=1, source_target_pairs={{0,24},{1,25},{2,26},{3,27},{4,28},{5,29},{6,30},{7,31},{8,0},{9,1... | collective-permute-start | bytes 258056 | tf_op jit(solution)/shard_map/ppermute | solution.py:649
  155.4 0.7 copy-start.7
  156.0 0.6 copy-start.8
  178.4 6.0 %copy-start.6 = (f32[768,256]{1,0:T(8,128)S(1)}, f32[768,256]{1,0:T(8,128)}, u32[]{:S(2)}) copy-start(f32[768,256]{1,0:T(8,128)} %get-tuple-element.43) | copy-start | bytes 2359300
  178.4 118.1 %all-to-all-start.1 = ((bf16[32,592,128]{2,1,0:T(8,128)(2,1)}), bf16[32,592,128]{2,1,0:T(8,128)(2,1)}, u32[]{:S(2)}, u32[]{:S(2)}) async-start(bf16[32,592,128]{2,1,0:T(8,128)(2,1)} %get-tuple-element.48), calls=%async_computation.1 | async-start | bytes 9699328 | tf_op jit(solution)/shard_map/all_to_all | solution.py:708
  184.3 88.6 %all-reduce.4.cloned.1.call-start = ((), (), s32[]{:S(2)}) async-start(), calls=%async_computation.2 | async-start | bytes 196608 | tf_op jit(solution)/shard_map/psum | solution.py:716
  184.4 6.8 %collective-permute-start.6 = (f32[384,256]{1,0:T(8,128)S(1)}, f32[384,256]{1,0:T(8,128)S(1)}, u32[]{:S(2)}, u32[]{:S(2)}) collective-permute-start(f32[384,256]{1,0:T(8,128)S(1)} %constant_dynamic-slice_fusion.2), channel_id=1, source_target_pairs={{0,1},{1,0},{2,3},{3,2},{4,5},{5,4},{6,7},{7,6},{8,9},{9,8},{10,11... | collective-permute-start | bytes 1179656 | tf_op jit(solution)/shard_map/ppermute | solution.py:653
  191.3 31.2 %collective-permute-start.7 = (f32[192,256]{1,0:T(8,128)S(1)}, f32[192,256]{1,0:T(8,128)S(1)}, u32[]{:S(2)}, u32[]{:S(2)}) collective-permute-start(f32[192,256]{1,0:T(8,128)S(1)} %constant_dynamic-slice_fusion.1), channel_id=1, source_target_pairs={{0,8},{8,0},{16,24},{24,16},{1,9},{9,1},{17,25},{25,17},{2,10},{10... | collective-permute-start | bytes 589832 | tf_op jit(solution)/shard_map/ppermute | solution.py:653
  222.6 6.2 %collective-permute-start.8 = (f32[96,256]{1,0:T(8,128)S(1)}, f32[96,256]{1,0:T(8,128)S(1)}, u32[]{:S(2)}, u32[]{:S(2)}) collective-permute-start(f32[96,256]{1,0:T(8,128)S(1)} %constant_dynamic-slice_fusion), channel_id=1, source_target_pairs={{0,16},{8,24},{16,0},{24,8},{1,17},{9,25},{17,1},{25,9},{2,18},{10... | collective-permute-start | bytes 294920 | tf_op jit(solution)/shard_map/ppermute | solution.py:653
  273.8 4.7 %collective-permute-start.9 = (f32[96,256]{1,0:T(8,128)S(1)}, f32[96,256]{1,0:T(8,128)S(1)}, u32[]{:S(2)}, u32[]{:S(2)}) collective-permute-start(f32[96,256]{1,0:T(8,128)S(1)} %broadcast_multiply_fusion), channel_id=1, source_target_pairs={{0,16},{8,24},{16,0},{24,8},{1,17},{9,25},{17,1},{25,9},{2,18},{10... | collective-permute-start | bytes 294920 | tf_op jit(solution)/shard_map/ppermute | solution.py:653
  279.5 7.9 %collective-permute-start.10 = (f32[192,256]{1,0:T(8,128)S(1)}, f32[192,256]{1,0:T(8,128)S(1)}, u32[]{:S(2)}, u32[]{:S(2)}) collective-permute-start(f32[192,256]{1,0:T(8,128)S(1)} %pad_maximum_fusion.2), channel_id=1, source_target_pairs={{0,8},{8,0},{16,24},{24,16},{1,9},{9,1},{17,25},{25,17},{2,10},{10... | collective-permute-start | bytes 589832 | tf_op jit(solution)/shard_map/ppermute | solution.py:653
  287.4 1.8 collective-permute-start.11
Sparse Core Ops, SparseCore 0:
  229.6 43.2 all-reduce.3
